TPU v7x, 32 devices: a whole 2x2x4 slice. The times are simulated.
32 devices in a mesh: gx: 8 (over y, x, core), gy: 4 (over z).
Axes of the slice: x: 2, y: 2, z: 4, core: 2. Of those that a mesh axis runs over, the one named last changes fastest.
Arguments:
- initial: float32 [128, 256, 128], P('gx', 'gy'), may hold values from -6 to 6, as said below
- material: int32 [128, 256, 128], P('gx', 'gy'), may hold values from 0 to 7
- goal_faces: int32 [128, 256, 128], P('gx', 'gy'), may hold values 0 or 1
- conductivity: float32 [8], replicated, may hold values from 0.2 to 2
Outputs:
- indicators: float32 [128, 256, 128], P('gx', 'gy')
- sensitivity: float32 [128, 256, 128], P('gx', 'gy')
Inputs may be any that keep to these rules, and one draw needn't show every extreme that they name: `initial`: temperatures.
All inputs are finite; a program needn't handle non-finite values. No bound on the sum of `goal_faces` on one device may be relied on, other than what follows from the above.
Results may differ from a plain program's by a relative error of at most 0.00002.
Values sent between devices are 32-bit elements; how exact they have to be, the bound alone decides.
No kernel may reach another device: no remote copies, remote signals or barrier semaphores. Data moves between devices by JAX's collectives and lax.ppermute only.
A program may use at most 64 MiB of HBM per device.

v0:
```python
import jax
import jax.numpy as jnp
from jax import lax
from jax.sharding import PartitionSpec as P

step_size = 0.075


def padded_2(block, sides, width):
    for axis, dim in sides:
        count = lax.axis_size(axis)
        forward = [(i, i + 1) for i in range(count - 1)]
        backward = [(target, source) for source, target in forward]
        low = lax.ppermute(
            lax.slice_in_dim(block, block.shape[dim] - width, None, axis=dim), axis, forward
        )
        high = lax.ppermute(lax.slice_in_dim(block, 0, width, axis=dim), axis, backward)
        block = jnp.concatenate([low, block, high], axis=dim)
    return block


def lookup(material, conductivity):
    result = jnp.zeros(material.shape, jnp.float32)
    for which in range(conductivity.shape[0]):
        result = jnp.where(material == which, conductivity[which], result)
    return result


def neighbours(padded):
    return [
        padded[2:, 1:-1, 1:-1],
        padded[:-2, 1:-1, 1:-1],
        padded[1:-1, 2:, 1:-1],
        padded[1:-1, :-2, 1:-1],
        padded[1:-1, 1:-1, 2:],
        padded[1:-1, 1:-1, :-2],
    ]


def face_values(padded):
    centre = padded[1:-1, 1:-1, 1:-1]
    return [0.5 * (centre + other) for other in neighbours(padded)]


def divergence(field, padded, weights):
    total = jnp.zeros_like(field)
    for weight, other in zip(weights, neighbours(padded)):
        total = total + weight * (other - field)
    return total


def patch_mean(padded):
    rows = padded[:-2] + padded[1:-1] + padded[2:]
    rows = rows[:, :-2] + rows[:, 1:-1] + rows[:, 2:]
    rows = rows[:, :, :-2] + rows[:, :, 1:-1] + rows[:, :, 2:]
    return rows / 27.0


def deep_plan(initial, material, goal_faces, conductivity):
    steps_count = 3
    margin = 5
    cells_x = initial.shape[0]
    cells_y = initial.shape[1]
    conduct = lookup(material, conductivity)
    stacked = jnp.stack([initial, conduct, goal_faces.astype(jnp.float32)], axis=0)
    widened = padded_2(stacked, (("gx", 1), ("gy", 2)), margin)
    start_x = lax.axis_index("gx") * cells_x - margin
    start_y = lax.axis_index("gy") * cells_y - margin
    where_x = start_x + jnp.arange(cells_x + 2 * margin, dtype=jnp.int32)
    where_y = start_y + jnp.arange(cells_y + 2 * margin, dtype=jnp.int32)
    inside_x = (where_x >= 0) & (where_x < cells_x * lax.axis_size("gx"))
    inside_y = (where_y >= 0) & (where_y < cells_y * lax.axis_size("gy"))
    inside = (inside_x[:, None] & inside_y[None, :]).astype(jnp.float32)[:, :, None]
    state = widened[0]
    weights = face_values(jnp.pad(widened[1], 1))

    def crop(field):
        return field[margin : margin + cells_x, margin : margin + cells_y]

    slope = divergence(state, jnp.pad(state, 1), weights)
    residuals = []
    for section in range(steps_count):
        following = (state + step_size * slope) * inside
        next_slope = divergence(following, jnp.pad(following, 1), weights)
        residuals.append(crop((following - state) / step_size - next_slope))
        state = following
        slope = next_slope
    flux = widened[2] * weights[0]
    adjoint = (flux - jnp.pad(flux, ((1, 0), (0, 0), (0, 0)))[:-1]) * inside
    indicators = jnp.zeros_like(initial)
    for section in range(steps_count - 1, -1, -1):
        padded = jnp.pad(adjoint, 1)
        indicators = indicators + residuals[section] * crop(patch_mean(padded) - adjoint)
        adjoint = (adjoint + step_size * divergence(adjoint, padded, weights)) * inside
    return (indicators, crop(adjoint))


def per_device(initial, material, goal_faces, conductivity):
    return deep_plan(initial, material, goal_faces, conductivity)


def solution(mesh):
    placed = (P("gx", "gy", None), P("gx", "gy", None), P("gx", "gy", None), P())
    return jax.shard_map(
        per_device,
        mesh=mesh,
        in_specs=placed,
        out_specs=(P("gx", "gy", None), P("gx", "gy", None)),
        check_vma=False,
    )
```

profile of v0, /device:TPU:3, one launch (start us, length us, event | category | flops | bytes accessed | tf_op | source)
XLA Modules:
  0.0 70.9 jit_solution(6736422263453049578)
XLA Ops:
  0.6 1.6 %fusion.165 = (f32[1]{0:T(128)}, f32[1]{0:T(128)}, f32[1]{0:T(128)}, f32[1]{0:T(128)}, f32[1]{0:T(128)}, /*index=5*/f32[1]{0:T(128)}, f32[1]{0:T(128)}, f32[1]{0:T(128)}) fusion(f32[8]{0:T(128)} %param.7), kind=kLoop, calls=%fused_computation.260 | loop fusion | bytes 64 | tf_op jit(solution)/shard_map/slice | solution.py:25
  2.3 1.1 %convert_bitcast_fusion = f32[1,16,64,128]{3,2,1,0:T(8,128)S(1)} fusion(s32[16,64,128]{2,1,0:T(8,128)} %param.6), kind=kLoop, calls=%fused_computation.244 | loop fusion | flops 131072 | bytes 1048576 | tf_op jit(solution)/shard_map/stack | solution.py:65
  3.4 5.3 %select_bitcast_fusion = f32[1,16,64,128]{3,2,1,0:T(8,128)S(1)} fusion(s32[16,64,128]{2,1,0:T(8,128)S(1)} %copy-done.1, f32[]{:T(128)} %bitcast.8, f32[]{:T(128)} %bitcast.7, f32[]{:T(128)} %bitcast.6, f32[]{:T(128)} %bitcast.5, f32[]{:T(128)} %bitcast.4, f32[]{:T(128)} %bitcast.3, f32[]{:T(128)} %bitcast.2, f32[]{:T(128)} %bitcast.1), kind=kLoop, calls=%fused_computation.245 | loop fusion | flops 2097152 | bytes 1048608 | tf_op jit(solution)/shard_map/stack | solution.py:65
  8.8 3.7 %collective-permute-start = (f32[3,5,64,128]{3,2,1,0:T(8,128)S(1)}, f32[3,5,64,128]{3,2,1,0:T(8,128)S(1)}, u32[]{:S(2)}, u32[]{:S(2)}) collective-permute-start(f32[3,5,64,128]{3,2,1,0:T(8,128)S(1)} %get-tuple-element.27), channel_id=1, source_target_pairs={{0,4},{4,8},{8,12},{12,16},{16,20},{20,24},{24,28},{1,5},{5,9},{9,... | collective-permute-start | bytes 1474568 | tf_op jit(solution)/shard_map/ppermute | solution.py:14
  12.5 1.9 %collective-permute-start.1 = (f32[3,5,64,128]{3,2,1,0:T(8,128)S(1)}, f32[3,5,64,128]{3,2,1,0:T(8,128)S(1)}, u32[]{:S(2)}, u32[]{:S(2)}) collective-permute-start(f32[3,5,64,128]{3,2,1,0:T(8,128)S(1)} %get-tuple-element.28), channel_id=1, source_target_pairs={{4,0},{8,4},{12,8},{16,12},{20,16},{24,20},{28,24},{5,1},{9,5},{13... | collective-permute-start | bytes 1474568 | tf_op jit(solution)/shard_map/ppermute | solution.py:17
  14.5 6.2 %collective-permute-done = f32[3,5,64,128]{3,2,1,0:T(8,128)S(1)} collective-permute-done((f32[3,5,64,128]{3,2,1,0:T(8,128)S(1)}, f32[3,5,64,128]{3,2,1,0:T(8,128)S(1)}, u32[]{:S(2)}, u32[]{:S(2)}) %collective-permute-start) | collective-permute-done | bytes 491552 | tf_op jit(solution)/shard_map/ppermute | solution.py:14
  20.7 4.5 %collective-permute-done.1 = f32[3,5,64,128]{3,2,1,0:T(8,128)S(1)} collective-permute-done((f32[3,5,64,128]{3,2,1,0:T(8,128)S(1)}, f32[3,5,64,128]{3,2,1,0:T(8,128)S(1)}, u32[]{:S(2)}, u32[]{:S(2)}) %collective-permute-start.1) | collective-permute-done | bytes 491552 | tf_op jit(solution)/shard_map/ppermute | solution.py:17
  25.2 3.2 %collective-permute-start.2 = (f32[3,26,5,128]{3,2,1,0:T(8,128)S(1)}, f32[3,26,5,128]{3,2,1,0:T(8,128)S(1)}, u32[]{:S(2)}, u32[]{:S(2)}) collective-permute-start(f32[3,26,5,128]{3,2,1,0:T(8,128)S(1)} %get-tuple-element.16), channel_id=1, source_target_pairs={{0,1},{1,2},{2,3},{4,5},{5,6},{6,7},{8,9},{9,10},{10,11},{12,13},{... | collective-permute-start | bytes 599048 | tf_op jit(solution)/shard_map/ppermute | solution.py:14
  28.5 1.3 %collective-permute-start.3 = (f32[3,26,5,128]{3,2,1,0:T(8,128)S(1)}, f32[3,26,5,128]{3,2,1,0:T(8,128)S(1)}, u32[]{:S(2)}, u32[]{:S(2)}) collective-permute-start(f32[3,26,5,128]{3,2,1,0:T(8,128)S(1)} %get-tuple-element.17), channel_id=1, source_target_pairs={{1,0},{2,1},{3,2},{5,4},{6,5},{7,6},{9,8},{10,9},{11,10},{13,12},{... | collective-permute-start | bytes 599048 | tf_op jit(solution)/shard_map/ppermute | solution.py:17
  29.9 5.1 %collective-permute-done.2 = f32[3,26,5,128]{3,2,1,0:T(8,128)S(1)} collective-permute-done((f32[3,26,5,128]{3,2,1,0:T(8,128)S(1)}, f32[3,26,5,128]{3,2,1,0:T(8,128)S(1)}, u32[]{:S(2)}, u32[]{:S(2)}) %collective-permute-start.2) | collective-permute-done | bytes 199712 | tf_op jit(solution)/shard_map/ppermute | solution.py:14
  35.0 4.1 %collective-permute-done.3 = f32[3,26,5,128]{3,2,1,0:T(8,128)S(1)} collective-permute-done((f32[3,26,5,128]{3,2,1,0:T(8,128)S(1)}, f32[3,26,5,128]{3,2,1,0:T(8,128)S(1)}, u32[]{:S(2)}, u32[]{:S(2)}) %collective-permute-start.3) | collective-permute-done | bytes 199712 | tf_op jit(solution)/shard_map/ppermute | solution.py:17
  39.1 0.5 pad_maximum_fusion
  39.8 1.9 %fusion.29 = (f32[26,74,128]{2,1,0:T(8,128)S(1)}, f32[26,74,128]{2,1,0:T(8,128)S(1)}, f32[26,74,128]{2,1,0:T(8,128)S(1)}, f32[26,74,128]{2,1,0:T(8,128)S(1)}, f3...) fusion(f32[26,74,128]{2,1,0:T(8,128)S(1)} %get-tuple-element.15, ...), kind=kLoop, calls=%fused_computation.94 | loop fusion | flops 7880704 | bytes 8873488 | tf_op jit(solution)/shard_map/mul | solution.py:83
  41.7 1.5 %add_multiply_fusion.1 = (f32[26,74,128]{2,1,0:T(8,128)S(1)}, f32[26,74,128]{2,1,0:T(8,128)S(1)}, f32[26,74,128]{2,1,0:T(8,128)S(1)}) fusion(f32[26,74,128]{2,1,0:T(8,128)S(1)} %get-tuple-element.6, f32[26,74]{1,0:T(8,128)S(1)} %and_convert_fusion, f32[26,74,128]{2,1,0:T(8,128)S(1)} %get-tuple-element.7, f32[26,74,128]{2,1,0:T(8,128)S(1)} %get-tuple-element.8, ...), kind=kLoop, calls=%fused_computation.200 | loop fusion | flops 5171712 | bytes 10843664 | tf_op jit(solution)/shard_map/mul | solution.py:83
  43.5 3.3 %add_multiply_fusion = (f32[26,74,128]{2,1,0:T(8,128)S(1)}, f32[26,74,128]{2,1,0:T(8,128)}, f32[26,74,128]{2,1,0:T(8,128)S(1)}) fusion(f32[26,74,128]{2,1,0:T(8,128)S(1)} %get-tuple-element.6, f32[26,74,128]{2,1,0:T(8,128)S(1)} %get-tuple-element.5, f32[26,74]{1,0:T(8,128)S(1)} %and_convert_fusion, f32[26,74,128]{2,1,0:T(8,128)S(1)} %get-tuple-element.7, ...), kind=kLoop, calls=%fused_computation.199 | loop fusion | flops 10589696 | bytes 12813840 | tf_op jit(solution)/shard_map/mul | solution.py:83
  46.8 1.3 %fusion.108 = f32[26,74,128]{2,1,0:T(8,128)S(1)} fusion(f32[26,74,128]{2,1,0:T(8,128)S(1)} %get-tuple-element.13, f32[26,74,128]{2,1,0:T(8,128)S(1)} %get-tuple-element.12, f32[26,74,128]{2,1,0:T(8,128)S(1)} %get-tuple-element.11, f32[26,74,128]{2,1,0:T(8,128)S(1)} %get-tuple-element.10, f32[26,74,128]{2,1,0:T(8,128)S(1)} %get-tuple-element.9, ...), kind=kLoop, calls=%fused_computation.173 | loop fusion | flops 4925440 | bytes 7888400 | tf_op jit(solution)/shard_map/mul | solution.py:94
  48.2 1.7 %fusion.3 = f32[26,76,130]{2,1,0:T(8,128)S(1)} fusion(f32[26,74,128]{2,1,0:T(8,128)S(1)} %get-tuple-element.13), kind=kLoop, calls=%fused_computation.61 | loop fusion | flops 513760 | bytes 2012608 | tf_op jit(solution)/shard_map/add | solution.py:53
  49.9 1.7 %fusion.1 = f32[26,76,130]{2,1,0:T(8,128)S(1)} fusion(f32[26,74,128]{2,1,0:T(8,128)S(1)} %fusion.7), kind=kLoop, calls=%fused_computation.59 | loop fusion | flops 513760 | bytes 2012608 | tf_op jit(solution)/shard_map/add | solution.py:53
  51.5 1.7 %fusion.5 = f32[26,76,130]{2,1,0:T(8,128)S(1)} fusion(f32[26,74,128]{2,1,0:T(8,128)S(1)} %fusion.108), kind=kLoop, calls=%fused_computation.63 | loop fusion | flops 513760 | bytes 2012608 | tf_op jit(solution)/shard_map/add | solution.py:53
  53.2 3.4 %fusion.122 = (f32[26,74,128]{2,1,0:T(8,128)S(1)}, f32[26,74,128]{2,1,0:T(8,128)}, f32[26,74,128]{2,1,0:T(8,128)}, f32[26,74,128]{2,1,0:T(8,128)}, f32[26,74,128...) fusion(f32[26,74,128]{2,1,0:T(8,128)S(1)} %get-tuple-element.12, ...), kind=kLoop, calls=%fused_computation.187 | loop fusion | flops 3940352 | bytes 15761408 | tf_op jit(solution)/shard_map/add | solution.py:48
  57.9 2.3 %fusion.164 = (f32[26,74,128]{2,1,0:T(8,128)}, f32[26,74,128]{2,1,0:T(8,128)}, f32[26,74,128]{2,1,0:T(8,128)}) fusion(f32[26,74,130]{2,1,0:T(8,128)S(1)} %slice_add_fusion), kind=kLoop, calls=%fused_computation.259 | loop fusion | bytes 5910528 | tf_op jit(solution)/shard_map/slice | solution.py:55
  60.2 3.6 %fusion.162 = (f32[26,74,128]{2,1,0:T(8,128)S(1)}, f32[26,74,128]{2,1,0:T(8,128)}, f32[26,74,128]{2,1,0:T(8,128)}, f32[26,74,128]{2,1,0:T(8,128)}, f32[26,74,128]{2,1,0:T(8,128)}, /*index=5*/f32[26,74,128]{2,1,0:T(8,128)}) fusion(f32[26,74,130]{2,1,0:T(8,128)S(1)} %slice_add_fusion.4, f32[26,74,130]{2,1,0:T(8,128)S(1)} %slice_add_fusion.2), kind=kLoop, calls=%fused_computation.257 | loop fusion | bytes 11821056 | tf_op jit(solution)/shard_map/slice | solution.py:55
  63.7 1.2 %fusion.135 = f32[16,64,128]{2,1,0:T(8,128)} fusion(f32[26,74,128]{2,1,0:T(8,128)S(1)} %get-tuple-element.38, f32[26,74,128]{2,1,0:T(8,128)S(1)} %get-tuple-element.37, f32[26,74,128]{2,1,0:T(8,128)S(1)} %get-tuple-element.36, f32[26,74,128]{2,1,0:T(8,128)S(1)} %get-tuple-element.29, f32[26,74,128]{2,1,0:T(8,128)S(1)} %fusion.108, ...), kind=kLoop, calls=%fused_computation.206 | loop fusion | flops 1179648 | bytes 4198400 | tf_op jit(solution)/shard_map/mul | solution.py:94
  64.9 6.0 %fusion.140 = f32[16,64,128]{2,1,0:T(8,128)} fusion(f32[26,74,128]{2,1,0:T(8,128)} %get-tuple-element.25, f32[26,74,128]{2,1,0:T(8,128)} %get-tuple-element.26, f32[26,74,128]{2,1,0:T(8,128)} %get-tuple-element.24, f32[26,74,128]{2,1,0:T(8,128)S(1)} %get-tuple-element.5, f32[26,74,128]{2,1,0:T(8,128)S(1)} %get-tuple-element.15, ...), kind=kLoop, calls=%fused_computation.214 | loop fusion | flops 4980736 | bytes 15204352 | tf_op jit(solution)/shard_map/add | solution.py:93
  (15 shorter events, 2.0 us)
Async XLA Ops:
  0.6 2.8 %copy-start.1 = (s32[16,64,128]{2,1,0:T(8,128)S(1)}, s32[16,64,128]{2,1,0:T(8,128)}, u32[]{:S(2)}) copy-start(s32[16,64,128]{2,1,0:T(8,128)} %param.5) | copy-start | bytes 1572868
  2.3 6.5 %copy-start = (f32[16,64,128]{2,1,0:T(8,128)S(1)}, f32[16,64,128]{2,1,0:T(8,128)}, u32[]{:S(2)}) copy-start(f32[16,64,128]{2,1,0:T(8,128)} %param.4) | copy-start | bytes 1572868
  8.8 11.9 %collective-permute-start = (f32[3,5,64,128]{3,2,1,0:T(8,128)S(1)}, f32[3,5,64,128]{3,2,1,0:T(8,128)S(1)}, u32[]{:S(2)}, u32[]{:S(2)}) collective-permute-start(f32[3,5,64,128]{3,2,1,0:T(8,128)S(1)} %get-tuple-element.27), channel_id=1, source_target_pairs={{0,4},{4,8},{8,12},{12,16},{16,20},{20,24},{24,28},{1,5},{5,9},{9,... | collective-permute-start | bytes 1474568 | tf_op jit(solution)/shard_map/ppermute | solution.py:14
  12.5 12.7 %collective-permute-start.1 = (f32[3,5,64,128]{3,2,1,0:T(8,128)S(1)}, f32[3,5,64,128]{3,2,1,0:T(8,128)S(1)}, u32[]{:S(2)}, u32[]{:S(2)}) collective-permute-start(f32[3,5,64,128]{3,2,1,0:T(8,128)S(1)} %get-tuple-element.28), channel_id=1, source_target_pairs={{4,0},{8,4},{12,8},{16,12},{20,16},{24,20},{28,24},{5,1},{9,5},{13... | collective-permute-start | bytes 1474568 | tf_op jit(solution)/shard_map/ppermute | solution.py:17
  25.2 9.7 %collective-permute-start.2 = (f32[3,26,5,128]{3,2,1,0:T(8,128)S(1)}, f32[3,26,5,128]{3,2,1,0:T(8,128)S(1)}, u32[]{:S(2)}, u32[]{:S(2)}) collective-permute-start(f32[3,26,5,128]{3,2,1,0:T(8,128)S(1)} %get-tuple-element.16), channel_id=1, source_target_pairs={{0,1},{1,2},{2,3},{4,5},{5,6},{6,7},{8,9},{9,10},{10,11},{12,13},{... | collective-permute-start | bytes 599048 | tf_op jit(solution)/shard_map/ppermute | solution.py:14
  28.5 10.6 %collective-permute-start.3 = (f32[3,26,5,128]{3,2,1,0:T(8,128)S(1)}, f32[3,26,5,128]{3,2,1,0:T(8,128)S(1)}, u32[]{:S(2)}, u32[]{:S(2)}) collective-permute-start(f32[3,26,5,128]{3,2,1,0:T(8,128)S(1)} %get-tuple-element.17), channel_id=1, source_target_pairs={{1,0},{2,1},{3,2},{5,4},{6,5},{7,6},{9,8},{10,9},{11,10},{13,12},{... | collective-permute-start | bytes 599048 | tf_op jit(solution)/shard_map/ppermute | solution.py:17
where the time goes:
time: 71.2 us; the launch traced here: 70.9 us
  other arithmetic  32.4 us (46%)
  waiting for transfers between devices  19.9 us (28%)
  starting transfers between devices  10.1 us (14%)
  local copies, waits for them, and re-layouts  7.67 us (11%)
  between operations  0.83 us (1%)
    ppermute x2, waiting for transfers between devices, padded_2(): lax.ppermute(lax.slice_in_dim(block, block.shape[dim] - width, None, axis...  11.3 us
    ppermute x2, waiting for transfers between devices, padded_2(): lax.ppermute(lax.slice_in_dim(block, 0, width, axis=dim), axis, backward)  8.58 us
    ppermute x2, starting transfers between devices, padded_2(): lax.ppermute(lax.slice_in_dim(block, block.shape[dim] - width, None, axis...  6.9 us
    mul x3, other arithmetic, deep_plan(): following = (state + step_size * slope) * inside  6.7 us
    another operation x2, other arithmetic, deep_plan(): jnp.stack([initial, conduct, goal_faces.astype(jnp.float32)], axis=0)  6.44 us
    add x1, other arithmetic, deep_plan(): indicators + residuals[section] * crop(patch_mean(padded) - adjoint)  5.97 us
    slice x2, local copies, waits for them, and re-layouts, patch_mean(): rows = rows[:, :, :-2] + rows[:, :, 1:-1] + rows[:, :, 2:]  5.82 us
    add x3, other arithmetic, patch_mean(): rows = padded[:-2] + padded[1:-1] + padded[2:]  5 us
  transfers between devices with their start and end apart: 4, of which 4 were waited for; matrix products, arithmetic and copies ran while one was open for 0% of the time, Pallas kernels for 0%

commit v1 on v0

v1 whole, which is shorter than its diff:
```python
import functools

import jax
import jax.numpy as jnp
from jax import lax
from jax.experimental import pallas as pl
from jax.experimental.pallas import tpu as pltpu
from jax.sharding import PartitionSpec as P

step_size = 0.075
HALO = 4
LIMIT = 40 * 1024 * 1024


def lanes_of(shape):
    return lax.broadcasted_iota(jnp.int32, shape, len(shape) - 1)


def half_weights(cond, lanes):
    lane = lanes_of((1, lanes))
    table = jnp.zeros((1, lanes), jnp.float32)
    for which in range(cond.shape[0]):
        table = jnp.where(lane == which, cond[which] * (0.5 * step_size), table)
    return table


def gather_rows(table, index):
    return jnp.take_along_axis(jnp.broadcast_to(table, index.shape), index, axis=1, mode="promise_in_bounds")


def far_kernel(initial, material, goal, cond, far, ids, flags, values, sems):
    cells_x, _, cells_z = initial.shape
    odd = lax.axis_index("gx") % 2
    planes = pl.ds(odd * (cells_x - HALO), HALO)
    moves = [
        pltpu.make_async_copy(source, target, sems.at[i])
        for i, (source, target) in enumerate((
            (cond, values),
            (material.at[planes], ids),
            (goal.at[planes], flags),
            (initial.at[planes], far.at[pl.ds(0, HALO)]),
        ))
    ]
    for move in moves:
        move.start()
    moves[0].wait()
    table = half_weights(values, cells_z)
    for move in moves[1:]:
        move.wait()
    for i in range(HALO):
        far[HALO + i] = gather_rows(table, ids[i])
        far[2 * HALO + i] = flags[i].astype(jnp.float32)


def pack_kernel(u, material, goal, cond, kh, up, down, near):
    cells_x, cells_y, cells_z = u.shape
    table = half_weights(cond, cells_z)
    low_half = lax.broadcasted_iota(jnp.int32, (8, cells_z), 0) < HALO
    top = cells_y - 8

    def pair(p, _):
        for i in (2 * p, 2 * p + 1):
            k = gather_rows(table, material[i])
            kh[i] = k
            up[i] = jnp.where(low_half, pltpu.roll(k[top:], HALO, 0), u[i, top:, :])
            down[i] = jnp.where(low_half, u[i, :8, :], pltpu.roll(k[:8], HALO, 0))
        for send, rows in ((up, pl.ds(top, 8)), (down, pl.ds(0, 8))):
            one = goal[2 * p, rows, :].astype(jnp.float32)
            two = pltpu.roll(goal[2 * p + 1, rows, :].astype(jnp.float32), HALO, 0)
            first, second = (two, one) if send is up else (one, two)
            send[cells_x + p] = jnp.where(low_half, first, second)
        return 0

    lax.fori_loop(0, cells_x // 2, pair, 0)
    odd = lax.axis_index("gx") % 2
    start = (1 - odd) * (cells_x - HALO)
    for i in range(HALO):
        near[i] = u[start + i]
        near[HALO + i] = kh[start + i]
        near[2 * HALO + i] = goal[start + i].astype(jnp.float32)


def halo_tiles(plane, cells_x, from_low, from_high, low_half):
    below, above = from_low[plane], from_high[plane]
    u = jnp.where(low_half, above, below)
    k = pltpu.roll(jnp.where(low_half, below, above), HALO, 0)
    return u, k


def goal_tiles(pair, cells_x, from_low, from_high, low_half):
    below, above = from_low[cells_x + pair], from_high[cells_x + pair]
    one = jnp.where(low_half, above, below)
    two = pltpu.roll(jnp.where(low_half, below, above), HALO, 0)
    return one, two


def corner_kernel(cells_x, from_low, from_high, near, far):
    cells_z = from_low.shape[-1]
    low_half = lax.broadcasted_iota(jnp.int32, (8, cells_z), 0) < HALO
    odd = lax.axis_index("gx") % 2
    last = cells_x - HALO
    for send, start in ((near, (1 - odd) * last), (far, odd * last)):
        for i in range(HALO):
            send[i], send[HALO + i] = halo_tiles(start + i, cells_x, from_low, from_high, low_half)
        for i in range(0, HALO, 2):
            one, two = goal_tiles(start // 2 + i // 2, cells_x, from_low, from_high, low_half)
            send[2 * HALO + i], send[2 * HALO + i + 1] = one, two


def main_kernel(initial, kh, goal, from_low, from_high, near, far, near_corner, far_corner, ind, sens,
                U, K, G, Wx, Wy, Wz, S, EA, EB, ZA, ZB, M0, Q3, AC, OI, OS, sems):
    cells_x, cells_y, cells_z = initial.shape
    H = HALO
    rows = cells_y + 8
    T = rows // 8
    top = H + cells_x
    planes = cells_x + 2 * H
    right = cells_z - 1
    low_half = lax.broadcasted_iota(jnp.int32, (8, cells_z), 0) < H
    lane = lanes_of((8, cells_z))
    gx, gy = lax.axis_index("gx"), lax.axis_index("gy")
    odd = gx % 2

    half = (1 - odd) * (3 * H)
    for source, offset, corner, at in (
        (near, half, near_corner, (1 - odd) * top),
        (far, 0, far_corner, odd * top),
    ):
        for field, ref in enumerate((U, K, G)):
            for i in range(H):
                ref[at + i, 0:cells_y, :] = source[offset + field * H + i]
                ref[at + i, cells_y:, :] = corner[field * H + i]

    def own(p, _):
        for i in (2 * p, 2 * p + 1):
            U[H + i, 0:cells_y, :] = initial[i]
            K[H + i, 0:cells_y, :] = kh[i]
            G[H + i, 0:cells_y, :] = goal[i].astype(jnp.float32)
            hu, hk = halo_tiles(i, cells_x, from_low, from_high, low_half)
            U[H + i, cells_y:, :] = hu
            K[H + i, cells_y:, :] = hk
        one, two = goal_tiles(p, cells_x, from_low, from_high, low_half)
        G[H + 2 * p, cells_y:, :] = one
        G[H + 2 * p + 1, cells_y:, :] = two
        return 0

    lax.fori_loop(0, cells_x // 2, own, 0)

    def rower(ref):
        return lambda i, j: ref[i, pl.ds(j, 8, stride=T), :]

    def tiler(ref):
        return lambda i, j: ref[i, j]

    def reader(load, start):
        seen = {}

        def read(d, j):
            if (d, j) not in seen:
                if j == -1:
                    seen[d, j] = pltpu.roll(load(start + d, T - 1), 1, 0)
                elif j == T:
                    seen[d, j] = pltpu.roll(load(start + d, 0), 7, 0)
                else:
                    seen[d, j] = load(start + d, j)
            return seen[d, j]

        return read

    def up_lane(value):
        return pltpu.roll(value, right, 1)

    def down_lane(value):
        return pltpu.roll(value, 1, 1)

    def inner_up(value):
        return jnp.where(lane == right, 0.0, up_lane(value))

    def inner_down(value):
        return jnp.where(lane == 0, 0.0, down_lane(value))

    def change(v, d, j, wx, wxm, wy, wym, wz, s):
        c = v(d, j)
        along = (wx * v(d + 1, j) + wxm * v(d - 1, j)) + (wy * v(d, j + 1) + wym * v(d, j - 1))
        return along + (wz * up_lane(c) + down_lane(wz * c)) - s * c

    def prelude(start, count):
        k, u, g = (reader(rower(ref), start) for ref in (K, U, G))
        for j in range(T):
            wx = {d: k(d, j) + k(d + 1, j) for d in range(-1, count)}
            flux = {d: g(d, j) * wx[d] for d in range(-1, count)}
            for d in range(count):
                i = start + d
                c = k(d, j)
                wy, wym = c + k(d, j + 1), c + k(d, j - 1)
                wzt, wzm = c + inner_up(c), c + inner_down(c)
                wz = jnp.where(lane == right, 0.0, wzt)
                s = ((wx[d] + wx[d - 1]) + (wy + wym)) + (wzt + wzm)
                Wx[i, j] = wx[d]
                Wy[i, j] = wy
                Wz[i, j] = wz
                S[i, j] = s
                EA[i, j] = change(u, d, j, wx[d], wx[d - 1], wy, wym, wz, s)
                ZA[i, j] = flux[d] - flux[d - 1]

    def prelude_body(p, _):
        prelude(1 + 2 * p, 2)
        return 0

    lax.fori_loop(0, (planes - 2) // 2, prelude_body, 0)
    for j in range(T):
        Wx[0, j] = K[0, pl.ds(j, 8, stride=T), :] + K[1, pl.ds(j, 8, stride=T), :]

    plane = jnp.zeros((T, 8, cells_z), jnp.float32)
    row = jnp.zeros((planes, 1, cells_z), jnp.float32)

    def clear_row(ref, r):
        ref[:, r % T, r // T : r // T + 1, :] = row

    @pl.when(gx == 0)
    def _():
        EA[H - 1] = plane
        Wx[H - 1] = plane

    @pl.when(gx == lax.axis_size("gx") - 1)
    def _():
        EA[top] = plane
        ZA[top] = plane
        Wx[top - 1] = plane

    @pl.when(gy == 0)
    def _():
        clear_row(EA, rows - 1)
        clear_row(Wy, rows - 1)

    @pl.when(gy == lax.axis_size("gy") - 1)
    def _():
        clear_row(EA, cells_y)
        clear_row(Wy, cells_y - 1)

    def sweep(E, Z, start, count, finish, box):
        e, z = reader(tiler(E), start), reader(tiler(Z), start)
        wxs, wys = reader(tiler(Wx), start), reader(tiler(Wy), start)
        for j in range(T):
            if box:
                sums = {d: z(d, j) + (z(d, j + 1) + z(d, j - 1)) for d in range(-1, count + 1)}
            for d in range(count):
                i = start + d
                weights = (wxs(d, j), wxs(d - 1, j), wys(d, j), wys(d, j - 1), Wz[i, j], S[i, j])
                em = change(e, d, j, *weights)
                zm = change(z, d, j, *weights)
                q = None
                if box:
                    xs = sums[d - 1] + sums[d] + sums[d + 1]
                    xs = xs + (inner_up(xs) + inner_down(xs))
                    q = xs * (1.0 / 27.0) - z(d, j)
                finish(i, j, e(d, j), em, z(d, j), zm, q)

    def store_a(i, j, e, em, z, zm, q):
        EB[i, j] = e + em
        ZB[i, j] = z + zm
        if q is not None:
            M0[i - H, j] = em
            Q3[i - H, j] = q

    def store_b(i, j, e, em, z, zm, q):
        EA[i, j] = e + em
        ZA[i, j] = z + zm
        if q is not None:
            AC[i - H, j] = em * q

    def store_c(i, j, e, em, z, zm, q):
        o = i - H
        total = AC[o, j] + em * Q3[o, j] + M0[o, j] * q
        OI[o, pl.ds(j, 8, stride=T), :] = total * (-1.0 / (step_size * step_size))
        OS[o, pl.ds(j, 8, stride=T), :] = (z + zm) * (1.0 / step_size)

    def middle(E, Z, finish):
        def body(p, _):
            sweep(E, Z, H + 2 * p, 2, finish, True)
            return 0

        lax.fori_loop(0, cells_x // 2, body, 0)

    sweep(EA, ZA, H - 2, 2, store_a, False)
    middle(EA, ZA, store_a)
    sweep(EA, ZA, top, 2, store_a, False)
    sweep(EB, ZB, H - 1, 1, store_b, False)
    middle(EB, ZB, store_b)
    sweep(EB, ZB, top, 1, store_b, False)

    def leave(p):
        pair = pl.ds(2 * p, 2)
        return [
            pltpu.make_async_copy(source.at[pair, pl.ds(0, cells_y), :], target.at[pair], sems.at[k, p])
            for k, (source, target) in enumerate(((OI, ind), (OS, sens)))
        ]

    def last(p, _):
        sweep(EA, ZA, H + 2 * p, 2, store_c, True)
        for move in leave(p):
            move.start()
        return 0

    lax.fori_loop(0, cells_x // 2, last, 0)

    def settle(p, _):
        for move in leave(p):
            move.wait()
        return 0

    lax.fori_loop(0, cells_x // 2, settle, 0)


def whole(memory=None):
    return pl.BlockSpec(memory_space=memory or pltpu.VMEM)


def exchange(up, down, axis):
    count = lax.axis_size(axis)
    forward = [(i, i + 1) for i in range(count - 1)]
    backward = [(b, a) for a, b in forward]
    return lax.ppermute(up, axis, forward), lax.ppermute(down, axis, backward)


def swap(pairs):
    return [(a, b) for a, b in pairs] + [(b, a) for a, b in pairs]


def per_device(initial, material, goal_faces, conductivity):
    cells_x, cells_y, cells_z = initial.shape
    f32 = jnp.float32
    params = pltpu.CompilerParams(vmem_limit_bytes=LIMIT)
    small = pltpu.CompilerParams(vmem_limit_bytes=LIMIT // 4)
    shape = jax.ShapeDtypeStruct
    hbm = whole(pltpu.HBM)
    send = shape((cells_x + cells_x // 2, 8, cells_z), f32)
    block = shape(initial.shape, f32)
    side = shape((3 * HALO, cells_y, cells_z), f32)
    count = lax.axis_size("gx")
    far_pairs = [(i, i + 1) for i in range(1, count - 1, 2)]
    near_pairs = [(i, i + 1) for i in range(0, count, 2)]

    here = [pltpu.with_memory_space_constraint(x, pltpu.HBM) for x in (initial, material, goal_faces, conductivity)]
    far = pl.pallas_call(
        far_kernel,
        out_shape=side,
        in_specs=[hbm] * 4,
        out_specs=whole(),
        scratch_shapes=[
            pltpu.VMEM((HALO, cells_y, cells_z), jnp.int32),
            pltpu.VMEM((HALO, cells_y, cells_z), jnp.int32),
            pltpu.SMEM(conductivity.shape, f32),
            pltpu.SemaphoreType.DMA((4,)),
        ],
        compiler_params=small,
        name="far",
    )(*here)
    far = lax.ppermute(far, "gx", swap(far_pairs))
    kh, up, down, near = pl.pallas_call(
        pack_kernel,
        out_shape=(block, send, send, side),
        in_specs=[whole(), whole(), whole(), whole(pltpu.SMEM)],
        out_specs=(whole(),) * 4,
        compiler_params=small,
        name="pack",
    )(initial, material, goal_faces, conductivity)
    from_low, from_high = exchange(up, down, "gy")
    near = lax.all_gather(near, "gx", axis_index_groups=[list(pair) for pair in near_pairs], tiled=True)
    corner = shape((3 * HALO, 8, cells_z), f32)
    near_corner, far_corner = pl.pallas_call(
        functools.partial(corner_kernel, cells_x),
        out_shape=(corner, corner),
        in_specs=[whole()] * 2,
        out_specs=(whole(), whole()),
        compiler_params=small,
        name="corners",
    )(from_low, from_high)
    far_corner = lax.ppermute(far_corner, "gx", swap(far_pairs))
    near_corner = lax.ppermute(near_corner, "gx", swap(near_pairs))
    planes = cells_x + 2 * HALO
    rows = cells_y + 8
    natural = pltpu.VMEM((planes, rows, cells_z), f32)
    wide = pltpu.VMEM((planes, rows // 8, 8, cells_z), f32)
    inner = pltpu.VMEM((cells_x, rows // 8, 8, cells_z), f32)
    out = pltpu.VMEM((cells_x, rows, cells_z), f32)
    return pl.pallas_call(
        main_kernel,
        out_shape=(block, block),
        in_specs=[whole()] * 9,
        out_specs=(hbm, hbm),
        scratch_shapes=[natural] * 3 + [wide] * 8 + [inner] * 3 + [out] * 2
        + [pltpu.SemaphoreType.DMA((2, cells_x // 2))],
        compiler_params=params,
        name="chain",
    )(initial, kh, goal_faces, from_low, from_high, near, far, near_corner, far_corner)


def solution(mesh):
    placed = (P("gx", "gy", None), P("gx", "gy", None), P("gx", "gy", None), P())
    return jax.shard_map(
        per_device,
        mesh=mesh,
        in_specs=placed,
        out_specs=(P("gx", "gy", None), P("gx", "gy", None)),
        check_vma=False,
    )
```

time: 71.2 us -> 31.4 us (0.44)
  the two profiles are of different devices: /device:TPU:3 before, /device:TPU:1 now
where the time goes in v1:
time: 31.4 us; the launch traced here: 31.1 us
  starting transfers between devices  13.3 us (42%)
  Pallas kernels  10.6 us (34%)
  waiting for transfers between devices  4.07 us (13%)
  blocking collectives  2.37 us (8%)
  between operations  0.76 us (2%)
    pallas_call x1, Pallas kernels, per_device(): pl.pallas_call(main_kernel, out_shape=(block, block), in_specs=[whole()]...  7.77 us
    ppermute x1, starting transfers between devices, per_device(): far = lax.ppermute(far, 'gx', swap(far_pairs))  4.51 us
    ppermute x2, starting transfers between devices, exchange(): return (lax.ppermute(up, axis, forward), lax.ppermute(down, axis, backward))  4.5 us
    ppermute x1, starting transfers between devices, per_device(): far_corner = lax.ppermute(far_corner, 'gx', swap(far_pairs))  4.2 us
    ppermute x2, waiting for transfers between devices, exchange(): return (lax.ppermute(up, axis, forward), lax.ppermute(down, axis, backward))  4.06 us
    all_gather x1, blocking collectives, per_device(): lax.all_gather(near, 'gx', axis_index_groups=[list(pair) for pair in near...  2.37 us
    pallas_call x1, Pallas kernels, per_device(): pl.pallas_call(pack_kernel, out_shape=(block, send, send, side), in_specs...  1.46 us
    pallas_call x1, Pallas kernels, per_device(): pl.pallas_call(far_kernel, out_shape=side, in_specs=[hbm] * 4, out_specs=...  1.35 us
  transfers between devices with their start and end apart: 5, of which 2 were waited for; matrix products, arithmetic and copies ran while one was open for 0% of the time, Pallas kernels for 5%

profile of v1, /device:TPU:1, one launch (start us, length us, event | category | flops | bytes accessed | tf_op | source)
XLA Modules:
  0.0 31.1 jit_solution(2348365873482408587)
XLA Ops:
  0.6 0.0 copy-start.1
  0.6 0.0 copy-start
  0.7 0.0 copy-start.3
  0.7 0.0 copy-start.2
  0.7 1.4 %far.1 = f32[12,64,128]{2,1,0:T(8,128)S(1)} custom-call(f32[16,64,128]{2,1,0:T(8,128)} %initial.3, s32[16,64,128]{2,1,0:T(8,128)} %material.3, s32[16,64,128]{2,1,0:T(8,128)} %goal.5, f32[8]{0:T(128)} %cond.3), custom_call_target="tpu_custom_call" | custom-call | tf_op jit(solution)/shard_map/far/pallas_call | solution.py:345
  2.0 4.5 %collective-permute-start.2 = (f32[12,64,128]{2,1,0:T(8,128)S(1)}, f32[12,64,128]{2,1,0:T(8,128)S(1)}, u32[]{:S(2)}, u32[]{:S(2)}) collective-permute-start(f32[12,64,128]{2,1,0:T(8,128)S(1)} %far.1), channel_id=1, source_target_pairs={{4,8},{12,16},{20,24},{8,4},{16,12},{24,20},{5,9},{13,17},{21,25},... | collective-permute-start | bytes 1179656 | tf_op jit(solution)/shard_map/ppermute | solution.py:359
  6.5 0.0 copy-done.1
  6.6 0.0 copy-done
  6.6 0.0 copy-done.3
  6.6 0.0 copy-done.2
  6.6 1.5 %pack.1 = (f32[16,64,128]{2,1,0:T(8,128)S(1)}, f32[24,8,128]{2,1,0:T(8,128)S(1)}, f32[24,8,128]{2,1,0:T(8,128)S(1)}, f32[12,64,128]{2,1,0:T(8,128)S(1)}) custom-call(f32[16,64,128]{2,1,0:T(8,128)S(1)} %copy-done, s32[16,64,128]{2,1,0:T(8,128)S(1)} %copy-done.2, s32[16,64,128]{2,1,0:T(8,128)S(1)} %copy-done.1, f32[8]{0:T(128)S(1)} %copy-done.3), custom_call_target="tpu_custom_call" | custom-call | tf_op jit(solution)/shard_map/pack/pallas_call | solution.py:360
  8.1 3.2 %collective-permute-start = (f32[24,8,128]{2,1,0:T(8,128)S(1)}, f32[24,8,128]{2,1,0:T(8,128)S(1)}, u32[]{:S(2)}, u32[]{:S(2)}) collective-permute-start(f32[24,8,128]{2,1,0:T(8,128)S(1)} %get-tuple-element.9), channel_id=1, source_target_pairs={{0,1},{1,2},{2,3},{4,5},{5,6},{6,7},{8,9},{9,10},{10,11},{12,13},{... | collective-permute-start | bytes 294920 | tf_op jit(solution)/shard_map/ppermute | solution.py:323
  11.3 1.3 %collective-permute-start.1 = (f32[24,8,128]{2,1,0:T(8,128)S(1)}, f32[24,8,128]{2,1,0:T(8,128)S(1)}, u32[]{:S(2)}, u32[]{:S(2)}) collective-permute-start(f32[24,8,128]{2,1,0:T(8,128)S(1)} %get-tuple-element.10), channel_id=1, source_target_pairs={{1,0},{2,1},{3,2},{5,4},{6,5},{7,6},{9,8},{10,9},{11,10},{13,12},{... | collective-permute-start | bytes 294920 | tf_op jit(solution)/shard_map/ppermute | solution.py:323
  12.6 0.3 %collective-permute-done.from_low = f32[24,8,128]{2,1,0:T(8,128)S(1)} collective-permute-done((f32[24,8,128]{2,1,0:T(8,128)S(1)}, f32[24,8,128]{2,1,0:T(8,128)S(1)}, u32[]{:S(2)}, u32[]{:S(2)}) %collective-permute-start) | collective-permute-done | bytes 98336 | tf_op jit(solution)/shard_map/ppermute | solution.py:323
  12.9 3.7 %collective-permute-done.1.from_high = f32[24,8,128]{2,1,0:T(8,128)S(1)} collective-permute-done((f32[24,8,128]{2,1,0:T(8,128)S(1)}, f32[24,8,128]{2,1,0:T(8,128)S(1)}, u32[]{:S(2)}, u32[]{:S(2)}) %collective-permute-start.1) | collective-permute-done | bytes 98336 | tf_op jit(solution)/shard_map/ppermute | solution.py:323
  16.6 0.1 collective-permute-start.3
  16.7 4.2 %collective-permute-start.4 = (f32[12,8,128]{2,1,0:T(8,128)S(1)}, f32[12,8,128]{2,1,0:T(8,128)S(1)}, u32[]{:S(2)}, u32[]{:S(2)}) collective-permute-start(f32[12,8,128]{2,1,0:T(8,128)S(1)} %get-tuple-element.13), channel_id=1, source_target_pairs={{4,8},{12,16},{20,24},{8,4},{16,12},{24,20},{5,9},{13,17},{21,25},... | collective-permute-start | bytes 147464 | tf_op jit(solution)/shard_map/ppermute | solution.py:379
  20.9 2.4 %all_gather.3.near = f32[24,64,128]{2,1,0:T(8,128)S(1)} all-gather(f32[12,64,128]{2,1,0:T(8,128)S(1)} %get-tuple-element.11), channel_id=1, replica_groups={{0,4},{8,12},{16,20},{24,28},{1,5},{9,13},{17,21},{25,29},{2,6},{10,14}..., dimensions={0}, use_global_device_ids=true | all-gather | bytes 1179648 | tf_op jit(solution)/shard_map/all_gather | solution.py:369
  23.3 0.0 collective-permute-done.3.near_corner
  23.3 0.0 collective-permute-done.4.far_corner
  23.3 0.0 collective-permute-done.2.far
  23.3 7.8 %chain.1 = (f32[16,64,128]{2,1,0:T(8,128)}, f32[16,64,128]{2,1,0:T(8,128)}) custom-call(f32[16,64,128]{2,1,0:T(8,128)S(1)} %copy-done, f32[16,64,128]{2,1,0:T(8,128)S(1)} %get-tuple-element.8.kh, s32[16,64,128]{2,1,0:T(8,128)S(1)} %copy-done.1, f32[24,8,128]{2,1,0:T(8,128)S(1)} %collective-permute-done.from_low, ...), custom_call_target="tpu_custom_call" | custom-call | tf_op jit(solution)/shard_map/chain/pallas_call | solution.py:387
  (1 shorter events, 0.0 us)
Async XLA Ops:
  0.6 5.9 %copy-start.1 = (s32[16,64,128]{2,1,0:T(8,128)S(1)}, s32[16,64,128]{2,1,0:T(8,128)}, u32[]{:S(2)}) copy-start(s32[16,64,128]{2,1,0:T(8,128)} %goal.5) | copy-start | bytes 1572868
  0.6 5.9 %copy-start = (f32[16,64,128]{2,1,0:T(8,128)S(1)}, f32[16,64,128]{2,1,0:T(8,128)}, u32[]{:S(2)}) copy-start(f32[16,64,128]{2,1,0:T(8,128)} %initial.3) | copy-start | bytes 1572868
  0.7 5.9 %copy-start.3 = (f32[8]{0:T(128)S(1)}, f32[8]{0:T(128)}, u32[]{:S(2)}) copy-start(f32[8]{0:T(128)} %cond.3) | copy-start | bytes 100
  0.7 5.9 %copy-start.2 = (s32[16,64,128]{2,1,0:T(8,128)S(1)}, s32[16,64,128]{2,1,0:T(8,128)}, u32[]{:S(2)}) copy-start(s32[16,64,128]{2,1,0:T(8,128)} %material.3) | copy-start | bytes 1572868
  2.0 21.3 %collective-permute-start.2 = (f32[12,64,128]{2,1,0:T(8,128)S(1)}, f32[12,64,128]{2,1,0:T(8,128)S(1)}, u32[]{:S(2)}, u32[]{:S(2)}) collective-permute-start(f32[12,64,128]{2,1,0:T(8,128)S(1)} %far.1), channel_id=1, source_target_pairs={{4,8},{12,16},{20,24},{8,4},{16,12},{24,20},{5,9},{13,17},{21,25},... | collective-permute-start | bytes 1179656 | tf_op jit(solution)/shard_map/ppermute | solution.py:359
  8.1 4.8 %collective-permute-start = (f32[24,8,128]{2,1,0:T(8,128)S(1)}, f32[24,8,128]{2,1,0:T(8,128)S(1)}, u32[]{:S(2)}, u32[]{:S(2)}) collective-permute-start(f32[24,8,128]{2,1,0:T(8,128)S(1)} %get-tuple-element.9), channel_id=1, source_target_pairs={{0,1},{1,2},{2,3},{4,5},{5,6},{6,7},{8,9},{9,10},{10,11},{12,13},{... | collective-permute-start | bytes 294920 | tf_op jit(solution)/shard_map/ppermute | solution.py:323
  11.3 5.4 %collective-permute-start.1 = (f32[24,8,128]{2,1,0:T(8,128)S(1)}, f32[24,8,128]{2,1,0:T(8,128)S(1)}, u32[]{:S(2)}, u32[]{:S(2)}) collective-permute-start(f32[24,8,128]{2,1,0:T(8,128)S(1)} %get-tuple-element.10), channel_id=1, source_target_pairs={{1,0},{2,1},{3,2},{5,4},{6,5},{7,6},{9,8},{10,9},{11,10},{13,12},{... | collective-permute-start | bytes 294920 | tf_op jit(solution)/shard_map/ppermute | solution.py:323
  16.6 6.7 %collective-permute-start.3 = (f32[12,8,128]{2,1,0:T(8,128)S(1)}, f32[12,8,128]{2,1,0:T(8,128)S(1)}, u32[]{:S(2)}, u32[]{:S(2)}) collective-permute-start(f32[12,8,128]{2,1,0:T(8,128)S(1)} %get-tuple-element.12), channel_id=1, source_target_pairs={{0,4},{8,12},{16,20},{24,28},{4,0},{12,8},{20,16},{28,24},{1,5},{9... | collective-permute-start | bytes 147464 | tf_op jit(solution)/shard_map/ppermute | solution.py:380
  16.7 6.6 %collective-permute-start.4 = (f32[12,8,128]{2,1,0:T(8,128)S(1)}, f32[12,8,128]{2,1,0:T(8,128)S(1)}, u32[]{:S(2)}, u32[]{:S(2)}) collective-permute-start(f32[12,8,128]{2,1,0:T(8,128)S(1)} %get-tuple-element.13), channel_id=1, source_target_pairs={{4,8},{12,16},{20,24},{8,4},{16,12},{24,20},{5,9},{13,17},{21,25},... | collective-permute-start | bytes 147464 | tf_op jit(solution)/shard_map/ppermute | solution.py:379

commit v2 on v0

v2 whole, which is shorter than its diff:
```python
import functools

import jax
import jax.numpy as jnp
from jax import lax
from jax.experimental import pallas as pl
from jax.experimental.pallas import tpu as pltpu
from jax.sharding import PartitionSpec as P

step_size = 0.075
HALO = 4
LIMIT = 40 * 1024 * 1024


def lanes_of(shape):
    return lax.broadcasted_iota(jnp.int32, shape, len(shape) - 1)


def half_weights(cond, lanes):
    lane = lanes_of((1, lanes))
    table = jnp.zeros((1, lanes), jnp.float32)
    for which in range(cond.shape[0]):
        table = jnp.where(lane == which, cond[which] * (0.5 * step_size), table)
    return table


def gather_rows(table, index):
    return jnp.take_along_axis(jnp.broadcast_to(table, index.shape), index, axis=1, mode="promise_in_bounds")


def edge_kernel(initial, material, goal, cond, up, down, u, ids, flags, values, sems):
    cells_x, cells_y, cells_z = initial.shape
    moves = [pltpu.make_async_copy(cond, values, sems.at[6])]
    for end, first in enumerate((0, cells_y - 8)):
        for k, (source, target) in enumerate(((material, ids), (initial, u), (goal, flags))):
            moves.append(pltpu.make_async_copy(
                source.at[:, pl.ds(first, 8), :], target.at[end], sems.at[3 * end + k]))
    for move in moves:
        move.start()
    low_half = lax.broadcasted_iota(jnp.int32, (8, cells_z), 0) < HALO
    moves[0].wait()
    table = half_weights(values, cells_z)
    for move in moves[1:]:
        move.wait()
    for i in range(cells_x):
        k_low = pltpu.roll(gather_rows(table, ids[0, i]), HALO, 0)
        k_high = pltpu.roll(gather_rows(table, ids[1, i]), HALO, 0)
        up[i] = jnp.where(low_half, k_high, u[1, i])
        down[i] = jnp.where(low_half, u[0, i], k_low)
    for p in range(cells_x // 2):
        one, two = flags[1, 2 * p], pltpu.roll(flags[1, 2 * p + 1], HALO, 0)
        up[cells_x + p] = jnp.where(low_half, two, one).astype(jnp.float32)
        one, two = flags[0, 2 * p], pltpu.roll(flags[0, 2 * p + 1], HALO, 0)
        down[cells_x + p] = jnp.where(low_half, one, two).astype(jnp.float32)


def face_planes(send, start, u, material, goal, table):
    cells_y = u.shape[1]
    for i in range(HALO):
        send[i, 0:cells_y, :] = u[start + i]
        send[HALO + i, 0:cells_y, :] = gather_rows(table, material[start + i])
        send[2 * HALO + i, 0:cells_y, :] = goal[start + i].astype(jnp.float32)


def far_kernel(u, material, goal, cond, up, far):
    cells_x, _, cells_z = u.shape
    odd = lax.axis_index("gx") % 2
    face_planes(far, odd * (cells_x - HALO), u, material, goal, half_weights(cond, cells_z))


def halo_tiles(plane, cells_x, from_low, from_high, low_half):
    below, above = from_low[plane], from_high[plane]
    u = jnp.where(low_half, above, below)
    k = pltpu.roll(jnp.where(low_half, below, above), HALO, 0)
    return u, k


def goal_tiles(pair, cells_x, from_low, from_high, low_half):
    below, above = from_low[cells_x + pair], from_high[cells_x + pair]
    one = jnp.where(low_half, above, below)
    two = pltpu.roll(jnp.where(low_half, below, above), HALO, 0)
    return one, two


def near_kernel(u, material, goal, cond, from_low, from_high, far, near, far_corner):
    cells_x, cells_y, cells_z = u.shape
    low_half = lax.broadcasted_iota(jnp.int32, (8, cells_z), 0) < HALO
    odd = lax.axis_index("gx") % 2
    last = cells_x - HALO
    face_planes(near, (1 - odd) * last, u, material, goal, half_weights(cond, cells_z))
    for send, rows, start in ((near, pl.ds(cells_y, 8), (1 - odd) * last), (far_corner, slice(None), odd * last)):
        for i in range(HALO):
            send[i, rows, :], send[HALO + i, rows, :] = halo_tiles(start + i, cells_x, from_low, from_high, low_half)
        for i in range(0, HALO, 2):
            one, two = goal_tiles(start // 2 + i // 2, cells_x, from_low, from_high, low_half)
            send[2 * HALO + i, rows, :], send[2 * HALO + i + 1, rows, :] = one, two


class Steps:
    def __init__(self, cells_x, cells_y, cells_z):
        self.rows = cells_y + 8
        self.cells = (cells_x, cells_y, cells_z)
        self.T = self.rows // 8
        self.right = cells_z - 1
        self.lane = lanes_of((8, cells_z))
        gx, gy = lax.axis_index("gx"), lax.axis_index("gy")
        self.odd = gx % 2
        self.sign = (1 - 2 * self.odd).astype(jnp.float32)
        self.no_far = (gx == 0) | (gx == lax.axis_size("gx") - 1)
        self.no_low, self.no_high = gy == 0, gy == lax.axis_size("gy") - 1

    def rower(self, ref):
        return lambda i, j: ref[i, pl.ds(j, 8, stride=self.T), :]

    def reader(self, load, start):
        seen = {}
        T = self.T

        def read(d, j):
            if (d, j) not in seen:
                if j == -1:
                    seen[d, j] = pltpu.roll(load(start + d, T - 1), 1, 0)
                elif j == T:
                    seen[d, j] = pltpu.roll(load(start + d, 0), 7, 0)
                else:
                    seen[d, j] = load(start + d, j)
            return seen[d, j]

        return read

    def up_lane(self, value):
        return pltpu.roll(value, self.right, 1)

    def down_lane(self, value):
        return pltpu.roll(value, 1, 1)

    def inner_up(self, value):
        return jnp.where(self.lane == self.right, 0.0, self.up_lane(value))

    def inner_down(self, value):
        return jnp.where(self.lane == 0, 0.0, self.down_lane(value))

    def change(self, v, d, j, wx, wxm, wy, wym, wz, s):
        c = v(d, j)
        along = (wx * v(d + 1, j) + wxm * v(d - 1, j)) + (wy * v(d, j + 1) + wym * v(d, j - 1))
        return along + (wz * self.up_lane(c) + self.down_lane(wz * c)) - s * c

    def prelude(self, loads, start, count, finish):
        k, u, g = (self.reader(load, start) for load in loads)
        for j in range(self.T):
            wx = {d: k(d, j) + k(d + 1, j) for d in range(-1, count)}
            flux = {d: (self.sign * g(d, j)) * wx[d] for d in range(-1, count)}
            for d in range(count):
                c = k(d, j)
                wy, wym = c + k(d, j + 1), c + k(d, j - 1)
                wzt, wzm = c + self.inner_up(c), c + self.inner_down(c)
                wz = jnp.where(self.lane == self.right, 0.0, wzt)
                s = ((wx[d] + wx[d - 1]) + (wy + wym)) + (wzt + wzm)
                e = self.change(u, d, j, wx[d], wx[d - 1], wy, wym, wz, s)
                finish(start + d, j, wx[d], wy, wz, s, e, flux[d] - flux[d - 1])

    def clear_rows(self, E, Wy, first, count):
        row = jnp.zeros((count, 1, self.cells[2]), jnp.float32)

        def clear(ref, r):
            at = r // self.T
            ref[first : first + count, r % self.T, at : at + 1, :] = row

        @pl.when(self.no_low)
        def _():
            clear(E, self.rows - 1)
            clear(Wy, self.rows - 1)

        @pl.when(self.no_high)
        def _():
            clear(E, self.cells[1])
            clear(Wy, self.cells[1] - 1)

    def sweep(self, loads, start, count, finish, boxes):
        le, lz, lwx, lwy, lwz, ls = loads
        e, z, wxs, wys = (self.reader(load, start) for load in (le, lz, lwx, lwy))
        for j in range(self.T):
            wanted = {d + o for d in range(count) if boxes[d] for o in (-1, 0, 1)}
            sums = {d: z(d, j) + (z(d, j + 1) + z(d, j - 1)) for d in sorted(wanted)}
            for d in range(count):
                i = start + d
                weights = (wxs(d, j), wxs(d - 1, j), wys(d, j), wys(d, j - 1), lwz(i, j), ls(i, j))
                em = self.change(e, d, j, *weights)
                zm = self.change(z, d, j, *weights)
                q = None
                if boxes[d]:
                    xs = sums[d - 1] + sums[d] + sums[d + 1]
                    xs = xs + (self.inner_up(xs) + self.inner_down(xs))
                    q = xs * (1.0 / 27.0) - z(d, j)
                finish(i, j, e(d, j), em, z(d, j), zm, q)

    def results(self, OI, OS, o, j, total, z):
        OI[o, pl.ds(j, 8, stride=self.T), :] = total * (-1.0 / (step_size * step_size))
        OS[o, pl.ds(j, 8, stride=self.T), :] = z * (1.0 / step_size)

    def leave(self, first, OI, OS, ind, sens, sems, p):
        pair = pl.ds(first, 2)
        return [
            pltpu.make_async_copy(source.at[pair, pl.ds(0, self.cells[1]), :], target.at[pair], sems.at[k, p])
            for k, (source, target) in enumerate(((OI, ind), (OS, sens)))
        ]


KEPT = (("EA", 5, 4), ("ZA", 5, 4), ("EB", 6, 2), ("ZB", 6, 2), ("Wx", 4, 4), ("Wy", 5, 3), ("Wz", 5, 3),
        ("S", 5, 3), ("M0", 6, 2), ("Q3", 6, 2), ("AC", 7, 1))
KEPT_PLANES = sum(count for _, _, count in KEPT)


def tiler(ref):
    return lambda i, j: ref[i, j]


def inner_kernel(initial, material, goal, cond, from_low, from_high, near, ind, sens, edge, kept,
                 U, K, G, Wx, Wy, Wz, S, EA, EB, ZA, ZB, M0, Q3, AC, OI, OS, sems):
    cells_x, cells_y, cells_z = initial.shape
    H = HALO
    steps = Steps(cells_x, cells_y, cells_z)
    odd = steps.odd
    planes = cells_x + 2 * H
    low_half = lax.broadcasted_iota(jnp.int32, (8, cells_z), 0) < H
    table = half_weights(cond, cells_z)
    side, step = odd * (planes - 1), 1 - 2 * odd

    def place(natural):
        return side + step * natural

    def own(p, _):
        ones = goal_tiles(p, cells_x, from_low, from_high, low_half)
        for d in range(2):
            i = 2 * p + d
            f = place(H + i)
            U[f, 0:cells_y, :] = initial[i]
            K[f, 0:cells_y, :] = gather_rows(table, material[i])
            G[f + 1 - odd, 0:cells_y, :] = goal[i].astype(jnp.float32)
            U[f, cells_y:, :], K[f, cells_y:, :] = halo_tiles(i, cells_x, from_low, from_high, low_half)
            G[f + 1 - odd, cells_y:, :] = ones[d]
        return 0

    lax.fori_loop(0, cells_x // 2, own, 0)
    for i in range(H):
        f = (1 - odd) * (H + cells_x + i) + odd * (planes - 1 - i)
        U[f] = near[i]
        K[f] = near[H + i]
        G[f + 1 - odd] = near[2 * H + i]
    for d in range(2):
        edge[d] = U[H + d]
        edge[2 + d] = K[H + d]
        edge[4 + d] = G[H + d + 1 - odd]

    def first_goal(i, j):
        return G[i + 1, pl.ds(j, 8, stride=steps.T), :]

    def begin(i, j, wx, wy, wz, s, e, z):
        Wx[i, j], Wy[i, j], Wz[i, j], S[i, j], EA[i, j], ZA[i, j] = wx, wy, wz, s, e, z

    def prelude(p, _):
        steps.prelude((steps.rower(K), steps.rower(U), first_goal), H + 1 + 2 * p, 2, begin)
        return 0

    lax.fori_loop(0, (planes - 2 - H) // 2, prelude, 0)
    for j in range(steps.T):
        k = steps.rower(K)
        Wx[H, j] = k(H, j) + k(H + 1, j)
    steps.clear_rows(EA, Wy, H + 1, planes - 2 - H)

    def store_a(i, j, e, em, z, zm, q):
        EB[i, j] = e + em
        ZB[i, j] = z + zm
        if q is not None:
            M0[i - H, j] = em
            Q3[i - H, j] = q

    def store_b(i, j, e, em, z, zm, q):
        EA[i, j] = e + em
        ZA[i, j] = z + zm
        if q is not None:
            AC[i - H, j] = em * q

    def store_c(i, j, e, em, z, zm, q):
        o = i - H
        total = AC[o, j] + em * Q3[o, j] + M0[o, j] * q
        steps.results(OI, OS, place(i) - H, j, total, z + zm)

    weights = tuple(tiler(ref) for ref in (Wx, Wy, Wz, S))

    def sweep(E, Z, start, finish, boxes):
        steps.sweep((tiler(E), tiler(Z)) + weights, start, len(boxes), finish, boxes)

    def many(E, Z, start, pairs, finish):
        def body(p, _):
            sweep(E, Z, start + 2 * p, finish, (True, True))
            return 0

        lax.fori_loop(0, pairs, body, 0)

    top = H + cells_x
    many(EA, ZA, H + 2, (cells_x - 2) // 2, store_a)
    sweep(EA, ZA, top, store_a, (False, False))
    many(EB, ZB, H + 3, (cells_x - 4) // 2, store_b)
    sweep(EB, ZB, top - 1, store_b, (True, False))

    def leave(p):
        f = H + 4 + 2 * p
        return steps.leave((1 - odd) * (f - H) + odd * (top - 2 - f), OI, OS, ind, sens, sems, p)

    def last(p, _):
        sweep(EA, ZA, H + 4 + 2 * p, store_c, (True, True))
        for move in leave(p):
            move.start()
        return 0

    lax.fori_loop(0, (cells_x - 4) // 2, last, 0)
    refs = dict(EA=EA, ZA=ZA, EB=EB, ZB=ZB, Wx=Wx, Wy=Wy, Wz=Wz, S=S, M0=M0, Q3=Q3, AC=AC)
    at = 0
    for name, first, count in KEPT:
        shift = H if name in ("M0", "Q3", "AC") else 0
        for d in range(count):
            kept[at + d] = refs[name][first - shift + d]
        at += count

    def settle(p, _):
        for move in leave(p):
            move.wait()
        return 0

    lax.fori_loop(0, (cells_x - 4) // 2, settle, 0)


def outer_kernel(far, far_corner, edge, kept, ind_in, sens_in, ind, sens,
                 U, K, G, Wx, Wy, Wz, S, EA, EB, EC, ZA, ZB, ZC, M0, Q3, AC, OI, OS, sems):
    cells_x, cells_y, cells_z = ind.shape
    H = HALO
    steps = Steps(cells_x, cells_y, cells_z)
    odd = steps.odd
    for i in range(H):
        f = (1 - odd) * i + odd * (H - 1 - i)
        for field, (ref, at) in enumerate(((U, f), (K, f), (G, f + 1 - odd))):
            ref[at, 0:cells_y, :] = far[field * H + i]
            ref[at, cells_y:, :] = far_corner[field * H + i]
    for d in range(2):
        U[H + d] = edge[d]
        K[H + d] = edge[2 + d]
        G[H + d + 1 - odd] = edge[4 + d]

    places, at = {}, 0
    for name, first, count in KEPT:
        places[name] = (first, at)
        at += count

    def mixed(ref, name, own_first, own_last):
        first, offset = places[name]

        def load(i, j):
            if own_first <= i <= own_last:
                return ref[i, j]
            return kept[offset + i - first, j]

        return load

    def first_goal(i, j):
        return G[i + 1, pl.ds(j, 8, stride=steps.T), :]

    def begin(i, j, wx, wy, wz, s, e, z):
        Wx[i, j], Wy[i, j], Wz[i, j], S[i, j], EA[i, j], ZA[i, j] = wx, wy, wz, s, e, z

    for start in (1, 3):
        steps.prelude((steps.rower(K), steps.rower(U), first_goal), start, 2, begin)
    for j in range(steps.T):
        k = steps.rower(K)
        Wx[0, j] = k(0, j) + k(1, j)
    steps.clear_rows(EA, Wy, 1, H)

    @pl.when(steps.no_far)
    def _():
        plane = jnp.zeros((steps.T, 8, cells_z), jnp.float32)
        EA[H - 1] = plane
        ZA[H - 1] = plane
        Wx[H - 1] = plane

    weights = (mixed(Wx, "Wx", 0, H), mixed(Wy, "Wy", 1, H), mixed(Wz, "Wz", 1, H), mixed(S, "S", 1, H))

    def store_a(i, j, e, em, z, zm, q):
        EB[i, j] = e + em
        ZB[i, j] = z + zm
        if q is not None:
            M0[i, j] = em
            Q3[i, j] = q

    def store_b(i, j, e, em, z, zm, q):
        EC[i, j] = e + em
        ZC[i, j] = z + zm
        if q is not None:
            AC[i, j] = em * q

    top = H + cells_x
    m0, q3, ac = mixed(M0, "M0", H, H + 1), mixed(Q3, "Q3", H, H + 1), mixed(AC, "AC", H, H + 2)

    def store_c(i, j, e, em, z, zm, q):
        total = ac(i, j) + em * q3(i, j) + m0(i, j) * q
        steps.results(OI, OS, (1 - odd) * (i - H) + odd * (top - 1 - i), j, total, z + zm)

    first = (mixed(EA, "EA", 1, H), mixed(ZA, "ZA", 1, H)) + weights
    second = (mixed(EB, "EB", 2, H + 1), mixed(ZB, "ZB", 2, H + 1)) + weights
    third = (mixed(EC, "EA", 3, H + 2), mixed(ZC, "ZA", 3, H + 2)) + weights
    steps.sweep(first, 2, 2, store_a, (False, False))
    steps.sweep(first, 4, 2, store_a, (True, True))
    steps.sweep(second, 3, 2, store_b, (False, True))
    steps.sweep(second, 5, 2, store_b, (True, True))
    moves = []
    for p in range(2):
        f = H + 2 * p
        steps.sweep(third, f, 2, store_c, (True, True))
        moves += steps.leave((1 - odd) * (f - H) + odd * (top - 2 - f), OI, OS, ind, sens, sems, p)
        for move in moves[-2:]:
            move.start()
    for move in moves:
        move.wait()


def whole(memory=None):
    return pl.BlockSpec(memory_space=memory or pltpu.VMEM)


def exchange(up, down, axis):
    count = lax.axis_size(axis)
    forward = [(i, i + 1) for i in range(count - 1)]
    backward = [(b, a) for a, b in forward]
    return lax.ppermute(up, axis, forward), lax.ppermute(down, axis, backward)


def swap(pairs):
    return [(a, b) for a, b in pairs] + [(b, a) for a, b in pairs]


def per_device(initial, material, goal_faces, conductivity):
    cells_x, cells_y, cells_z = initial.shape
    f32 = jnp.float32
    params = pltpu.CompilerParams(vmem_limit_bytes=LIMIT)
    small = pltpu.CompilerParams(vmem_limit_bytes=LIMIT // 4)
    shape = jax.ShapeDtypeStruct
    hbm, vmem, smem = whole(pltpu.HBM), whole(), whole(pltpu.SMEM)
    rows = cells_y + 8
    planes = cells_x + 2 * HALO
    send = shape((cells_x + cells_x // 2, 8, cells_z), f32)
    block = shape(initial.shape, f32)
    count = lax.axis_size("gx")
    far_pairs = [(i, i + 1) for i in range(1, count - 1, 2)]
    near_pairs = [(i, i + 1) for i in range(0, count, 2)]

    here = [pltpu.with_memory_space_constraint(x, pltpu.HBM) for x in (initial, material, goal_faces, conductivity)]
    ends = (2, cells_x, 8, cells_z)
    up, down = pl.pallas_call(
        edge_kernel,
        out_shape=(send, send),
        in_specs=[hbm] * 4,
        out_specs=(vmem, vmem),
        scratch_shapes=[
            pltpu.VMEM(ends, f32),
            pltpu.VMEM(ends, jnp.int32),
            pltpu.VMEM(ends, jnp.int32),
            pltpu.SMEM(conductivity.shape, f32),
            pltpu.SemaphoreType.DMA((7,)),
        ],
        compiler_params=small,
        name="edges",
    )(*here)
    from_low, from_high = exchange(up, down, "gy")
    far = pl.pallas_call(
        far_kernel,
        out_shape=shape((3 * HALO, cells_y, cells_z), f32),
        in_specs=[vmem, vmem, vmem, smem, whole(pl.ANY)],
        out_specs=vmem,
        compiler_params=small,
        name="far",
    )(initial, material, goal_faces, conductivity, up)
    far_sent = far
    far = lax.ppermute(far, "gx", swap(far_pairs))
    near, far_corner = pl.pallas_call(
        near_kernel,
        out_shape=(shape((3 * HALO, rows, cells_z), f32), shape((3 * HALO, 8, cells_z), f32)),
        in_specs=[vmem, vmem, vmem, smem, vmem, vmem, whole(pl.ANY)],
        out_specs=(vmem, vmem),
        compiler_params=small,
        cost_estimate=pl.CostEstimate(flops=1000, bytes_accessed=1000, transcendentals=0),
        name="near",
    )(initial, material, goal_faces, conductivity, from_low, from_high, far_sent)
    near = lax.ppermute(near, "gx", swap(near_pairs))
    far_corner = lax.ppermute(far_corner, "gx", swap(far_pairs))

    def tiles(count):
        return pltpu.VMEM((count, rows // 8, 8, cells_z), f32)

    def natural(count):
        return pltpu.VMEM((count, rows, cells_z), f32)

    ind, sens, edge, kept = pl.pallas_call(
        inner_kernel,
        out_shape=(block, block, shape((6, rows, cells_z), f32), shape((KEPT_PLANES, rows // 8, 8, cells_z), f32)),
        in_specs=[vmem, vmem, vmem, smem, vmem, vmem, vmem],
        out_specs=(hbm, hbm, vmem, vmem),
        scratch_shapes=[natural(planes), natural(planes), natural(planes + 1)]
        + [tiles(planes)] * 8 + [tiles(cells_x)] * 3 + [natural(cells_x)] * 2
        + [pltpu.SemaphoreType.DMA((2, (cells_x - 4) // 2))],
        compiler_params=params,
        cost_estimate=pl.CostEstimate(flops=1000, bytes_accessed=1000, transcendentals=0),
        name="inner",
    )(initial, material, goal_faces, conductivity, from_low, from_high, near)
    return pl.pallas_call(
        outer_kernel,
        out_shape=(block, block),
        in_specs=[vmem] * 4 + [hbm, hbm],
        out_specs=(hbm, hbm),
        scratch_shapes=[natural(HALO + 2), natural(HALO + 2), natural(HALO + 3)]
        + [tiles(2 * HALO)] * 13 + [natural(cells_x)] * 2 + [pltpu.SemaphoreType.DMA((2, 2))],
        input_output_aliases={4: 0, 5: 1},
        compiler_params=small,
        name="outer",
    )(far, far_corner, edge, kept, ind, sens)


def solution(mesh):
    placed = (P("gx", "gy", None), P("gx", "gy", None), P("gx", "gy", None), P())
    return jax.shard_map(
        per_device,
        mesh=mesh,
        in_specs=placed,
        out_specs=(P("gx", "gy", None), P("gx", "gy", None)),
        check_vma=False,
    )
```

time: 71.2 us -> 29.1 us (0.41)
  the two profiles are of different devices: /device:TPU:3 before, /device:TPU:27 now
where the time goes in v2:
time: 29.1 us; the launch traced here: 28.9 us
  Pallas kernels  12.4 us (43%)
  starting transfers between devices  12 us (41%)
  waiting for transfers between devices  3.81 us (13%)
  between operations  0.75 us (3%)
    pallas_call x1, Pallas kernels, per_device(): pl.pallas_call(inner_kernel, out_shape=(block, block, shape((6, rows, cel...  7.66 us
    ppermute x1, starting transfers between devices, per_device(): far_corner = lax.ppermute(far_corner, 'gx', swap(far_pairs))  3.43 us
    ppermute x2, starting transfers between devices, exchange(): return (lax.ppermute(up, axis, forward), lax.ppermute(down, axis, backward))  3.37 us
    ppermute x2, waiting for transfers between devices, exchange(): return (lax.ppermute(up, axis, forward), lax.ppermute(down, axis, backward))  3.31 us
    ppermute x1, starting transfers between devices, per_device(): far = lax.ppermute(far, 'gx', swap(far_pairs))  3.02 us
    ppermute x1, starting transfers between devices, per_device(): near = lax.ppermute(near, 'gx', swap(near_pairs))  2.16 us
    pallas_call x1, Pallas kernels, per_device(): pl.pallas_call(outer_kernel, out_shape=(block, block), in_specs=[vmem] *...  1.93 us
    pallas_call x1, Pallas kernels, per_device(): pl.pallas_call(edge_kernel, out_shape=(send, send), in_specs=[hbm] * 4, o...  1.34 us
  transfers between devices with their start and end apart: 5, of which 2 were waited for; matrix products, arithmetic and copies ran while one was open for 0% of the time, Pallas kernels for 29%

profile of v2, /device:TPU:27, one launch (start us, length us, event | category | flops | bytes accessed | tf_op | source)
XLA Modules:
  0.0 28.9 jit_solution(4444590454963877998)
XLA Ops:
  0.6 0.0 copy-start.3
  0.6 0.0 copy-start.2
  0.7 0.0 copy-start.1
  0.7 0.0 copy-start
  0.7 1.3 %edges.1 = (f32[24,8,128]{2,1,0:T(8,128)S(1)}, f32[24,8,128]{2,1,0:T(8,128)S(1)}) custom-call(f32[16,64,128]{2,1,0:T(8,128)} %initial.3, s32[16,64,128]{2,1,0:T(8,128)} %material.7, s32[16,64,128]{2,1,0:T(8,128)} %goal.7, f32[8]{0:T(128)} %cond.7), custom_call_target="tpu_custom_call" | custom-call | tf_op jit(solution)/shard_map/edges/pallas_call | solution.py:457
  2.0 2.1 %collective-permute-start.2 = (f32[24,8,128]{2,1,0:T(8,128)S(1)}, f32[24,8,128]{2,1,0:T(8,128)S(1)}, u32[]{:S(2)}, u32[]{:S(2)}) collective-permute-start(f32[24,8,128]{2,1,0:T(8,128)S(1)} %get-tuple-element.11), channel_id=1, source_target_pairs={{1,0},{2,1},{3,2},{5,4},{6,5},{7,6},{9,8},{10,9},{11,10},{13,12},{... | collective-permute-start | bytes 294920 | tf_op jit(solution)/shard_map/ppermute | solution.py:433
  4.1 1.3 %collective-permute-start.1 = (f32[24,8,128]{2,1,0:T(8,128)S(1)}, f32[24,8,128]{2,1,0:T(8,128)S(1)}, u32[]{:S(2)}, u32[]{:S(2)}) collective-permute-start(f32[24,8,128]{2,1,0:T(8,128)S(1)} %get-tuple-element.10.up), channel_id=1, source_target_pairs={{0,1},{1,2},{2,3},{4,5},{5,6},{6,7},{8,9},{9,10},{10,11},{12,13},{... | collective-permute-start | bytes 294920 | tf_op jit(solution)/shard_map/ppermute | solution.py:433
  5.4 0.0 copy-done.3
  5.4 0.0 copy-done.2
  5.4 0.0 copy-done.1
  5.4 0.0 copy-done
  5.4 0.7 %far.1 = f32[12,64,128]{2,1,0:T(8,128)S(1)} custom-call(f32[16,64,128]{2,1,0:T(8,128)S(1)} %copy-done, s32[16,64,128]{2,1,0:T(8,128)S(1)} %copy-done.1, s32[16,64,128]{2,1,0:T(8,128)S(1)} %copy-done.2, f32[8]{0:T(128)S(1)} %copy-done.3, f32[24,8,128]{2,1,0:T(8,128)S(1)} %get-tuple-element.10.up), custom_call_target="tpu_custom_call" | custom-call | tf_op jit(solution)/shard_map/far/pallas_call | solution.py:473
  6.2 0.0 collective-permute-done.2.from_high
  6.2 3.3 %collective-permute-done.1.from_low = f32[24,8,128]{2,1,0:T(8,128)S(1)} collective-permute-done((f32[24,8,128]{2,1,0:T(8,128)S(1)}, f32[24,8,128]{2,1,0:T(8,128)S(1)}, u32[]{:S(2)}, u32[]{:S(2)}) %collective-permute-start.1) | collective-permute-done | bytes 98336 | tf_op jit(solution)/shard_map/ppermute | solution.py:433
  9.5 0.7 %near.1 = (f32[12,72,128]{2,1,0:T(8,128)S(1)}, f32[12,8,128]{2,1,0:T(8,128)S(1)}) custom-call(f32[16,64,128]{2,1,0:T(8,128)S(1)} %copy-done, s32[16,64,128]{2,1,0:T(8,128)S(1)} %copy-done.1, s32[16,64,128]{2,1,0:T(8,128)S(1)} %copy-done.2, f32[8]{0:T(128)S(1)} %copy-done.3, f32[24,8,128]{2,1,0:T(8,128)S(1)} %collective-permute-done.1.from_low, ...), custom_call_target="tpu_custom_call" | custom-call | flops 1000 | bytes 1000 | tf_op jit(solution)/shard_map/near/pallas_call | solution.py:483
  10.2 2.2 %collective-permute-start.4 = (f32[12,72,128]{2,1,0:T(8,128)S(1)}, f32[12,72,128]{2,1,0:T(8,128)S(1)}, u32[]{:S(2)}, u32[]{:S(2)}) collective-permute-start(f32[12,72,128]{2,1,0:T(8,128)S(1)} %get-tuple-element.13), channel_id=1, source_target_pairs={{0,4},{8,12},{16,20},{24,28},{4,0},{12,8},{20,16},{28,24},{1,5},{9... | collective-permute-start | bytes 1327112 | tf_op jit(solution)/shard_map/ppermute | solution.py:492
  12.3 3.0 %collective-permute-start = (f32[12,64,128]{2,1,0:T(8,128)S(1)}, f32[12,64,128]{2,1,0:T(8,128)S(1)}, u32[]{:S(2)}, u32[]{:S(2)}) collective-permute-start(f32[12,64,128]{2,1,0:T(8,128)S(1)} %far.1), channel_id=1, source_target_pairs={{4,8},{12,16},{20,24},{8,4},{16,12},{24,20},{5,9},{13,17},{21,25},... | collective-permute-start | bytes 1179656 | tf_op jit(solution)/shard_map/ppermute | solution.py:482
  15.4 3.4 %collective-permute-start.3 = (f32[12,8,128]{2,1,0:T(8,128)S(1)}, f32[12,8,128]{2,1,0:T(8,128)S(1)}, u32[]{:S(2)}, u32[]{:S(2)}) collective-permute-start(f32[12,8,128]{2,1,0:T(8,128)S(1)} %get-tuple-element.12), channel_id=1, source_target_pairs={{4,8},{12,16},{20,24},{8,4},{16,12},{24,20},{5,9},{13,17},{21,25},... | collective-permute-start | bytes 147464 | tf_op jit(solution)/shard_map/ppermute | solution.py:493
  18.8 0.0 collective-permute-done.4.near
  18.8 7.7 %inner.1 = (f32[16,64,128]{2,1,0:T(8,128)}, f32[16,64,128]{2,1,0:T(8,128)}, f32[6,72,128]{2,1,0:T(8,128)S(1)}, f32[30,9,8,128]{3,2,1,0:T(8,128)S(1)}) custom-call(f32[16,64,128]{2,1,0:T(8,128)S(1)} %copy-done, s32[16,64,128]{2,1,0:T(8,128)S(1)} %copy-done.1, s32[16,64,128]{2,1,0:T(8,128)S(1)} %copy-done.2, f32[8]{0:T(128)S(1)} %copy-done.3, ...), custom_call_target="tpu_custom_call" | custom-call | flops 1000 | bytes 1000 | tf_op jit(solution)/shard_map/inner/pallas_call | solution.py:501
  26.5 0.5 %collective-permute-done.3.far_corner = f32[12,8,128]{2,1,0:T(8,128)S(1)} collective-permute-done((f32[12,8,128]{2,1,0:T(8,128)S(1)}, f32[12,8,128]{2,1,0:T(8,128)S(1)}, u32[]{:S(2)}, u32[]{:S(2)}) %collective-permute-start.3) | collective-permute-done | bytes 49184 | tf_op jit(solution)/shard_map/ppermute | solution.py:493
  27.0 0.0 collective-permute-done.far
  27.0 1.9 %outer.1 = (f32[16,64,128]{2,1,0:T(8,128)}, f32[16,64,128]{2,1,0:T(8,128)}) custom-call(f32[12,64,128]{2,1,0:T(8,128)S(1)} %collective-permute-done.far, f32[12,8,128]{2,1,0:T(8,128)S(1)} %collective-permute-done.3.far_corner, f32[6,72,128]{2,1,0:T(8,128)S(1)} %get-tuple-element.14.edge, ...), custom_call_target="tpu_custom_call", output_to_operand_aliasing={{0}: (4, {}), {1}: (5, {})} | custom-call | tf_op jit(solution)/shard_map/outer/pallas_call | solution.py:513
Async XLA Ops:
  0.6 4.8 %copy-start.3 = (f32[8]{0:T(128)S(1)}, f32[8]{0:T(128)}, u32[]{:S(2)}) copy-start(f32[8]{0:T(128)} %cond.7) | copy-start | bytes 100
  0.6 4.8 %copy-start.2 = (s32[16,64,128]{2,1,0:T(8,128)S(1)}, s32[16,64,128]{2,1,0:T(8,128)}, u32[]{:S(2)}) copy-start(s32[16,64,128]{2,1,0:T(8,128)} %goal.7) | copy-start | bytes 1572868
  0.7 4.8 %copy-start.1 = (s32[16,64,128]{2,1,0:T(8,128)S(1)}, s32[16,64,128]{2,1,0:T(8,128)}, u32[]{:S(2)}) copy-start(s32[16,64,128]{2,1,0:T(8,128)} %material.7) | copy-start | bytes 1572868
  0.7 4.8 %copy-start = (f32[16,64,128]{2,1,0:T(8,128)S(1)}, f32[16,64,128]{2,1,0:T(8,128)}, u32[]{:S(2)}) copy-start(f32[16,64,128]{2,1,0:T(8,128)} %initial.3) | copy-start | bytes 1572868
  2.0 4.1 %collective-permute-start.2 = (f32[24,8,128]{2,1,0:T(8,128)S(1)}, f32[24,8,128]{2,1,0:T(8,128)S(1)}, u32[]{:S(2)}, u32[]{:S(2)}) collective-permute-start(f32[24,8,128]{2,1,0:T(8,128)S(1)} %get-tuple-element.11), channel_id=1, source_target_pairs={{1,0},{2,1},{3,2},{5,4},{6,5},{7,6},{9,8},{10,9},{11,10},{13,12},{... | collective-permute-start | bytes 294920 | tf_op jit(solution)/shard_map/ppermute | solution.py:433
  4.1 5.4 %collective-permute-start.1 = (f32[24,8,128]{2,1,0:T(8,128)S(1)}, f32[24,8,128]{2,1,0:T(8,128)S(1)}, u32[]{:S(2)}, u32[]{:S(2)}) collective-permute-start(f32[24,8,128]{2,1,0:T(8,128)S(1)} %get-tuple-element.10.up), channel_id=1, source_target_pairs={{0,1},{1,2},{2,3},{4,5},{5,6},{6,7},{8,9},{9,10},{10,11},{12,13},{... | collective-permute-start | bytes 294920 | tf_op jit(solution)/shard_map/ppermute | solution.py:433
  10.2 8.6 %collective-permute-start.4 = (f32[12,72,128]{2,1,0:T(8,128)S(1)}, f32[12,72,128]{2,1,0:T(8,128)S(1)}, u32[]{:S(2)}, u32[]{:S(2)}) collective-permute-start(f32[12,72,128]{2,1,0:T(8,128)S(1)} %get-tuple-element.13), channel_id=1, source_target_pairs={{0,4},{8,12},{16,20},{24,28},{4,0},{12,8},{20,16},{28,24},{1,5},{9... | collective-permute-start | bytes 1327112 | tf_op jit(solution)/shard_map/ppermute | solution.py:492
  12.3 14.6 %collective-permute-start = (f32[12,64,128]{2,1,0:T(8,128)S(1)}, f32[12,64,128]{2,1,0:T(8,128)S(1)}, u32[]{:S(2)}, u32[]{:S(2)}) collective-permute-start(f32[12,64,128]{2,1,0:T(8,128)S(1)} %far.1), channel_id=1, source_target_pairs={{4,8},{12,16},{20,24},{8,4},{16,12},{24,20},{5,9},{13,17},{21,25},... | collective-permute-start | bytes 1179656 | tf_op jit(solution)/shard_map/ppermute | solution.py:482
  15.4 11.6 %collective-permute-start.3 = (f32[12,8,128]{2,1,0:T(8,128)S(1)}, f32[12,8,128]{2,1,0:T(8,128)S(1)}, u32[]{:S(2)}, u32[]{:S(2)}) collective-permute-start(f32[12,8,128]{2,1,0:T(8,128)S(1)} %get-tuple-element.12), channel_id=1, source_target_pairs={{4,8},{12,16},{20,24},{8,4},{16,12},{24,20},{5,9},{13,17},{21,25},... | collective-permute-start | bytes 147464 | tf_op jit(solution)/shard_map/ppermute | solution.py:493

commit v3 on v2

--- a/solution.py
+++ b/solution.py
@@ -28,7 +28,7 @@
     return jnp.take_along_axis(jnp.broadcast_to(table, index.shape), index, axis=1, mode="promise_in_bounds")
 
 
-def edge_kernel(initial, material, goal, cond, up, down, u, ids, flags, values, sems):
+def edge_kernel(initial, material, goal, cond, up, down, shared, u, ids, flags, values, sems):
     cells_x, cells_y, cells_z = initial.shape
     moves = [pltpu.make_async_copy(cond, values, sems.at[6])]
     for end, first in enumerate((0, cells_y - 8)):
@@ -40,6 +40,7 @@
     low_half = lax.broadcasted_iota(jnp.int32, (8, cells_z), 0) < HALO
     moves[0].wait()
     table = half_weights(values, cells_z)
+    shared[...] = jnp.broadcast_to(table, shared.shape)
     for move in moves[1:]:
         move.wait()
     for i in range(cells_x):
@@ -62,10 +63,10 @@
         send[2 * HALO + i, 0:cells_y, :] = goal[start + i].astype(jnp.float32)
 
 
-def far_kernel(u, material, goal, cond, up, far):
-    cells_x, _, cells_z = u.shape
+def far_kernel(u, material, goal, table, up, far):
+    cells_x = u.shape[0]
     odd = lax.axis_index("gx") % 2
-    face_planes(far, odd * (cells_x - HALO), u, material, goal, half_weights(cond, cells_z))
+    face_planes(far, odd * (cells_x - HALO), u, material, goal, table[0:1])
 
 
 def halo_tiles(plane, cells_x, from_low, from_high, low_half):
@@ -82,18 +83,36 @@
     return one, two
 
 
-def near_kernel(u, material, goal, cond, from_low, from_high, far, near, far_corner):
+def near_kernel(u, material, goal, table, from_low, from_high, far, near_a, near_b, far_corner):
     cells_x, cells_y, cells_z = u.shape
     low_half = lax.broadcasted_iota(jnp.int32, (8, cells_z), 0) < HALO
     odd = lax.axis_index("gx") % 2
     last = cells_x - HALO
-    face_planes(near, (1 - odd) * last, u, material, goal, half_weights(cond, cells_z))
+    near = Halves(near_a, near_b)
+    face_planes(near, (1 - odd) * last, u, material, goal, table[0:1])
     for send, rows, start in ((near, pl.ds(cells_y, 8), (1 - odd) * last), (far_corner, slice(None), odd * last)):
         for i in range(HALO):
             send[i, rows, :], send[HALO + i, rows, :] = halo_tiles(start + i, cells_x, from_low, from_high, low_half)
         for i in range(0, HALO, 2):
             one, two = goal_tiles(start // 2 + i // 2, cells_x, from_low, from_high, low_half)
             send[2 * HALO + i, rows, :], send[2 * HALO + i + 1, rows, :] = one, two
+
+
+class Halves:
+    def __init__(self, *parts):
+        self.parts, self.size = parts, parts[0].shape[0]
+
+    def at_plane(self, index):
+        plane, *rest = index if isinstance(index, tuple) else (index,)
+        return self.parts[plane // self.size], (plane % self.size, *rest)
+
+    def __getitem__(self, index):
+        ref, inside = self.at_plane(index)
+        return ref[inside]
+
+    def __setitem__(self, index, value):
+        ref, inside = self.at_plane(index)
+        ref[inside] = value
 
 
 class Steps:
@@ -215,7 +234,7 @@
     return lambda i, j: ref[i, j]
 
 
-def inner_kernel(initial, material, goal, cond, from_low, from_high, near, ind, sens, edge, kept,
+def inner_kernel(initial, material, goal, table, from_low, from_high, near_a, near_b, ind, sens, edge, kept,
                  U, K, G, Wx, Wy, Wz, S, EA, EB, ZA, ZB, M0, Q3, AC, OI, OS, sems):
     cells_x, cells_y, cells_z = initial.shape
     H = HALO
@@ -223,7 +242,7 @@
     odd = steps.odd
     planes = cells_x + 2 * H
     low_half = lax.broadcasted_iota(jnp.int32, (8, cells_z), 0) < H
-    table = half_weights(cond, cells_z)
+    near = Halves(near_a, near_b)
     side, step = odd * (planes - 1), 1 - 2 * odd
 
     def place(natural):
@@ -235,7 +254,7 @@
             i = 2 * p + d
             f = place(H + i)
             U[f, 0:cells_y, :] = initial[i]
-            K[f, 0:cells_y, :] = gather_rows(table, material[i])
+            K[f, 0:cells_y, :] = gather_rows(table[0:1], material[i])
             G[f + 1 - odd, 0:cells_y, :] = goal[i].astype(jnp.float32)
             U[f, cells_y:, :], K[f, cells_y:, :] = halo_tiles(i, cells_x, from_low, from_high, low_half)
             G[f + 1 - odd, cells_y:, :] = ones[d]
@@ -443,7 +462,7 @@
     params = pltpu.CompilerParams(vmem_limit_bytes=LIMIT)
     small = pltpu.CompilerParams(vmem_limit_bytes=LIMIT // 4)
     shape = jax.ShapeDtypeStruct
-    hbm, vmem, smem = whole(pltpu.HBM), whole(), whole(pltpu.SMEM)
+    hbm, vmem = whole(pltpu.HBM), whole()
     rows = cells_y + 8
     planes = cells_x + 2 * HALO
     send = shape((cells_x + cells_x // 2, 8, cells_z), f32)
@@ -454,11 +473,11 @@
 
     here = [pltpu.with_memory_space_constraint(x, pltpu.HBM) for x in (initial, material, goal_faces, conductivity)]
     ends = (2, cells_x, 8, cells_z)
-    up, down = pl.pallas_call(
+    up, down, table = pl.pallas_call(
         edge_kernel,
-        out_shape=(send, send),
+        out_shape=(send, send, shape((8, cells_z), f32)),
         in_specs=[hbm] * 4,
-        out_specs=(vmem, vmem),
+        out_specs=(vmem, vmem, vmem),
         scratch_shapes=[
             pltpu.VMEM(ends, f32),
             pltpu.VMEM(ends, jnp.int32),
@@ -473,23 +492,25 @@
     far = pl.pallas_call(
         far_kernel,
         out_shape=shape((3 * HALO, cells_y, cells_z), f32),
-        in_specs=[vmem, vmem, vmem, smem, whole(pl.ANY)],
+        in_specs=[vmem] * 4 + [whole(pl.ANY)],
         out_specs=vmem,
         compiler_params=small,
         name="far",
-    )(initial, material, goal_faces, conductivity, up)
+    )(initial, material, goal_faces, table, up)
     far_sent = far
     far = lax.ppermute(far, "gx", swap(far_pairs))
-    near, far_corner = pl.pallas_call(
+    part = shape((3 * HALO // 2, rows, cells_z), f32)
+    near_a, near_b, far_corner = pl.pallas_call(
         near_kernel,
-        out_shape=(shape((3 * HALO, rows, cells_z), f32), shape((3 * HALO, 8, cells_z), f32)),
-        in_specs=[vmem, vmem, vmem, smem, vmem, vmem, whole(pl.ANY)],
-        out_specs=(vmem, vmem),
+        out_shape=(part, part, shape((3 * HALO, 8, cells_z), f32)),
+        in_specs=[vmem] * 6 + [whole(pl.ANY)],
+        out_specs=(vmem,) * 3,
         compiler_params=small,
         cost_estimate=pl.CostEstimate(flops=1000, bytes_accessed=1000, transcendentals=0),
         name="near",
-    )(initial, material, goal_faces, conductivity, from_low, from_high, far_sent)
-    near = lax.ppermute(near, "gx", swap(near_pairs))
+    )(initial, material, goal_faces, table, from_low, from_high, far_sent)
+    near_a = lax.ppermute(near_a, "gx", swap(near_pairs))
+    near_b = lax.ppermute(near_b, "gx", swap(near_pairs))
     far_corner = lax.ppermute(far_corner, "gx", swap(far_pairs))
 
     def tiles(count):
@@ -501,7 +522,7 @@
     ind, sens, edge, kept = pl.pallas_call(
         inner_kernel,
         out_shape=(block, block, shape((6, rows, cells_z), f32), shape((KEPT_PLANES, rows // 8, 8, cells_z), f32)),
-        in_specs=[vmem, vmem, vmem, smem, vmem, vmem, vmem],
+        in_specs=[vmem] * 8,
         out_specs=(hbm, hbm, vmem, vmem),
         scratch_shapes=[natural(planes), natural(planes), natural(planes + 1)]
         + [tiles(planes)] * 8 + [tiles(cells_x)] * 3 + [natural(cells_x)] * 2
@@ -509,7 +530,7 @@
         compiler_params=params,
         cost_estimate=pl.CostEstimate(flops=1000, bytes_accessed=1000, transcendentals=0),
         name="inner",
-    )(initial, material, goal_faces, conductivity, from_low, from_high, near)
+    )(initial, material, goal_faces, table, from_low, from_high, near_a, near_b)
     return pl.pallas_call(
         outer_kernel,
         out_shape=(block, block),

time: 29.1 us -> 28.3 us (0.973)
  Pallas kernels: 12.4 us -> 10.7 us
  waiting for transfers between devices: 3.81 us -> 4.78 us
  starting transfers between devices: 12 us -> 11.6 us
    ppermute x1 -> x2, starting transfers between devices: 2.16 us -> 0.56 us  [the longest x1 0.39 us: per_device(): near_a = lax.ppermute(near_a, 'gx', swap(near_pairs))]
    ppermute x2, waiting for transfers between devices: 3.31 us -> 4.77 us  [exchange(): return (lax.ppermute(up, axis, forward), lax.ppermute(down, axis, backward))]
    ppermute x1, starting transfers between devices: 3.02 us -> 3.68 us  [per_device(): far = lax.ppermute(far, 'gx', swap(far_pairs))]
    ppermute x1, starting transfers between devices: 3.43 us -> 4.03 us  [per_device(): far_corner = lax.ppermute(far_corner, 'gx', swap(far_pairs))]
    pallas_call x1, Pallas kernels: 0.71 us -> 0.15 us  [per_device(): pl.pallas_call(far_kernel, out_shape=shape((3 * HALO, cells_y, cells_z),...]
    pallas_call x2, Pallas kernels: 2.06 us -> 1.51 us  [the longest x1 1.34 us: per_device(): pl.pallas_call(edge_kernel, out_shape=(send, send, shape((8, cells_z), f3...]
    pallas_call x1, Pallas kernels: 7.66 us -> 7.14 us  [per_device(): pl.pallas_call(inner_kernel, out_shape=(block, block, shape((6, rows, cel...]
    ppermute x1, waiting for transfers between devices: 0.49 us -> 0.01 us  [per_device(): far_corner = lax.ppermute(far_corner, 'gx', swap(far_pairs))]
  transfers between devices with their start and end apart: 5 -> 6, of which waited for: 2 -> 2; matrix products, arithmetic and copies ran while one was open for 0% -> 0% of each run, Pallas kernels for 29% -> 26%
where the time goes in v3:
time: 28.3 us; the launch traced here: 28.1 us
  starting transfers between devices  11.6 us (41%)
  Pallas kernels  10.7 us (38%)
  waiting for transfers between devices  4.78 us (17%)
  between operations  0.75 us (3%)
    pallas_call x1, Pallas kernels, per_device(): pl.pallas_call(inner_kernel, out_shape=(block, block, shape((6, rows, cel...  7.14 us
    ppermute x2, waiting for transfers between devices, exchange(): return (lax.ppermute(up, axis, forward), lax.ppermute(down, axis, backward))  4.77 us
    ppermute x1, starting transfers between devices, per_device(): far_corner = lax.ppermute(far_corner, 'gx', swap(far_pairs))  4.03 us
    ppermute x1, starting transfers between devices, per_device(): far = lax.ppermute(far, 'gx', swap(far_pairs))  3.68 us
    ppermute x2, starting transfers between devices, exchange(): return (lax.ppermute(up, axis, forward), lax.ppermute(down, axis, backward))  3.37 us
    pallas_call x1, Pallas kernels, per_device(): pl.pallas_call(outer_kernel, out_shape=(block, block), in_specs=[vmem] *...  1.94 us
    pallas_call x1, Pallas kernels, per_device(): pl.pallas_call(edge_kernel, out_shape=(send, send, shape((8, cells_z), f3...  1.34 us
  transfers between devices with their start and end apart: 6, of which 2 were waited for; matrix products, arithmetic and copies ran while one was open for 0% of the time, Pallas kernels for 26%

profile of v3, /device:TPU:27, one launch (start us, length us, event | category | flops | bytes accessed | tf_op | source)
XLA Modules:
  0.0 28.1 jit_solution(9772643501512619330)
XLA Ops:
  0.6 0.0 copy-start.2
  0.6 0.0 copy-start.1
  0.7 0.0 copy-start
  0.7 1.3 %edges.1 = (f32[24,8,128]{2,1,0:T(8,128)S(1)}, f32[24,8,128]{2,1,0:T(8,128)S(1)}, f32[8,128]{1,0:T(8,128)S(1)}) custom-call(f32[16,64,128]{2,1,0:T(8,128)} %initial.3, s32[16,64,128]{2,1,0:T(8,128)} %material.7, s32[16,64,128]{2,1,0:T(8,128)} %goal.7, f32[8]{0:T(128)} %cond.1), custom_call_target="tpu_custom_call" | custom-call | tf_op jit(solution)/shard_map/edges/pallas_call | solution.py:476
  2.0 0.0 copy-done.2
  2.0 0.0 copy-done.1
  2.0 0.2 copy-done
  2.2 0.2 far.1
  2.3 3.7 %collective-permute-start = (f32[12,64,128]{2,1,0:T(8,128)S(1)}, f32[12,64,128]{2,1,0:T(8,128)S(1)}, u32[]{:S(2)}, u32[]{:S(2)}) collective-permute-start(f32[12,64,128]{2,1,0:T(8,128)S(1)} %far.1), channel_id=1, source_target_pairs={{4,8},{12,16},{20,24},{8,4},{16,12},{24,20},{5,9},{13,17},{21,25},... | collective-permute-start | bytes 1179656 | tf_op jit(solution)/shard_map/ppermute | solution.py:501
  6.0 2.1 %collective-permute-start.2 = (f32[24,8,128]{2,1,0:T(8,128)S(1)}, f32[24,8,128]{2,1,0:T(8,128)S(1)}, u32[]{:S(2)}, u32[]{:S(2)}) collective-permute-start(f32[24,8,128]{2,1,0:T(8,128)S(1)} %get-tuple-element.14), channel_id=1, source_target_pairs={{1,0},{2,1},{3,2},{5,4},{6,5},{7,6},{9,8},{10,9},{11,10},{13,12},{... | collective-permute-start | bytes 294920 | tf_op jit(solution)/shard_map/ppermute | solution.py:452
  8.1 1.3 %collective-permute-start.1 = (f32[24,8,128]{2,1,0:T(8,128)S(1)}, f32[24,8,128]{2,1,0:T(8,128)S(1)}, u32[]{:S(2)}, u32[]{:S(2)}) collective-permute-start(f32[24,8,128]{2,1,0:T(8,128)S(1)} %get-tuple-element.13.up), channel_id=1, source_target_pairs={{0,1},{1,2},{2,3},{4,5},{5,6},{6,7},{8,9},{9,10},{10,11},{12,13},{... | collective-permute-start | bytes 294920 | tf_op jit(solution)/shard_map/ppermute | solution.py:452
  9.4 0.7 %collective-permute-done.2.from_high = f32[24,8,128]{2,1,0:T(8,128)S(1)} collective-permute-done((f32[24,8,128]{2,1,0:T(8,128)S(1)}, f32[24,8,128]{2,1,0:T(8,128)S(1)}, u32[]{:S(2)}, u32[]{:S(2)}) %collective-permute-start.2) | collective-permute-done | bytes 98336 | tf_op jit(solution)/shard_map/ppermute | solution.py:452
  10.1 4.1 %collective-permute-done.1.from_low = f32[24,8,128]{2,1,0:T(8,128)S(1)} collective-permute-done((f32[24,8,128]{2,1,0:T(8,128)S(1)}, f32[24,8,128]{2,1,0:T(8,128)S(1)}, u32[]{:S(2)}, u32[]{:S(2)}) %collective-permute-start.1) | collective-permute-done | bytes 98336 | tf_op jit(solution)/shard_map/ppermute | solution.py:452
  14.2 0.2 near.1
  14.4 0.4 %collective-permute-start.4 = (f32[6,72,128]{2,1,0:T(8,128)S(1)}, f32[6,72,128]{2,1,0:T(8,128)S(1)}, u32[]{:S(2)}, u32[]{:S(2)}) collective-permute-start(f32[6,72,128]{2,1,0:T(8,128)S(1)} %get-tuple-element.16), channel_id=1, source_target_pairs={{0,4},{8,12},{16,20},{24,28},{4,0},{12,8},{20,16},{28,24},{1,5},{9... | collective-permute-start | bytes 663560 | tf_op jit(solution)/shard_map/ppermute | solution.py:512
  14.8 0.2 collective-permute-start.5
  14.9 4.0 %collective-permute-start.3 = (f32[12,8,128]{2,1,0:T(8,128)S(1)}, f32[12,8,128]{2,1,0:T(8,128)S(1)}, u32[]{:S(2)}, u32[]{:S(2)}) collective-permute-start(f32[12,8,128]{2,1,0:T(8,128)S(1)} %get-tuple-element.15), channel_id=1, source_target_pairs={{4,8},{12,16},{20,24},{8,4},{16,12},{24,20},{5,9},{13,17},{21,25},... | collective-permute-start | bytes 147464 | tf_op jit(solution)/shard_map/ppermute | solution.py:514
  19.0 0.0 collective-permute-done.4.near_a
  19.0 0.0 collective-permute-done.5.near_b
  19.0 7.1 %inner.1 = (f32[16,64,128]{2,1,0:T(8,128)}, f32[16,64,128]{2,1,0:T(8,128)}, f32[6,72,128]{2,1,0:T(8,128)S(1)}, f32[30,9,8,128]{3,2,1,0:T(8,128)S(1)}) custom-call(f32[16,64,128]{2,1,0:T(8,128)S(1)} %copy-done, s32[16,64,128]{2,1,0:T(8,128)S(1)} %copy-done.1, s32[16,64,128]{2,1,0:T(8,128)S(1)} %copy-done.2, f32[8,128]{1,0:T(8,128)S(1)} %get-tuple-element.12.table, ...), custom_call_target="tpu_custom_call" | custom-call | flops 1000 | bytes 1000 | tf_op jit(solution)/shard_map/inner/pallas_call | solution.py:522
  26.1 0.0 collective-permute-done.3.far_corner
  26.1 0.0 collective-permute-done.far
  26.1 1.9 %outer.1 = (f32[16,64,128]{2,1,0:T(8,128)}, f32[16,64,128]{2,1,0:T(8,128)}) custom-call(f32[12,64,128]{2,1,0:T(8,128)S(1)} %collective-permute-done.far, f32[12,8,128]{2,1,0:T(8,128)S(1)} %collective-permute-done.3.far_corner, f32[6,72,128]{2,1,0:T(8,128)S(1)} %get-tuple-element.18.edge, ...), custom_call_target="tpu_custom_call", output_to_operand_aliasing={{0}: (4, {}), {1}: (5, {})} | custom-call | tf_op jit(solution)/shard_map/outer/pallas_call | solution.py:534
Async XLA Ops:
  0.6 1.4 %copy-start.2 = (s32[16,64,128]{2,1,0:T(8,128)S(1)}, s32[16,64,128]{2,1,0:T(8,128)}, u32[]{:S(2)}) copy-start(s32[16,64,128]{2,1,0:T(8,128)} %goal.7) | copy-start | bytes 1572868
  0.6 1.4 %copy-start.1 = (s32[16,64,128]{2,1,0:T(8,128)S(1)}, s32[16,64,128]{2,1,0:T(8,128)}, u32[]{:S(2)}) copy-start(s32[16,64,128]{2,1,0:T(8,128)} %material.7) | copy-start | bytes 1572868
  0.7 1.5 %copy-start = (f32[16,64,128]{2,1,0:T(8,128)S(1)}, f32[16,64,128]{2,1,0:T(8,128)}, u32[]{:S(2)}) copy-start(f32[16,64,128]{2,1,0:T(8,128)} %initial.3) | copy-start | bytes 1572868
  2.3 23.8 %collective-permute-start = (f32[12,64,128]{2,1,0:T(8,128)S(1)}, f32[12,64,128]{2,1,0:T(8,128)S(1)}, u32[]{:S(2)}, u32[]{:S(2)}) collective-permute-start(f32[12,64,128]{2,1,0:T(8,128)S(1)} %far.1), channel_id=1, source_target_pairs={{4,8},{12,16},{20,24},{8,4},{16,12},{24,20},{5,9},{13,17},{21,25},... | collective-permute-start | bytes 1179656 | tf_op jit(solution)/shard_map/ppermute | solution.py:501
  6.0 4.1 %collective-permute-start.2 = (f32[24,8,128]{2,1,0:T(8,128)S(1)}, f32[24,8,128]{2,1,0:T(8,128)S(1)}, u32[]{:S(2)}, u32[]{:S(2)}) collective-permute-start(f32[24,8,128]{2,1,0:T(8,128)S(1)} %get-tuple-element.14), channel_id=1, source_target_pairs={{1,0},{2,1},{3,2},{5,4},{6,5},{7,6},{9,8},{10,9},{11,10},{13,12},{... | collective-permute-start | bytes 294920 | tf_op jit(solution)/shard_map/ppermute | solution.py:452
  8.1 6.1 %collective-permute-start.1 = (f32[24,8,128]{2,1,0:T(8,128)S(1)}, f32[24,8,128]{2,1,0:T(8,128)S(1)}, u32[]{:S(2)}, u32[]{:S(2)}) collective-permute-start(f32[24,8,128]{2,1,0:T(8,128)S(1)} %get-tuple-element.13.up), channel_id=1, source_target_pairs={{0,1},{1,2},{2,3},{4,5},{5,6},{6,7},{8,9},{9,10},{10,11},{12,13},{... | collective-permute-start | bytes 294920 | tf_op jit(solution)/shard_map/ppermute | solution.py:452
  14.4 4.6 %collective-permute-start.4 = (f32[6,72,128]{2,1,0:T(8,128)S(1)}, f32[6,72,128]{2,1,0:T(8,128)S(1)}, u32[]{:S(2)}, u32[]{:S(2)}) collective-permute-start(f32[6,72,128]{2,1,0:T(8,128)S(1)} %get-tuple-element.16), channel_id=1, source_target_pairs={{0,4},{8,12},{16,20},{24,28},{4,0},{12,8},{20,16},{28,24},{1,5},{9... | collective-permute-start | bytes 663560 | tf_op jit(solution)/shard_map/ppermute | solution.py:512
  14.8 4.2 %collective-permute-start.5 = (f32[6,72,128]{2,1,0:T(8,128)S(1)}, f32[6,72,128]{2,1,0:T(8,128)S(1)}, u32[]{:S(2)}, u32[]{:S(2)}) collective-permute-start(f32[6,72,128]{2,1,0:T(8,128)S(1)} %get-tuple-element.17), channel_id=1, source_target_pairs={{0,4},{8,12},{16,20},{24,28},{4,0},{12,8},{20,16},{28,24},{1,5},{9... | collective-permute-start | bytes 663560 | tf_op jit(solution)/shard_map/ppermute | solution.py:513
  14.9 11.2 %collective-permute-start.3 = (f32[12,8,128]{2,1,0:T(8,128)S(1)}, f32[12,8,128]{2,1,0:T(8,128)S(1)}, u32[]{:S(2)}, u32[]{:S(2)}) collective-permute-start(f32[12,8,128]{2,1,0:T(8,128)S(1)} %get-tuple-element.15), channel_id=1, source_target_pairs={{4,8},{12,16},{20,24},{8,4},{16,12},{24,20},{5,9},{13,17},{21,25},... | collective-permute-start | bytes 147464 | tf_op jit(solution)/shard_map/ppermute | solution.py:514

commit v4 on v3

--- a/solution.py
+++ b/solution.py
@@ -506,7 +506,7 @@
         in_specs=[vmem] * 6 + [whole(pl.ANY)],
         out_specs=(vmem,) * 3,
         compiler_params=small,
-        cost_estimate=pl.CostEstimate(flops=1000, bytes_accessed=1000, transcendentals=0),
+        cost_estimate=pl.CostEstimate(flops=10**9, bytes_accessed=1000, transcendentals=0),
         name="near",
     )(initial, material, goal_faces, table, from_low, from_high, far_sent)
     near_a = lax.ppermute(near_a, "gx", swap(near_pairs))

time: 28.3 us -> 25.8 us (0.912)
  the two profiles are of different devices: /device:TPU:27 before, /device:TPU:1 now
where the time goes in v4:
time: 25.8 us; the launch traced here: 25.6 us
  starting transfers between devices  14 us (54%)
  Pallas kernels  10.8 us (42%)
  between operations  0.78 us (3%)
    pallas_call x1, Pallas kernels, per_device(): pl.pallas_call(inner_kernel, out_shape=(block, block, shape((6, rows, cel...  7.14 us
    ppermute x2, starting transfers between devices, exchange(): return (lax.ppermute(up, axis, forward), lax.ppermute(down, axis, backward))  5.96 us
    ppermute x1, starting transfers between devices, per_device(): far = lax.ppermute(far, 'gx', swap(far_pairs))  4.4 us
    ppermute x1, starting transfers between devices, per_device(): far_corner = lax.ppermute(far_corner, 'gx', swap(far_pairs))  3.07 us
    pallas_call x1, Pallas kernels, per_device(): pl.pallas_call(outer_kernel, out_shape=(block, block), in_specs=[vmem] *...  1.93 us
    pallas_call x1, Pallas kernels, per_device(): pl.pallas_call(edge_kernel, out_shape=(send, send, shape((8, cells_z), f3...  1.34 us
  transfers between devices with their start and end apart: 6, of which 0 were waited for; matrix products, arithmetic and copies ran while one was open for 0% of the time, Pallas kernels for 29%

profile of v4, /device:TPU:1, one launch (start us, length us, event | category | flops | bytes accessed | tf_op | source)
XLA Modules:
  0.0 25.6 jit_solution(2157409202284460898)
XLA Ops:
  0.6 0.0 copy-start.2
  0.6 0.0 copy-start.1
  0.7 0.0 copy-start
  0.7 1.3 %edges.1 = (f32[24,8,128]{2,1,0:T(8,128)S(1)}, f32[24,8,128]{2,1,0:T(8,128)S(1)}, f32[8,128]{1,0:T(8,128)S(1)}) custom-call(f32[16,64,128]{2,1,0:T(8,128)} %initial.3, s32[16,64,128]{2,1,0:T(8,128)} %material.7, s32[16,64,128]{2,1,0:T(8,128)} %goal.7, f32[8]{0:T(128)} %cond.1), custom_call_target="tpu_custom_call" | custom-call | tf_op jit(solution)/shard_map/edges/pallas_call | solution.py:476
  2.0 1.3 %collective-permute-start.2 = (f32[24,8,128]{2,1,0:T(8,128)S(1)}, f32[24,8,128]{2,1,0:T(8,128)S(1)}, u32[]{:S(2)}, u32[]{:S(2)}) collective-permute-start(f32[24,8,128]{2,1,0:T(8,128)S(1)} %get-tuple-element.14), channel_id=1, source_target_pairs={{1,0},{2,1},{3,2},{5,4},{6,5},{7,6},{9,8},{10,9},{11,10},{13,12},{... | collective-permute-start | bytes 294920 | tf_op jit(solution)/shard_map/ppermute | solution.py:452
  3.3 4.7 %collective-permute-start.1 = (f32[24,8,128]{2,1,0:T(8,128)S(1)}, f32[24,8,128]{2,1,0:T(8,128)S(1)}, u32[]{:S(2)}, u32[]{:S(2)}) collective-permute-start(f32[24,8,128]{2,1,0:T(8,128)S(1)} %get-tuple-element.13.up), channel_id=1, source_target_pairs={{0,1},{1,2},{2,3},{4,5},{5,6},{6,7},{8,9},{9,10},{10,11},{12,13},{... | collective-permute-start | bytes 294920 | tf_op jit(solution)/shard_map/ppermute | solution.py:452
  8.0 0.0 copy-done.2
  8.0 0.0 copy-done.1
  8.0 0.0 copy-done
  8.0 0.2 far.1
  8.2 4.4 %collective-permute-start = (f32[12,64,128]{2,1,0:T(8,128)S(1)}, f32[12,64,128]{2,1,0:T(8,128)S(1)}, u32[]{:S(2)}, u32[]{:S(2)}) collective-permute-start(f32[12,64,128]{2,1,0:T(8,128)S(1)} %far.1), channel_id=1, source_target_pairs={{4,8},{12,16},{20,24},{8,4},{16,12},{24,20},{5,9},{13,17},{21,25},... | collective-permute-start | bytes 1179656 | tf_op jit(solution)/shard_map/ppermute | solution.py:501
  12.6 0.0 collective-permute-done.2.from_high
  12.6 0.0 collective-permute-done.1.from_low
  12.6 0.2 near.1
  12.8 0.1 collective-permute-start.4
  12.9 0.5 %collective-permute-start.5 = (f32[6,72,128]{2,1,0:T(8,128)S(1)}, f32[6,72,128]{2,1,0:T(8,128)S(1)}, u32[]{:S(2)}, u32[]{:S(2)}) collective-permute-start(f32[6,72,128]{2,1,0:T(8,128)S(1)} %get-tuple-element.17), channel_id=1, source_target_pairs={{0,4},{8,12},{16,20},{24,28},{4,0},{12,8},{20,16},{28,24},{1,5},{9... | collective-permute-start | bytes 663560 | tf_op jit(solution)/shard_map/ppermute | solution.py:513
  13.4 3.1 %collective-permute-start.3 = (f32[12,8,128]{2,1,0:T(8,128)S(1)}, f32[12,8,128]{2,1,0:T(8,128)S(1)}, u32[]{:S(2)}, u32[]{:S(2)}) collective-permute-start(f32[12,8,128]{2,1,0:T(8,128)S(1)} %get-tuple-element.15), channel_id=1, source_target_pairs={{4,8},{12,16},{20,24},{8,4},{16,12},{24,20},{5,9},{13,17},{21,25},... | collective-permute-start | bytes 147464 | tf_op jit(solution)/shard_map/ppermute | solution.py:514
  16.4 0.0 collective-permute-done.4.near_a
  16.4 0.0 collective-permute-done.5.near_b
  16.5 7.1 %inner.1 = (f32[16,64,128]{2,1,0:T(8,128)}, f32[16,64,128]{2,1,0:T(8,128)}, f32[6,72,128]{2,1,0:T(8,128)S(1)}, f32[30,9,8,128]{3,2,1,0:T(8,128)S(1)}) custom-call(f32[16,64,128]{2,1,0:T(8,128)S(1)} %copy-done, s32[16,64,128]{2,1,0:T(8,128)S(1)} %copy-done.1, s32[16,64,128]{2,1,0:T(8,128)S(1)} %copy-done.2, f32[8,128]{1,0:T(8,128)S(1)} %get-tuple-element.12.table, ...), custom_call_target="tpu_custom_call" | custom-call | flops 1000 | bytes 1000 | tf_op jit(solution)/shard_map/inner/pallas_call | solution.py:522
  23.6 0.0 collective-permute-done.3.far_corner
  23.6 0.0 collective-permute-done.far
  23.6 1.9 %outer.1 = (f32[16,64,128]{2,1,0:T(8,128)}, f32[16,64,128]{2,1,0:T(8,128)}) custom-call(f32[12,64,128]{2,1,0:T(8,128)S(1)} %collective-permute-done.far, f32[12,8,128]{2,1,0:T(8,128)S(1)} %collective-permute-done.3.far_corner, f32[6,72,128]{2,1,0:T(8,128)S(1)} %get-tuple-element.18.edge, ...), custom_call_target="tpu_custom_call", output_to_operand_aliasing={{0}: (4, {}), {1}: (5, {})} | custom-call | tf_op jit(solution)/shard_map/outer/pallas_call | solution.py:534
Async XLA Ops:
  0.6 7.4 %copy-start.2 = (s32[16,64,128]{2,1,0:T(8,128)S(1)}, s32[16,64,128]{2,1,0:T(8,128)}, u32[]{:S(2)}) copy-start(s32[16,64,128]{2,1,0:T(8,128)} %goal.7) | copy-start | bytes 1572868
  0.6 7.4 %copy-start.1 = (s32[16,64,128]{2,1,0:T(8,128)S(1)}, s32[16,64,128]{2,1,0:T(8,128)}, u32[]{:S(2)}) copy-start(s32[16,64,128]{2,1,0:T(8,128)} %material.7) | copy-start | bytes 1572868
  0.7 7.4 %copy-start = (f32[16,64,128]{2,1,0:T(8,128)S(1)}, f32[16,64,128]{2,1,0:T(8,128)}, u32[]{:S(2)}) copy-start(f32[16,64,128]{2,1,0:T(8,128)} %initial.3) | copy-start | bytes 1572868
  2.0 10.6 %collective-permute-start.2 = (f32[24,8,128]{2,1,0:T(8,128)S(1)}, f32[24,8,128]{2,1,0:T(8,128)S(1)}, u32[]{:S(2)}, u32[]{:S(2)}) collective-permute-start(f32[24,8,128]{2,1,0:T(8,128)S(1)} %get-tuple-element.14), channel_id=1, source_target_pairs={{1,0},{2,1},{3,2},{5,4},{6,5},{7,6},{9,8},{10,9},{11,10},{13,12},{... | collective-permute-start | bytes 294920 | tf_op jit(solution)/shard_map/ppermute | solution.py:452
  3.3 9.3 %collective-permute-start.1 = (f32[24,8,128]{2,1,0:T(8,128)S(1)}, f32[24,8,128]{2,1,0:T(8,128)S(1)}, u32[]{:S(2)}, u32[]{:S(2)}) collective-permute-start(f32[24,8,128]{2,1,0:T(8,128)S(1)} %get-tuple-element.13.up), channel_id=1, source_target_pairs={{0,1},{1,2},{2,3},{4,5},{5,6},{6,7},{8,9},{9,10},{10,11},{12,13},{... | collective-permute-start | bytes 294920 | tf_op jit(solution)/shard_map/ppermute | solution.py:452
  8.2 15.4 %collective-permute-start = (f32[12,64,128]{2,1,0:T(8,128)S(1)}, f32[12,64,128]{2,1,0:T(8,128)S(1)}, u32[]{:S(2)}, u32[]{:S(2)}) collective-permute-start(f32[12,64,128]{2,1,0:T(8,128)S(1)} %far.1), channel_id=1, source_target_pairs={{4,8},{12,16},{20,24},{8,4},{16,12},{24,20},{5,9},{13,17},{21,25},... | collective-permute-start | bytes 1179656 | tf_op jit(solution)/shard_map/ppermute | solution.py:501
  12.8 3.6 %collective-permute-start.4 = (f32[6,72,128]{2,1,0:T(8,128)S(1)}, f32[6,72,128]{2,1,0:T(8,128)S(1)}, u32[]{:S(2)}, u32[]{:S(2)}) collective-permute-start(f32[6,72,128]{2,1,0:T(8,128)S(1)} %get-tuple-element.16), channel_id=1, source_target_pairs={{0,4},{8,12},{16,20},{24,28},{4,0},{12,8},{20,16},{28,24},{1,5},{9... | collective-permute-start | bytes 663560 | tf_op jit(solution)/shard_map/ppermute | solution.py:512
  12.9 3.6 %collective-permute-start.5 = (f32[6,72,128]{2,1,0:T(8,128)S(1)}, f32[6,72,128]{2,1,0:T(8,128)S(1)}, u32[]{:S(2)}, u32[]{:S(2)}) collective-permute-start(f32[6,72,128]{2,1,0:T(8,128)S(1)} %get-tuple-element.17), channel_id=1, source_target_pairs={{0,4},{8,12},{16,20},{24,28},{4,0},{12,8},{20,16},{28,24},{1,5},{9... | collective-permute-start | bytes 663560 | tf_op jit(solution)/shard_map/ppermute | solution.py:513
  13.4 10.2 %collective-permute-start.3 = (f32[12,8,128]{2,1,0:T(8,128)S(1)}, f32[12,8,128]{2,1,0:T(8,128)S(1)}, u32[]{:S(2)}, u32[]{:S(2)}) collective-permute-start(f32[12,8,128]{2,1,0:T(8,128)S(1)} %get-tuple-element.15), channel_id=1, source_target_pairs={{4,8},{12,16},{20,24},{8,4},{16,12},{24,20},{5,9},{13,17},{21,25},... | collective-permute-start | bytes 147464 | tf_op jit(solution)/shard_map/ppermute | solution.py:514

commit v5 on v4

--- a/solution.py
+++ b/solution.py
@@ -230,6 +230,19 @@
 KEPT_PLANES = sum(count for _, _, count in KEPT)
 
 
+def turns(count, body, together=3):
+    full = count // together
+
+    def turn(p, _):
+        for d in range(together):
+            body(together * p + d)
+        return 0
+
+    lax.fori_loop(0, full, turn, 0)
+    for p in range(full * together, count):
+        body(p)
+
+
 def tiler(ref):
     return lambda i, j: ref[i, j]
 
@@ -277,11 +290,10 @@
     def begin(i, j, wx, wy, wz, s, e, z):
         Wx[i, j], Wy[i, j], Wz[i, j], S[i, j], EA[i, j], ZA[i, j] = wx, wy, wz, s, e, z
 
-    def prelude(p, _):
+    def prelude(p):
         steps.prelude((steps.rower(K), steps.rower(U), first_goal), H + 1 + 2 * p, 2, begin)
-        return 0
-
-    lax.fori_loop(0, (planes - 2 - H) // 2, prelude, 0)
+
+    turns((planes - 2 - H) // 2, prelude)
     for j in range(steps.T):
         k = steps.rower(K)
         Wx[H, j] = k(H, j) + k(H + 1, j)
@@ -311,11 +323,7 @@
         steps.sweep((tiler(E), tiler(Z)) + weights, start, len(boxes), finish, boxes)
 
     def many(E, Z, start, pairs, finish):
-        def body(p, _):
-            sweep(E, Z, start + 2 * p, finish, (True, True))
-            return 0
-
-        lax.fori_loop(0, pairs, body, 0)
+        turns(pairs, lambda p: sweep(E, Z, start + 2 * p, finish, (True, True)))
 
     top = H + cells_x
     many(EA, ZA, H + 2, (cells_x - 2) // 2, store_a)
@@ -327,13 +335,12 @@
         f = H + 4 + 2 * p
         return steps.leave((1 - odd) * (f - H) + odd * (top - 2 - f), OI, OS, ind, sens, sems, p)
 
-    def last(p, _):
+    def last(p):
         sweep(EA, ZA, H + 4 + 2 * p, store_c, (True, True))
         for move in leave(p):
             move.start()
-        return 0
-
-    lax.fori_loop(0, (cells_x - 4) // 2, last, 0)
+
+    turns((cells_x - 4) // 2, last)
     refs = dict(EA=EA, ZA=ZA, EB=EB, ZB=ZB, Wx=Wx, Wy=Wy, Wz=Wz, S=S, M0=M0, Q3=Q3, AC=AC)
     at = 0
     for name, first, count in KEPT:

time: 25.8 us -> 24.6 us (0.953)
  Pallas kernels: 10.8 us -> 9.59 us
    pallas_call x1, Pallas kernels: 7.14 us -> 5.95 us  [per_device(): pl.pallas_call(inner_kernel, out_shape=(block, block, shape((6, rows, cel...]
  transfers between devices with their start and end apart: 6 -> 6, of which waited for: 0 -> 0; matrix products, arithmetic and copies ran while one was open for 0% -> 0% of each run, Pallas kernels for 29% -> 26%
where the time goes in v5:
time: 24.6 us; the launch traced here: 24.4 us
  starting transfers between devices  14 us (57%)
  Pallas kernels  9.59 us (39%)
  between operations  0.78 us (3%)
    ppermute x2, starting transfers between devices, exchange(): return (lax.ppermute(up, axis, forward), lax.ppermute(down, axis, backward))  5.96 us
    pallas_call x1, Pallas kernels, per_device(): pl.pallas_call(inner_kernel, out_shape=(block, block, shape((6, rows, cel...  5.95 us
    ppermute x1, starting transfers between devices, per_device(): far = lax.ppermute(far, 'gx', swap(far_pairs))  4.4 us
    ppermute x1, starting transfers between devices, per_device(): far_corner = lax.ppermute(far_corner, 'gx', swap(far_pairs))  3.07 us
    pallas_call x1, Pallas kernels, per_device(): pl.pallas_call(outer_kernel, out_shape=(block, block), in_specs=[vmem] *...  1.93 us
    pallas_call x1, Pallas kernels, per_device(): pl.pallas_call(edge_kernel, out_shape=(send, send, shape((8, cells_z), f3...  1.34 us
    ppermute x1, starting transfers between devices, per_device(): near_b = lax.ppermute(near_b, 'gx', swap(near_pairs))  0.5 us
  transfers between devices with their start and end apart: 6, of which 0 were waited for; matrix products, arithmetic and copies ran while one was open for 0% of the time, Pallas kernels for 26%

profile of v5, /device:TPU:1, one launch (start us, length us, event | category | flops | bytes accessed | tf_op | source)
XLA Modules:
  0.0 24.4 jit_solution(1517852374266589195)
XLA Ops:
  0.6 0.0 copy-start.2
  0.6 0.0 copy-start.1
  0.7 0.0 copy-start
  0.7 1.3 %edges.1 = (f32[24,8,128]{2,1,0:T(8,128)S(1)}, f32[24,8,128]{2,1,0:T(8,128)S(1)}, f32[8,128]{1,0:T(8,128)S(1)}) custom-call(f32[16,64,128]{2,1,0:T(8,128)} %initial.3, s32[16,64,128]{2,1,0:T(8,128)} %material.7, s32[16,64,128]{2,1,0:T(8,128)} %goal.7, f32[8]{0:T(128)} %cond.1), custom_call_target="tpu_custom_call" | custom-call | tf_op jit(solution)/shard_map/edges/pallas_call | solution.py:483
  2.0 1.3 %collective-permute-start.2 = (f32[24,8,128]{2,1,0:T(8,128)S(1)}, f32[24,8,128]{2,1,0:T(8,128)S(1)}, u32[]{:S(2)}, u32[]{:S(2)}) collective-permute-start(f32[24,8,128]{2,1,0:T(8,128)S(1)} %get-tuple-element.14), channel_id=1, source_target_pairs={{1,0},{2,1},{3,2},{5,4},{6,5},{7,6},{9,8},{10,9},{11,10},{13,12},{... | collective-permute-start | bytes 294920 | tf_op jit(solution)/shard_map/ppermute | solution.py:459
  3.3 4.7 %collective-permute-start.1 = (f32[24,8,128]{2,1,0:T(8,128)S(1)}, f32[24,8,128]{2,1,0:T(8,128)S(1)}, u32[]{:S(2)}, u32[]{:S(2)}) collective-permute-start(f32[24,8,128]{2,1,0:T(8,128)S(1)} %get-tuple-element.13.up), channel_id=1, source_target_pairs={{0,1},{1,2},{2,3},{4,5},{5,6},{6,7},{8,9},{9,10},{10,11},{12,13},{... | collective-permute-start | bytes 294920 | tf_op jit(solution)/shard_map/ppermute | solution.py:459
  8.0 0.0 copy-done.2
  8.0 0.0 copy-done.1
  8.0 0.0 copy-done
  8.0 0.2 far.1
  8.2 4.4 %collective-permute-start = (f32[12,64,128]{2,1,0:T(8,128)S(1)}, f32[12,64,128]{2,1,0:T(8,128)S(1)}, u32[]{:S(2)}, u32[]{:S(2)}) collective-permute-start(f32[12,64,128]{2,1,0:T(8,128)S(1)} %far.1), channel_id=1, source_target_pairs={{4,8},{12,16},{20,24},{8,4},{16,12},{24,20},{5,9},{13,17},{21,25},... | collective-permute-start | bytes 1179656 | tf_op jit(solution)/shard_map/ppermute | solution.py:508
  12.6 0.0 collective-permute-done.2.from_high
  12.6 0.0 collective-permute-done.1.from_low
  12.6 0.2 near.1
  12.8 0.1 collective-permute-start.4
  12.9 0.5 %collective-permute-start.5 = (f32[6,72,128]{2,1,0:T(8,128)S(1)}, f32[6,72,128]{2,1,0:T(8,128)S(1)}, u32[]{:S(2)}, u32[]{:S(2)}) collective-permute-start(f32[6,72,128]{2,1,0:T(8,128)S(1)} %get-tuple-element.17), channel_id=1, source_target_pairs={{0,4},{8,12},{16,20},{24,28},{4,0},{12,8},{20,16},{28,24},{1,5},{9... | collective-permute-start | bytes 663560 | tf_op jit(solution)/shard_map/ppermute | solution.py:520
  13.4 3.1 %collective-permute-start.3 = (f32[12,8,128]{2,1,0:T(8,128)S(1)}, f32[12,8,128]{2,1,0:T(8,128)S(1)}, u32[]{:S(2)}, u32[]{:S(2)}) collective-permute-start(f32[12,8,128]{2,1,0:T(8,128)S(1)} %get-tuple-element.15), channel_id=1, source_target_pairs={{4,8},{12,16},{20,24},{8,4},{16,12},{24,20},{5,9},{13,17},{21,25},... | collective-permute-start | bytes 147464 | tf_op jit(solution)/shard_map/ppermute | solution.py:521
  16.4 0.0 collective-permute-done.4.near_a
  16.4 0.0 collective-permute-done.5.near_b
  16.5 6.0 %inner.1 = (f32[16,64,128]{2,1,0:T(8,128)}, f32[16,64,128]{2,1,0:T(8,128)}, f32[6,72,128]{2,1,0:T(8,128)S(1)}, f32[30,9,8,128]{3,2,1,0:T(8,128)S(1)}) custom-call(f32[16,64,128]{2,1,0:T(8,128)S(1)} %copy-done, s32[16,64,128]{2,1,0:T(8,128)S(1)} %copy-done.1, s32[16,64,128]{2,1,0:T(8,128)S(1)} %copy-done.2, f32[8,128]{1,0:T(8,128)S(1)} %get-tuple-element.12.table, ...), custom_call_target="tpu_custom_call" | custom-call | flops 1000 | bytes 1000 | tf_op jit(solution)/shard_map/inner/pallas_call | solution.py:529
  22.4 0.0 collective-permute-done.3.far_corner
  22.4 0.0 collective-permute-done.far
  22.4 1.9 %outer.1 = (f32[16,64,128]{2,1,0:T(8,128)}, f32[16,64,128]{2,1,0:T(8,128)}) custom-call(f32[12,64,128]{2,1,0:T(8,128)S(1)} %collective-permute-done.far, f32[12,8,128]{2,1,0:T(8,128)S(1)} %collective-permute-done.3.far_corner, f32[6,72,128]{2,1,0:T(8,128)S(1)} %get-tuple-element.18.edge, ...), custom_call_target="tpu_custom_call", output_to_operand_aliasing={{0}: (4, {}), {1}: (5, {})} | custom-call | tf_op jit(solution)/shard_map/outer/pallas_call | solution.py:541
Async XLA Ops:
  0.6 7.4 %copy-start.2 = (s32[16,64,128]{2,1,0:T(8,128)S(1)}, s32[16,64,128]{2,1,0:T(8,128)}, u32[]{:S(2)}) copy-start(s32[16,64,128]{2,1,0:T(8,128)} %goal.7) | copy-start | bytes 1572868
  0.6 7.4 %copy-start.1 = (s32[16,64,128]{2,1,0:T(8,128)S(1)}, s32[16,64,128]{2,1,0:T(8,128)}, u32[]{:S(2)}) copy-start(s32[16,64,128]{2,1,0:T(8,128)} %material.7) | copy-start | bytes 1572868
  0.7 7.4 %copy-start = (f32[16,64,128]{2,1,0:T(8,128)S(1)}, f32[16,64,128]{2,1,0:T(8,128)}, u32[]{:S(2)}) copy-start(f32[16,64,128]{2,1,0:T(8,128)} %initial.3) | copy-start | bytes 1572868
  2.0 10.6 %collective-permute-start.2 = (f32[24,8,128]{2,1,0:T(8,128)S(1)}, f32[24,8,128]{2,1,0:T(8,128)S(1)}, u32[]{:S(2)}, u32[]{:S(2)}) collective-permute-start(f32[24,8,128]{2,1,0:T(8,128)S(1)} %get-tuple-element.14), channel_id=1, source_target_pairs={{1,0},{2,1},{3,2},{5,4},{6,5},{7,6},{9,8},{10,9},{11,10},{13,12},{... | collective-permute-start | bytes 294920 | tf_op jit(solution)/shard_map/ppermute | solution.py:459
  3.3 9.3 %collective-permute-start.1 = (f32[24,8,128]{2,1,0:T(8,128)S(1)}, f32[24,8,128]{2,1,0:T(8,128)S(1)}, u32[]{:S(2)}, u32[]{:S(2)}) collective-permute-start(f32[24,8,128]{2,1,0:T(8,128)S(1)} %get-tuple-element.13.up), channel_id=1, source_target_pairs={{0,1},{1,2},{2,3},{4,5},{5,6},{6,7},{8,9},{9,10},{10,11},{12,13},{... | collective-permute-start | bytes 294920 | tf_op jit(solution)/shard_map/ppermute | solution.py:459
  8.2 14.3 %collective-permute-start = (f32[12,64,128]{2,1,0:T(8,128)S(1)}, f32[12,64,128]{2,1,0:T(8,128)S(1)}, u32[]{:S(2)}, u32[]{:S(2)}) collective-permute-start(f32[12,64,128]{2,1,0:T(8,128)S(1)} %far.1), channel_id=1, source_target_pairs={{4,8},{12,16},{20,24},{8,4},{16,12},{24,20},{5,9},{13,17},{21,25},... | collective-permute-start | bytes 1179656 | tf_op jit(solution)/shard_map/ppermute | solution.py:508
  12.8 3.6 %collective-permute-start.4 = (f32[6,72,128]{2,1,0:T(8,128)S(1)}, f32[6,72,128]{2,1,0:T(8,128)S(1)}, u32[]{:S(2)}, u32[]{:S(2)}) collective-permute-start(f32[6,72,128]{2,1,0:T(8,128)S(1)} %get-tuple-element.16), channel_id=1, source_target_pairs={{0,4},{8,12},{16,20},{24,28},{4,0},{12,8},{20,16},{28,24},{1,5},{9... | collective-permute-start | bytes 663560 | tf_op jit(solution)/shard_map/ppermute | solution.py:519
  12.9 3.6 %collective-permute-start.5 = (f32[6,72,128]{2,1,0:T(8,128)S(1)}, f32[6,72,128]{2,1,0:T(8,128)S(1)}, u32[]{:S(2)}, u32[]{:S(2)}) collective-permute-start(f32[6,72,128]{2,1,0:T(8,128)S(1)} %get-tuple-element.17), channel_id=1, source_target_pairs={{0,4},{8,12},{16,20},{24,28},{4,0},{12,8},{20,16},{28,24},{1,5},{9... | collective-permute-start | bytes 663560 | tf_op jit(solution)/shard_map/ppermute | solution.py:520
  13.4 9.1 %collective-permute-start.3 = (f32[12,8,128]{2,1,0:T(8,128)S(1)}, f32[12,8,128]{2,1,0:T(8,128)S(1)}, u32[]{:S(2)}, u32[]{:S(2)}) collective-permute-start(f32[12,8,128]{2,1,0:T(8,128)S(1)} %get-tuple-element.15), channel_id=1, source_target_pairs={{4,8},{12,16},{20,24},{8,4},{16,12},{24,20},{5,9},{13,17},{21,25},... | collective-permute-start | bytes 147464 | tf_op jit(solution)/shard_map/ppermute | solution.py:521

commit v6 on v5

--- a/solution.py
+++ b/solution.py
@@ -63,10 +63,24 @@
         send[2 * HALO + i, 0:cells_y, :] = goal[start + i].astype(jnp.float32)
 
 
+def far_order(odd, cells_x):
+    last = cells_x - HALO
+    return (
+        lambda f: odd * (last + f) + (1 - odd) * (HALO - 1 - f),
+        lambda f: odd * (last + f) + (1 - odd) * max(HALO - 2 - f, 0),
+    )
+
+
 def far_kernel(u, material, goal, table, up, far):
-    cells_x = u.shape[0]
-    odd = lax.axis_index("gx") % 2
-    face_planes(far, odd * (cells_x - HALO), u, material, goal, table[0:1])
+    plane, cell = far_order(lax.axis_index("gx") % 2, u.shape[0])
+    kappa = [gather_rows(table[0:1], material[plane(f)]) for f in range(HALO)]
+    face = kappa[0] + kappa[1]
+    far[3] = face * (u[plane(0)] - u[plane(1)])
+    far[7] = face * goal[cell(0)].astype(jnp.float32)
+    for f in range(1, HALO):
+        far[f - 1] = u[plane(f)]
+        far[3 + f] = kappa[f]
+        far[7 + f] = goal[cell(f)].astype(jnp.float32)
 
 
 def halo_tiles(plane, cells_x, from_low, from_high, low_half):
@@ -90,12 +104,35 @@
     last = cells_x - HALO
     near = Halves(near_a, near_b)
     face_planes(near, (1 - odd) * last, u, material, goal, table[0:1])
-    for send, rows, start in ((near, pl.ds(cells_y, 8), (1 - odd) * last), (far_corner, slice(None), odd * last)):
+
+    def all_tiles(start):
+        us, ks, gs = [], [], []
         for i in range(HALO):
-            send[i, rows, :], send[HALO + i, rows, :] = halo_tiles(start + i, cells_x, from_low, from_high, low_half)
+            hu, hk = halo_tiles(start + i, cells_x, from_low, from_high, low_half)
+            us.append(hu)
+            ks.append(hk)
         for i in range(0, HALO, 2):
-            one, two = goal_tiles(start // 2 + i // 2, cells_x, from_low, from_high, low_half)
-            send[2 * HALO + i, rows, :], send[2 * HALO + i + 1, rows, :] = one, two
+            gs += goal_tiles(start // 2 + i // 2, cells_x, from_low, from_high, low_half)
+        return us, ks, gs
+
+    for field, tiles in enumerate(all_tiles((1 - odd) * last)):
+        for i in range(HALO):
+            near[field * HALO + i, pl.ds(cells_y, 8), :] = tiles[i]
+
+    us, ks, gs = all_tiles(odd * last)
+    is_odd = jnp.broadcast_to(odd == 1, low_half.shape)
+    us, ks = [[jnp.where(is_odd, t[f], t[HALO - 1 - f]) for f in range(HALO)] for t in (us, ks)]
+    gs = [jnp.where(is_odd, gs[f], gs[max(HALO - 2 - f, 0)]) for f in range(HALO)]
+    flux = gs[0] * (ks[0] + ks[1])
+    sub = lax.broadcasted_iota(jnp.int32, low_half.shape, 0)
+    two, four = (sub == 3) | (sub == 4), (sub >= 2) & (sub <= 5)
+    far_corner[0] = jnp.where(two, pltpu.roll(us[1], HALO, 0), us[3])
+    far_corner[1] = ks[3]
+    far_corner[2] = jnp.where(two, pltpu.roll(flux, HALO, 0), gs[3])
+    far_corner[3] = ks[2]
+    far_corner[4] = gs[2]
+    far_corner[5] = jnp.where(four, pltpu.roll(ks[1], HALO, 0), us[2])
+    far_corner[6] = gs[1]
 
 
 class Halves:
@@ -159,23 +196,29 @@
     def inner_down(self, value):
         return jnp.where(self.lane == 0, 0.0, self.down_lane(value))
 
-    def change(self, v, d, j, wx, wxm, wy, wym, wz, s):
+    def change(self, v, d, j, wx, wxm, wy, wym, wz, s, inflow=None):
         c = v(d, j)
-        along = (wx * v(d + 1, j) + wxm * v(d - 1, j)) + (wy * v(d, j + 1) + wym * v(d, j - 1))
+        below = wxm * v(d - 1, j) if inflow is None else inflow
+        along = (wx * v(d + 1, j) + below) + (wy * v(d, j + 1) + wym * v(d, j - 1))
         return along + (wz * self.up_lane(c) + self.down_lane(wz * c)) - s * c
 
-    def prelude(self, loads, start, count, finish):
+    def prelude(self, loads, start, count, finish, outermost=None):
         k, u, g = (self.reader(load, start) for load in loads)
         for j in range(self.T):
-            wx = {d: k(d, j) + k(d + 1, j) for d in range(-1, count)}
-            flux = {d: (self.sign * g(d, j)) * wx[d] for d in range(-1, count)}
+            low = -1 if outermost is None else 0
+            wx = {d: k(d, j) + k(d + 1, j) for d in range(low, count)}
+            flux = {d: (self.sign * g(d, j)) * wx[d] for d in range(low, count)}
+            inflow = None
+            if outermost is not None:
+                inflow, flux[-1] = outermost[0](j), self.sign * outermost[1](j)
             for d in range(count):
                 c = k(d, j)
                 wy, wym = c + k(d, j + 1), c + k(d, j - 1)
                 wzt, wzm = c + self.inner_up(c), c + self.inner_down(c)
                 wz = jnp.where(self.lane == self.right, 0.0, wzt)
-                s = ((wx[d] + wx[d - 1]) + (wy + wym)) + (wzt + wzm)
-                e = self.change(u, d, j, wx[d], wx[d - 1], wy, wym, wz, s)
+                wxm = wx.get(d - 1)
+                s = ((wx[d] if wxm is None else wx[d] + wxm) + (wy + wym)) + (wzt + wzm)
+                e = self.change(u, d, j, wx[d], wxm, wy, wym, wz, s, inflow if d == 0 else None)
                 finish(start + d, j, wx[d], wy, wz, s, e, flux[d] - flux[d - 1])
 
     def clear_rows(self, E, Wy, first, count):
@@ -358,16 +401,28 @@
 
 
 def outer_kernel(far, far_corner, edge, kept, ind_in, sens_in, ind, sens,
-                 U, K, G, Wx, Wy, Wz, S, EA, EB, EC, ZA, ZB, ZC, M0, Q3, AC, OI, OS, sems):
+                 U, K, G, FU, FG, Wx, Wy, Wz, S, EA, EB, EC, ZA, ZB, ZC, M0, Q3, AC, OI, OS, sems):
     cells_x, cells_y, cells_z = ind.shape
     H = HALO
     steps = Steps(cells_x, cells_y, cells_z)
     odd = steps.odd
-    for i in range(H):
-        f = (1 - odd) * i + odd * (H - 1 - i)
-        for field, (ref, at) in enumerate(((U, f), (K, f), (G, f + 1 - odd))):
-            ref[at, 0:cells_y, :] = far[field * H + i]
-            ref[at, cells_y:, :] = far_corner[field * H + i]
+    FU[0:cells_y, :] = far[3]
+    FU[cells_y:, :] = jnp.zeros((8, cells_z), jnp.float32)
+    FG[0:cells_y, :] = far[7]
+    for f in range(1, H):
+        U[f, 0:cells_y, :] = far[f - 1]
+        K[f, 0:cells_y, :] = far[3 + f]
+        G[f + 1, 0:cells_y, :] = far[7 + f]
+    tiles = [far_corner[i] for i in range(7)]
+    turned = {i: pltpu.roll(tiles[i], HALO, 0) for i in (0, 2, 5)}
+    for ref, values in (
+        (U, (turned[0], tiles[5], tiles[0])),
+        (K, (turned[5], tiles[3], tiles[1])),
+        (G, (tiles[6], tiles[4], tiles[2])),
+    ):
+        for f in range(1, H):
+            ref[f + 1 if ref is G else f, cells_y:, :] = values[f - 1]
+    FG[cells_y:, :] = turned[2]
     for d in range(2):
         U[H + d] = edge[d]
         K[H + d] = edge[2 + d]
@@ -394,11 +449,12 @@
     def begin(i, j, wx, wy, wz, s, e, z):
         Wx[i, j], Wy[i, j], Wz[i, j], S[i, j], EA[i, j], ZA[i, j] = wx, wy, wz, s, e, z
 
-    for start in (1, 3):
-        steps.prelude((steps.rower(K), steps.rower(U), first_goal), start, 2, begin)
-    for j in range(steps.T):
-        k = steps.rower(K)
-        Wx[0, j] = k(0, j) + k(1, j)
+    def fluxes(ref):
+        return lambda j: ref[pl.ds(j, 8, stride=steps.T), :]
+
+    fields = (steps.rower(K), steps.rower(U), first_goal)
+    steps.prelude(fields, 1, 2, begin, (fluxes(FU), fluxes(FG)))
+    steps.prelude(fields, 3, 2, begin)
     steps.clear_rows(EA, Wy, 1, H)
 
     @pl.when(steps.no_far)
@@ -408,7 +464,7 @@
         ZA[H - 1] = plane
         Wx[H - 1] = plane
 
-    weights = (mixed(Wx, "Wx", 0, H), mixed(Wy, "Wy", 1, H), mixed(Wz, "Wz", 1, H), mixed(S, "S", 1, H))
+    weights = (mixed(Wx, "Wx", 1, H), mixed(Wy, "Wy", 1, H), mixed(Wz, "Wz", 1, H), mixed(S, "S", 1, H))
 
     def store_a(i, j, e, em, z, zm, q):
         EB[i, j] = e + em
@@ -498,7 +554,7 @@
     from_low, from_high = exchange(up, down, "gy")
     far = pl.pallas_call(
         far_kernel,
-        out_shape=shape((3 * HALO, cells_y, cells_z), f32),
+        out_shape=shape((3 * HALO - 1, cells_y, cells_z), f32),
         in_specs=[vmem] * 4 + [whole(pl.ANY)],
         out_specs=vmem,
         compiler_params=small,
@@ -509,7 +565,7 @@
     part = shape((3 * HALO // 2, rows, cells_z), f32)
     near_a, near_b, far_corner = pl.pallas_call(
         near_kernel,
-        out_shape=(part, part, shape((3 * HALO, 8, cells_z), f32)),
+        out_shape=(part, part, shape((7, 8, cells_z), f32)),
         in_specs=[vmem] * 6 + [whole(pl.ANY)],
         out_specs=(vmem,) * 3,
         compiler_params=small,
@@ -544,7 +600,7 @@
         in_specs=[vmem] * 4 + [hbm, hbm],
         out_specs=(hbm, hbm),
         scratch_shapes=[natural(HALO + 2), natural(HALO + 2), natural(HALO + 3)]
-        + [tiles(2 * HALO)] * 13 + [natural(cells_x)] * 2 + [pltpu.SemaphoreType.DMA((2, 2))],
+        + [pltpu.VMEM((rows, cells_z), f32)] * 2 + [tiles(2 * HALO)] * 13 + [natural(cells_x)] * 2 + [pltpu.SemaphoreType.DMA((2, 2))],
         input_output_aliases={4: 0, 5: 1},
         compiler_params=small,
         name="outer",

time: 24.6 us -> 24.6 us (level)
  no operation moved by 1% of the time
where the time goes in v6:
time: 24.6 us; the launch traced here: 24.4 us
  starting transfers between devices  14 us (57%)
  Pallas kernels  9.6 us (39%)
  between operations  0.78 us (3%)
    ppermute x2, starting transfers between devices, exchange(): return (lax.ppermute(up, axis, forward), lax.ppermute(down, axis, backward))  5.96 us
    pallas_call x1, Pallas kernels, per_device(): pl.pallas_call(inner_kernel, out_shape=(block, block, shape((6, rows, cel...  5.95 us
    ppermute x1, starting transfers between devices, per_device(): far = lax.ppermute(far, 'gx', swap(far_pairs))  4.39 us
    ppermute x1, starting transfers between devices, per_device(): far_corner = lax.ppermute(far_corner, 'gx', swap(far_pairs))  3.07 us
    pallas_call x1, Pallas kernels, per_device(): pl.pallas_call(outer_kernel, out_shape=(block, block), in_specs=[vmem] *...  1.97 us
    pallas_call x1, Pallas kernels, per_device(): pl.pallas_call(edge_kernel, out_shape=(send, send, shape((8, cells_z), f3...  1.34 us
    ppermute x1, starting transfers between devices, per_device(): near_b = lax.ppermute(near_b, 'gx', swap(near_pairs))  0.5 us
  transfers between devices with their start and end apart: 6, of which 0 were waited for; matrix products, arithmetic and copies ran while one was open for 0% of the time, Pallas kernels for 26%

profile of v6, /device:TPU:1, one launch (start us, length us, event | category | flops | bytes accessed | tf_op | source)
XLA Modules:
  0.0 24.4 jit_solution(12915968253413633028)
XLA Ops:
  0.6 0.0 copy-start.2
  0.6 0.0 copy-start.1
  0.7 0.0 copy-start
  0.7 1.3 %edges.1 = (f32[24,8,128]{2,1,0:T(8,128)S(1)}, f32[24,8,128]{2,1,0:T(8,128)S(1)}, f32[8,128]{1,0:T(8,128)S(1)}) custom-call(f32[16,64,128]{2,1,0:T(8,128)} %initial.3, s32[16,64,128]{2,1,0:T(8,128)} %material.7, s32[16,64,128]{2,1,0:T(8,128)} %goal.7, f32[8]{0:T(128)} %cond.1), custom_call_target="tpu_custom_call" | custom-call | tf_op jit(solution)/shard_map/edges/pallas_call | solution.py:539
  2.0 1.3 %collective-permute-start.2 = (f32[24,8,128]{2,1,0:T(8,128)S(1)}, f32[24,8,128]{2,1,0:T(8,128)S(1)}, u32[]{:S(2)}, u32[]{:S(2)}) collective-permute-start(f32[24,8,128]{2,1,0:T(8,128)S(1)} %get-tuple-element.14), channel_id=1, source_target_pairs={{1,0},{2,1},{3,2},{5,4},{6,5},{7,6},{9,8},{10,9},{11,10},{13,12},{... | collective-permute-start | bytes 294920 | tf_op jit(solution)/shard_map/ppermute | solution.py:515
  3.3 4.7 %collective-permute-start.1 = (f32[24,8,128]{2,1,0:T(8,128)S(1)}, f32[24,8,128]{2,1,0:T(8,128)S(1)}, u32[]{:S(2)}, u32[]{:S(2)}) collective-permute-start(f32[24,8,128]{2,1,0:T(8,128)S(1)} %get-tuple-element.13.up), channel_id=1, source_target_pairs={{0,1},{1,2},{2,3},{4,5},{5,6},{6,7},{8,9},{9,10},{10,11},{12,13},{... | collective-permute-start | bytes 294920 | tf_op jit(solution)/shard_map/ppermute | solution.py:515
  8.0 0.0 copy-done.2
  8.0 0.0 copy-done.1
  8.0 0.0 copy-done
  8.0 0.2 far.1
  8.2 4.4 %collective-permute-start = (f32[11,64,128]{2,1,0:T(8,128)S(1)}, f32[11,64,128]{2,1,0:T(8,128)S(1)}, u32[]{:S(2)}, u32[]{:S(2)}) collective-permute-start(f32[11,64,128]{2,1,0:T(8,128)S(1)} %far.1), channel_id=1, source_target_pairs={{4,8},{12,16},{20,24},{8,4},{16,12},{24,20},{5,9},{13,17},{21,25},... | collective-permute-start | bytes 1081352 | tf_op jit(solution)/shard_map/ppermute | solution.py:564
  12.6 0.0 collective-permute-done.2.from_high
  12.6 0.0 collective-permute-done.1.from_low
  12.6 0.2 near.1
  12.8 0.1 collective-permute-start.4
  12.9 0.5 %collective-permute-start.5 = (f32[6,72,128]{2,1,0:T(8,128)S(1)}, f32[6,72,128]{2,1,0:T(8,128)S(1)}, u32[]{:S(2)}, u32[]{:S(2)}) collective-permute-start(f32[6,72,128]{2,1,0:T(8,128)S(1)} %get-tuple-element.17), channel_id=1, source_target_pairs={{0,4},{8,12},{16,20},{24,28},{4,0},{12,8},{20,16},{28,24},{1,5},{9... | collective-permute-start | bytes 663560 | tf_op jit(solution)/shard_map/ppermute | solution.py:576
  13.4 3.1 %collective-permute-start.3 = (f32[7,8,128]{2,1,0:T(8,128)S(1)}, f32[7,8,128]{2,1,0:T(8,128)S(1)}, u32[]{:S(2)}, u32[]{:S(2)}) collective-permute-start(f32[7,8,128]{2,1,0:T(8,128)S(1)} %get-tuple-element.15), channel_id=1, source_target_pairs={{4,8},{12,16},{20,24},{8,4},{16,12},{24,20},{5,9},{13,17},{21,25},... | collective-permute-start | bytes 86024 | tf_op jit(solution)/shard_map/ppermute | solution.py:577
  16.4 0.0 collective-permute-done.4.near_a
  16.4 0.0 collective-permute-done.5.near_b
  16.5 5.9 %inner.1 = (f32[16,64,128]{2,1,0:T(8,128)}, f32[16,64,128]{2,1,0:T(8,128)}, f32[6,72,128]{2,1,0:T(8,128)S(1)}, f32[30,9,8,128]{3,2,1,0:T(8,128)S(1)}) custom-call(f32[16,64,128]{2,1,0:T(8,128)S(1)} %copy-done, s32[16,64,128]{2,1,0:T(8,128)S(1)} %copy-done.1, s32[16,64,128]{2,1,0:T(8,128)S(1)} %copy-done.2, f32[8,128]{1,0:T(8,128)S(1)} %get-tuple-element.12.table, ...), custom_call_target="tpu_custom_call" | custom-call | flops 1000 | bytes 1000 | tf_op jit(solution)/shard_map/inner/pallas_call | solution.py:585
  22.4 0.0 collective-permute-done.3.far_corner
  22.4 0.0 collective-permute-done.far
  22.4 2.0 %outer.1 = (f32[16,64,128]{2,1,0:T(8,128)}, f32[16,64,128]{2,1,0:T(8,128)}) custom-call(f32[11,64,128]{2,1,0:T(8,128)S(1)} %collective-permute-done.far, f32[7,8,128]{2,1,0:T(8,128)S(1)} %collective-permute-done.3.far_corner, f32[6,72,128]{2,1,0:T(8,128)S(1)} %get-tuple-element.18.edge, ...), custom_call_target="tpu_custom_call", output_to_operand_aliasing={{0}: (4, {}), {1}: (5, {})} | custom-call | tf_op jit(solution)/shard_map/outer/pallas_call | solution.py:597
Async XLA Ops:
  0.6 7.4 %copy-start.2 = (s32[16,64,128]{2,1,0:T(8,128)S(1)}, s32[16,64,128]{2,1,0:T(8,128)}, u32[]{:S(2)}) copy-start(s32[16,64,128]{2,1,0:T(8,128)} %goal.7) | copy-start | bytes 1572868
  0.6 7.4 %copy-start.1 = (s32[16,64,128]{2,1,0:T(8,128)S(1)}, s32[16,64,128]{2,1,0:T(8,128)}, u32[]{:S(2)}) copy-start(s32[16,64,128]{2,1,0:T(8,128)} %material.7) | copy-start | bytes 1572868
  0.7 7.4 %copy-start = (f32[16,64,128]{2,1,0:T(8,128)S(1)}, f32[16,64,128]{2,1,0:T(8,128)}, u32[]{:S(2)}) copy-start(f32[16,64,128]{2,1,0:T(8,128)} %initial.3) | copy-start | bytes 1572868
  2.0 10.6 %collective-permute-start.2 = (f32[24,8,128]{2,1,0:T(8,128)S(1)}, f32[24,8,128]{2,1,0:T(8,128)S(1)}, u32[]{:S(2)}, u32[]{:S(2)}) collective-permute-start(f32[24,8,128]{2,1,0:T(8,128)S(1)} %get-tuple-element.14), channel_id=1, source_target_pairs={{1,0},{2,1},{3,2},{5,4},{6,5},{7,6},{9,8},{10,9},{11,10},{13,12},{... | collective-permute-start | bytes 294920 | tf_op jit(solution)/shard_map/ppermute | solution.py:515
  3.3 9.3 %collective-permute-start.1 = (f32[24,8,128]{2,1,0:T(8,128)S(1)}, f32[24,8,128]{2,1,0:T(8,128)S(1)}, u32[]{:S(2)}, u32[]{:S(2)}) collective-permute-start(f32[24,8,128]{2,1,0:T(8,128)S(1)} %get-tuple-element.13.up), channel_id=1, source_target_pairs={{0,1},{1,2},{2,3},{4,5},{5,6},{6,7},{8,9},{9,10},{10,11},{12,13},{... | collective-permute-start | bytes 294920 | tf_op jit(solution)/shard_map/ppermute | solution.py:515
  8.2 14.2 %collective-permute-start = (f32[11,64,128]{2,1,0:T(8,128)S(1)}, f32[11,64,128]{2,1,0:T(8,128)S(1)}, u32[]{:S(2)}, u32[]{:S(2)}) collective-permute-start(f32[11,64,128]{2,1,0:T(8,128)S(1)} %far.1), channel_id=1, source_target_pairs={{4,8},{12,16},{20,24},{8,4},{16,12},{24,20},{5,9},{13,17},{21,25},... | collective-permute-start | bytes 1081352 | tf_op jit(solution)/shard_map/ppermute | solution.py:564
  12.8 3.6 %collective-permute-start.4 = (f32[6,72,128]{2,1,0:T(8,128)S(1)}, f32[6,72,128]{2,1,0:T(8,128)S(1)}, u32[]{:S(2)}, u32[]{:S(2)}) collective-permute-start(f32[6,72,128]{2,1,0:T(8,128)S(1)} %get-tuple-element.16), channel_id=1, source_target_pairs={{0,4},{8,12},{16,20},{24,28},{4,0},{12,8},{20,16},{28,24},{1,5},{9... | collective-permute-start | bytes 663560 | tf_op jit(solution)/shard_map/ppermute | solution.py:575
  12.9 3.6 %collective-permute-start.5 = (f32[6,72,128]{2,1,0:T(8,128)S(1)}, f32[6,72,128]{2,1,0:T(8,128)S(1)}, u32[]{:S(2)}, u32[]{:S(2)}) collective-permute-start(f32[6,72,128]{2,1,0:T(8,128)S(1)} %get-tuple-element.17), channel_id=1, source_target_pairs={{0,4},{8,12},{16,20},{24,28},{4,0},{12,8},{20,16},{28,24},{1,5},{9... | collective-permute-start | bytes 663560 | tf_op jit(solution)/shard_map/ppermute | solution.py:576
  13.4 9.1 %collective-permute-start.3 = (f32[7,8,128]{2,1,0:T(8,128)S(1)}, f32[7,8,128]{2,1,0:T(8,128)S(1)}, u32[]{:S(2)}, u32[]{:S(2)}) collective-permute-start(f32[7,8,128]{2,1,0:T(8,128)S(1)} %get-tuple-element.15), channel_id=1, source_target_pairs={{4,8},{12,16},{20,24},{8,4},{16,12},{24,20},{5,9},{13,17},{21,25},... | collective-permute-start | bytes 86024 | tf_op jit(solution)/shard_map/ppermute | solution.py:577

commit v7 on v6

--- a/solution.py
+++ b/solution.py
@@ -290,8 +290,8 @@
     return lambda i, j: ref[i, j]
 
 
-def inner_kernel(initial, material, goal, table, from_low, from_high, near_a, near_b, ind, sens, edge, kept,
-                 U, K, G, Wx, Wy, Wz, S, EA, EB, ZA, ZB, M0, Q3, AC, OI, OS, sems):
+def inner_kernel(initial, material, goal, table, from_low, from_high, near_a, near_b, OI, OS, edge, kept,
+                 U, K, G, Wx, Wy, Wz, S, EA, EB, ZA, ZB, M0, Q3, AC):
     cells_x, cells_y, cells_z = initial.shape
     H = HALO
     steps = Steps(cells_x, cells_y, cells_z)
@@ -374,16 +374,7 @@
     many(EB, ZB, H + 3, (cells_x - 4) // 2, store_b)
     sweep(EB, ZB, top - 1, store_b, (True, False))
 
-    def leave(p):
-        f = H + 4 + 2 * p
-        return steps.leave((1 - odd) * (f - H) + odd * (top - 2 - f), OI, OS, ind, sens, sems, p)
-
-    def last(p):
-        sweep(EA, ZA, H + 4 + 2 * p, store_c, (True, True))
-        for move in leave(p):
-            move.start()
-
-    turns((cells_x - 4) // 2, last)
+    turns((cells_x - 4) // 2, lambda p: sweep(EA, ZA, H + 4 + 2 * p, store_c, (True, True)))
     refs = dict(EA=EA, ZA=ZA, EB=EB, ZB=ZB, Wx=Wx, Wy=Wy, Wz=Wz, S=S, M0=M0, Q3=Q3, AC=AC)
     at = 0
     for name, first, count in KEPT:
@@ -392,20 +383,20 @@
             kept[at + d] = refs[name][first - shift + d]
         at += count
 
-    def settle(p, _):
-        for move in leave(p):
-            move.wait()
-        return 0
-
-    lax.fori_loop(0, (cells_x - 4) // 2, settle, 0)
-
-
-def outer_kernel(far, far_corner, edge, kept, ind_in, sens_in, ind, sens,
+
+def outer_kernel(far, far_corner, edge, kept, inner_ind, inner_sens, ind, sens,
                  U, K, G, FU, FG, Wx, Wy, Wz, S, EA, EB, EC, ZA, ZB, ZC, M0, Q3, AC, OI, OS, sems):
     cells_x, cells_y, cells_z = ind.shape
     H = HALO
     steps = Steps(cells_x, cells_y, cells_z)
     odd = steps.odd
+    done = pl.ds((1 - odd) * H, cells_x - H)
+    moves = [
+        pltpu.make_async_copy(source.at[done, pl.ds(0, cells_y), :], target.at[done], sems.at[k, 2])
+        for k, (source, target) in enumerate(((inner_ind, ind), (inner_sens, sens)))
+    ]
+    for move in moves:
+        move.start()
     FU[0:cells_y, :] = far[3]
     FU[cells_y:, :] = jnp.zeros((8, cells_z), jnp.float32)
     FG[0:cells_y, :] = far[7]
@@ -446,7 +437,21 @@
     def first_goal(i, j):
         return G[i + 1, pl.ds(j, 8, stride=steps.T), :]
 
+    sub = lax.broadcasted_iota(jnp.int32, (8, cells_z), 0)
+    T = steps.T
+    no_far, no_low, no_high = (
+        jnp.broadcast_to(flag, sub.shape) for flag in (steps.no_far, steps.no_low, steps.no_high))
+
+    def cleared(value, j, r, flag):
+        if r % T != j:
+            return value
+        return jnp.where((sub == r // T) & flag, 0.0, value)
+
     def begin(i, j, wx, wy, wz, s, e, z):
+        e = cleared(cleared(e, j, steps.rows - 1, no_low), j, cells_y, no_high)
+        wy = cleared(cleared(wy, j, steps.rows - 1, no_low), j, cells_y - 1, no_high)
+        if i == H - 1:
+            wx, e, z = (jnp.where(no_far, 0.0, value) for value in (wx, e, z))
         Wx[i, j], Wy[i, j], Wz[i, j], S[i, j], EA[i, j], ZA[i, j] = wx, wy, wz, s, e, z
 
     def fluxes(ref):
@@ -455,15 +460,6 @@
     fields = (steps.rower(K), steps.rower(U), first_goal)
     steps.prelude(fields, 1, 2, begin, (fluxes(FU), fluxes(FG)))
     steps.prelude(fields, 3, 2, begin)
-    steps.clear_rows(EA, Wy, 1, H)
-
-    @pl.when(steps.no_far)
-    def _():
-        plane = jnp.zeros((steps.T, 8, cells_z), jnp.float32)
-        EA[H - 1] = plane
-        ZA[H - 1] = plane
-        Wx[H - 1] = plane
-
     weights = (mixed(Wx, "Wx", 1, H), mixed(Wy, "Wy", 1, H), mixed(Wz, "Wz", 1, H), mixed(S, "S", 1, H))
 
     def store_a(i, j, e, em, z, zm, q):
@@ -493,7 +489,6 @@
     steps.sweep(first, 4, 2, store_a, (True, True))
     steps.sweep(second, 3, 2, store_b, (False, True))
     steps.sweep(second, 5, 2, store_b, (True, True))
-    moves = []
     for p in range(2):
         f = H + 2 * p
         steps.sweep(third, f, 2, store_c, (True, True))
@@ -582,14 +577,14 @@
     def natural(count):
         return pltpu.VMEM((count, rows, cells_z), f32)
 
+    wide_block = shape((cells_x, rows, cells_z), f32)
     ind, sens, edge, kept = pl.pallas_call(
         inner_kernel,
-        out_shape=(block, block, shape((6, rows, cells_z), f32), shape((KEPT_PLANES, rows // 8, 8, cells_z), f32)),
+        out_shape=(wide_block, wide_block, shape((6, rows, cells_z), f32), shape((KEPT_PLANES, rows // 8, 8, cells_z), f32)),
         in_specs=[vmem] * 8,
-        out_specs=(hbm, hbm, vmem, vmem),
+        out_specs=(vmem,) * 4,
         scratch_shapes=[natural(planes), natural(planes), natural(planes + 1)]
-        + [tiles(planes)] * 8 + [tiles(cells_x)] * 3 + [natural(cells_x)] * 2
-        + [pltpu.SemaphoreType.DMA((2, (cells_x - 4) // 2))],
+        + [tiles(planes)] * 8 + [tiles(cells_x)] * 3,
         compiler_params=params,
         cost_estimate=pl.CostEstimate(flops=1000, bytes_accessed=1000, transcendentals=0),
         name="inner",
@@ -597,11 +592,10 @@
     return pl.pallas_call(
         outer_kernel,
         out_shape=(block, block),
-        in_specs=[vmem] * 4 + [hbm, hbm],
+        in_specs=[vmem] * 6,
         out_specs=(hbm, hbm),
         scratch_shapes=[natural(HALO + 2), natural(HALO + 2), natural(HALO + 3)]
-        + [pltpu.VMEM((rows, cells_z), f32)] * 2 + [tiles(2 * HALO)] * 13 + [natural(cells_x)] * 2 + [pltpu.SemaphoreType.DMA((2, 2))],
-        input_output_aliases={4: 0, 5: 1},
+        + [pltpu.VMEM((rows, cells_z), f32)] * 2 + [tiles(2 * HALO)] * 13 + [natural(cells_x)] * 2 + [pltpu.SemaphoreType.DMA((2, 3))],
         compiler_params=small,
         name="outer",
     )(far, far_corner, edge, kept, ind, sens)

time: 24.6 us -> 23.8 us (0.967)
  Pallas kernels: 9.6 us -> 8.84 us
    pallas_call x1, Pallas kernels: 5.95 us -> 5.26 us  [per_device(): pl.pallas_call(inner_kernel, out_shape=(wide_block, wide_block, shape((6,...]
  transfers between devices with their start and end apart: 6 -> 6, of which waited for: 0 -> 0; matrix products, arithmetic and copies ran while one was open for 0% -> 0% of each run, Pallas kernels for 26% -> 24%
where the time goes in v7:
time: 23.8 us; the launch traced here: 23.6 us
  starting transfers between devices  14 us (59%)
  Pallas kernels  8.84 us (37%)
  between operations  0.78 us (3%)
    ppermute x2, starting transfers between devices, exchange(): return (lax.ppermute(up, axis, forward), lax.ppermute(down, axis, backward))  5.96 us
    pallas_call x1, Pallas kernels, per_device(): pl.pallas_call(inner_kernel, out_shape=(wide_block, wide_block, shape((6,...  5.26 us
    ppermute x1, starting transfers between devices, per_device(): far = lax.ppermute(far, 'gx', swap(far_pairs))  4.39 us
    ppermute x1, starting transfers between devices, per_device(): far_corner = lax.ppermute(far_corner, 'gx', swap(far_pairs))  3.07 us
    pallas_call x1, Pallas kernels, per_device(): pl.pallas_call(outer_kernel, out_shape=(block, block), in_specs=[vmem] *...  1.89 us
    pallas_call x1, Pallas kernels, per_device(): pl.pallas_call(edge_kernel, out_shape=(send, send, shape((8, cells_z), f3...  1.34 us
    ppermute x1, starting transfers between devices, per_device(): near_b = lax.ppermute(near_b, 'gx', swap(near_pairs))  0.5 us
  transfers between devices with their start and end apart: 6, of which 0 were waited for; matrix products, arithmetic and copies ran while one was open for 0% of the time, Pallas kernels for 24%

profile of v7, /device:TPU:1, one launch (start us, length us, event | category | flops | bytes accessed | tf_op | source)
XLA Modules:
  0.0 23.6 jit_solution(2387201011858819389)
XLA Ops:
  0.6 0.0 copy-start.2
  0.6 0.0 copy-start.1
  0.7 0.0 copy-start
  0.7 1.3 %edges.1 = (f32[24,8,128]{2,1,0:T(8,128)S(1)}, f32[24,8,128]{2,1,0:T(8,128)S(1)}, f32[8,128]{1,0:T(8,128)S(1)}) custom-call(f32[16,64,128]{2,1,0:T(8,128)} %initial.3, s32[16,64,128]{2,1,0:T(8,128)} %material.7, s32[16,64,128]{2,1,0:T(8,128)} %goal.7, f32[8]{0:T(128)} %cond.1), custom_call_target="tpu_custom_call" | custom-call | tf_op jit(solution)/shard_map/edges/pallas_call | solution.py:534
  2.0 1.3 %collective-permute-start.2 = (f32[24,8,128]{2,1,0:T(8,128)S(1)}, f32[24,8,128]{2,1,0:T(8,128)S(1)}, u32[]{:S(2)}, u32[]{:S(2)}) collective-permute-start(f32[24,8,128]{2,1,0:T(8,128)S(1)} %get-tuple-element.14), channel_id=1, source_target_pairs={{1,0},{2,1},{3,2},{5,4},{6,5},{7,6},{9,8},{10,9},{11,10},{13,12},{... | collective-permute-start | bytes 294920 | tf_op jit(solution)/shard_map/ppermute | solution.py:510
  3.3 4.7 %collective-permute-start.1 = (f32[24,8,128]{2,1,0:T(8,128)S(1)}, f32[24,8,128]{2,1,0:T(8,128)S(1)}, u32[]{:S(2)}, u32[]{:S(2)}) collective-permute-start(f32[24,8,128]{2,1,0:T(8,128)S(1)} %get-tuple-element.13.up), channel_id=1, source_target_pairs={{0,1},{1,2},{2,3},{4,5},{5,6},{6,7},{8,9},{9,10},{10,11},{12,13},{... | collective-permute-start | bytes 294920 | tf_op jit(solution)/shard_map/ppermute | solution.py:510
  8.0 0.0 copy-done.2
  8.0 0.0 copy-done.1
  8.0 0.0 copy-done
  8.0 0.2 far.1
  8.2 4.4 %collective-permute-start = (f32[11,64,128]{2,1,0:T(8,128)S(1)}, f32[11,64,128]{2,1,0:T(8,128)S(1)}, u32[]{:S(2)}, u32[]{:S(2)}) collective-permute-start(f32[11,64,128]{2,1,0:T(8,128)S(1)} %far.1), channel_id=1, source_target_pairs={{4,8},{12,16},{20,24},{8,4},{16,12},{24,20},{5,9},{13,17},{21,25},... | collective-permute-start | bytes 1081352 | tf_op jit(solution)/shard_map/ppermute | solution.py:559
  12.6 0.0 collective-permute-done.2.from_high
  12.6 0.0 collective-permute-done.1.from_low
  12.6 0.2 near.1
  12.8 0.1 collective-permute-start.4
  12.9 0.5 %collective-permute-start.5 = (f32[6,72,128]{2,1,0:T(8,128)S(1)}, f32[6,72,128]{2,1,0:T(8,128)S(1)}, u32[]{:S(2)}, u32[]{:S(2)}) collective-permute-start(f32[6,72,128]{2,1,0:T(8,128)S(1)} %get-tuple-element.17), channel_id=1, source_target_pairs={{0,4},{8,12},{16,20},{24,28},{4,0},{12,8},{20,16},{28,24},{1,5},{9... | collective-permute-start | bytes 663560 | tf_op jit(solution)/shard_map/ppermute | solution.py:571
  13.4 3.1 %collective-permute-start.3 = (f32[7,8,128]{2,1,0:T(8,128)S(1)}, f32[7,8,128]{2,1,0:T(8,128)S(1)}, u32[]{:S(2)}, u32[]{:S(2)}) collective-permute-start(f32[7,8,128]{2,1,0:T(8,128)S(1)} %get-tuple-element.15), channel_id=1, source_target_pairs={{4,8},{12,16},{20,24},{8,4},{16,12},{24,20},{5,9},{13,17},{21,25},... | collective-permute-start | bytes 86024 | tf_op jit(solution)/shard_map/ppermute | solution.py:572
  16.4 0.0 collective-permute-done.4.near_a
  16.4 0.0 collective-permute-done.5.near_b
  16.5 5.3 %inner.1 = (f32[16,72,128]{2,1,0:T(8,128)S(1)}, f32[16,72,128]{2,1,0:T(8,128)S(1)}, f32[6,72,128]{2,1,0:T(8,128)S(1)}, f32[30,9,8,128]{3,2,1,0:T(8,128)S(1)}) custom-call(f32[16,64,128]{2,1,0:T(8,128)S(1)} %copy-done, s32[16,64,128]{2,1,0:T(8,128)S(1)} %copy-done.1, s32[16,64,128]{2,1,0:T(8,128)S(1)} %copy-done.2, f32[8,128]{1,0:T(8,128)S(1)} %get-tuple-element.12.table, ...), custom_call_target="tpu_custom_call" | custom-call | flops 1000 | bytes 1000 | tf_op jit(solution)/shard_map/inner/pallas_call | solution.py:581
  21.7 0.0 collective-permute-done.3.far_corner
  21.7 0.0 collective-permute-done.far
  21.7 1.9 %outer.1 = (f32[16,64,128]{2,1,0:T(8,128)}, f32[16,64,128]{2,1,0:T(8,128)}) custom-call(f32[11,64,128]{2,1,0:T(8,128)S(1)} %collective-permute-done.far, f32[7,8,128]{2,1,0:T(8,128)S(1)} %collective-permute-done.3.far_corner, f32[6,72,128]{2,1,0:T(8,128)S(1)} %get-tuple-element.18.edge, f32[30,9,8,128]{3,2,1,0:T(8,128)S(1)} %get-tuple-element.19.kept, ...), custom_call_target="tpu_custom_call" | custom-call | tf_op jit(solution)/shard_map/outer/pallas_call | solution.py:592
Async XLA Ops:
  0.6 7.4 %copy-start.2 = (s32[16,64,128]{2,1,0:T(8,128)S(1)}, s32[16,64,128]{2,1,0:T(8,128)}, u32[]{:S(2)}) copy-start(s32[16,64,128]{2,1,0:T(8,128)} %goal.7) | copy-start | bytes 1572868
  0.6 7.4 %copy-start.1 = (s32[16,64,128]{2,1,0:T(8,128)S(1)}, s32[16,64,128]{2,1,0:T(8,128)}, u32[]{:S(2)}) copy-start(s32[16,64,128]{2,1,0:T(8,128)} %material.7) | copy-start | bytes 1572868
  0.7 7.4 %copy-start = (f32[16,64,128]{2,1,0:T(8,128)S(1)}, f32[16,64,128]{2,1,0:T(8,128)}, u32[]{:S(2)}) copy-start(f32[16,64,128]{2,1,0:T(8,128)} %initial.3) | copy-start | bytes 1572868
  2.0 10.6 %collective-permute-start.2 = (f32[24,8,128]{2,1,0:T(8,128)S(1)}, f32[24,8,128]{2,1,0:T(8,128)S(1)}, u32[]{:S(2)}, u32[]{:S(2)}) collective-permute-start(f32[24,8,128]{2,1,0:T(8,128)S(1)} %get-tuple-element.14), channel_id=1, source_target_pairs={{1,0},{2,1},{3,2},{5,4},{6,5},{7,6},{9,8},{10,9},{11,10},{13,12},{... | collective-permute-start | bytes 294920 | tf_op jit(solution)/shard_map/ppermute | solution.py:510
  3.3 9.3 %collective-permute-start.1 = (f32[24,8,128]{2,1,0:T(8,128)S(1)}, f32[24,8,128]{2,1,0:T(8,128)S(1)}, u32[]{:S(2)}, u32[]{:S(2)}) collective-permute-start(f32[24,8,128]{2,1,0:T(8,128)S(1)} %get-tuple-element.13.up), channel_id=1, source_target_pairs={{0,1},{1,2},{2,3},{4,5},{5,6},{6,7},{8,9},{9,10},{10,11},{12,13},{... | collective-permute-start | bytes 294920 | tf_op jit(solution)/shard_map/ppermute | solution.py:510
  8.2 13.6 %collective-permute-start = (f32[11,64,128]{2,1,0:T(8,128)S(1)}, f32[11,64,128]{2,1,0:T(8,128)S(1)}, u32[]{:S(2)}, u32[]{:S(2)}) collective-permute-start(f32[11,64,128]{2,1,0:T(8,128)S(1)} %far.1), channel_id=1, source_target_pairs={{4,8},{12,16},{20,24},{8,4},{16,12},{24,20},{5,9},{13,17},{21,25},... | collective-permute-start | bytes 1081352 | tf_op jit(solution)/shard_map/ppermute | solution.py:559
  12.8 3.6 %collective-permute-start.4 = (f32[6,72,128]{2,1,0:T(8,128)S(1)}, f32[6,72,128]{2,1,0:T(8,128)S(1)}, u32[]{:S(2)}, u32[]{:S(2)}) collective-permute-start(f32[6,72,128]{2,1,0:T(8,128)S(1)} %get-tuple-element.16), channel_id=1, source_target_pairs={{0,4},{8,12},{16,20},{24,28},{4,0},{12,8},{20,16},{28,24},{1,5},{9... | collective-permute-start | bytes 663560 | tf_op jit(solution)/shard_map/ppermute | solution.py:570
  12.9 3.6 %collective-permute-start.5 = (f32[6,72,128]{2,1,0:T(8,128)S(1)}, f32[6,72,128]{2,1,0:T(8,128)S(1)}, u32[]{:S(2)}, u32[]{:S(2)}) collective-permute-start(f32[6,72,128]{2,1,0:T(8,128)S(1)} %get-tuple-element.17), channel_id=1, source_target_pairs={{0,4},{8,12},{16,20},{24,28},{4,0},{12,8},{20,16},{28,24},{1,5},{9... | collective-permute-start | bytes 663560 | tf_op jit(solution)/shard_map/ppermute | solution.py:571
  13.4 8.4 %collective-permute-start.3 = (f32[7,8,128]{2,1,0:T(8,128)S(1)}, f32[7,8,128]{2,1,0:T(8,128)S(1)}, u32[]{:S(2)}, u32[]{:S(2)}) collective-permute-start(f32[7,8,128]{2,1,0:T(8,128)S(1)} %get-tuple-element.15), channel_id=1, source_target_pairs={{4,8},{12,16},{20,24},{8,4},{16,12},{24,20},{5,9},{13,17},{21,25},... | collective-permute-start | bytes 86024 | tf_op jit(solution)/shard_map/ppermute | solution.py:572

commit v8 on v7

--- a/solution.py
+++ b/solution.py
@@ -273,7 +273,7 @@
 KEPT_PLANES = sum(count for _, _, count in KEPT)
 
 
-def turns(count, body, together=3):
+def turns(count, body, together=9):
     full = count // together
 
     def turn(p, _):
@@ -458,8 +458,8 @@
         return lambda j: ref[pl.ds(j, 8, stride=steps.T), :]
 
     fields = (steps.rower(K), steps.rower(U), first_goal)
+    steps.prelude(fields, 3, 2, begin)
     steps.prelude(fields, 1, 2, begin, (fluxes(FU), fluxes(FG)))
-    steps.prelude(fields, 3, 2, begin)
     weights = (mixed(Wx, "Wx", 1, H), mixed(Wy, "Wy", 1, H), mixed(Wz, "Wz", 1, H), mixed(S, "S", 1, H))
 
     def store_a(i, j, e, em, z, zm, q):
@@ -485,11 +485,11 @@
     first = (mixed(EA, "EA", 1, H), mixed(ZA, "ZA", 1, H)) + weights
     second = (mixed(EB, "EB", 2, H + 1), mixed(ZB, "ZB", 2, H + 1)) + weights
     third = (mixed(EC, "EA", 3, H + 2), mixed(ZC, "ZA", 3, H + 2)) + weights
+    steps.sweep(first, 4, 2, store_a, (True, True))
     steps.sweep(first, 2, 2, store_a, (False, False))
-    steps.sweep(first, 4, 2, store_a, (True, True))
+    steps.sweep(second, 5, 2, store_b, (True, True))
     steps.sweep(second, 3, 2, store_b, (False, True))
-    steps.sweep(second, 5, 2, store_b, (True, True))
-    for p in range(2):
+    for p in (1, 0):
         f = H + 2 * p
         steps.sweep(third, f, 2, store_c, (True, True))
         moves += steps.leave((1 - odd) * (f - H) + odd * (top - 2 - f), OI, OS, ind, sens, sems, p)

time: 23.8 us -> 23.3 us (0.979)
  Pallas kernels: 8.84 us -> 8.12 us
    pallas_call x1, Pallas kernels: 5.26 us -> 4.61 us  [per_device(): pl.pallas_call(inner_kernel, out_shape=(wide_block, wide_block, shape((6,...]
  transfers between devices with their start and end apart: 6 -> 6, of which waited for: 0 -> 1; matrix products, arithmetic and copies ran while one was open for 0% -> 0% of each run, Pallas kernels for 24% -> 21%
where the time goes in v8:
time: 23.3 us; the launch traced here: 23.1 us
  starting transfers between devices  14 us (60%)
  Pallas kernels  8.12 us (35%)
  between operations  0.77 us (3%)
    ppermute x2, starting transfers between devices, exchange(): return (lax.ppermute(up, axis, forward), lax.ppermute(down, axis, backward))  5.96 us
    pallas_call x1, Pallas kernels, per_device(): pl.pallas_call(inner_kernel, out_shape=(wide_block, wide_block, shape((6,...  4.61 us
    ppermute x1, starting transfers between devices, per_device(): far = lax.ppermute(far, 'gx', swap(far_pairs))  4.39 us
    ppermute x1, starting transfers between devices, per_device(): far_corner = lax.ppermute(far_corner, 'gx', swap(far_pairs))  3.07 us
    pallas_call x1, Pallas kernels, per_device(): pl.pallas_call(outer_kernel, out_shape=(block, block), in_specs=[vmem] *...  1.82 us
    pallas_call x1, Pallas kernels, per_device(): pl.pallas_call(edge_kernel, out_shape=(send, send, shape((8, cells_z), f3...  1.34 us
    ppermute x1, starting transfers between devices, per_device(): near_b = lax.ppermute(near_b, 'gx', swap(near_pairs))  0.5 us
  transfers between devices with their start and end apart: 6, of which 1 were waited for; matrix products, arithmetic and copies ran while one was open for 0% of the time, Pallas kernels for 21%

profile of v8, /device:TPU:1, one launch (start us, length us, event | category | flops | bytes accessed | tf_op | source)
XLA Modules:
  0.0 23.1 jit_solution(9707718182744869401)
XLA Ops:
  0.6 0.0 copy-start.2
  0.6 0.0 copy-start.1
  0.7 0.0 copy-start
  0.7 1.3 %edges.1 = (f32[24,8,128]{2,1,0:T(8,128)S(1)}, f32[24,8,128]{2,1,0:T(8,128)S(1)}, f32[8,128]{1,0:T(8,128)S(1)}) custom-call(f32[16,64,128]{2,1,0:T(8,128)} %initial.3, s32[16,64,128]{2,1,0:T(8,128)} %material.7, s32[16,64,128]{2,1,0:T(8,128)} %goal.7, f32[8]{0:T(128)} %cond.1), custom_call_target="tpu_custom_call" | custom-call | tf_op jit(solution)/shard_map/edges/pallas_call | solution.py:534
  2.0 1.3 %collective-permute-start.2 = (f32[24,8,128]{2,1,0:T(8,128)S(1)}, f32[24,8,128]{2,1,0:T(8,128)S(1)}, u32[]{:S(2)}, u32[]{:S(2)}) collective-permute-start(f32[24,8,128]{2,1,0:T(8,128)S(1)} %get-tuple-element.14), channel_id=1, source_target_pairs={{1,0},{2,1},{3,2},{5,4},{6,5},{7,6},{9,8},{10,9},{11,10},{13,12},{... | collective-permute-start | bytes 294920 | tf_op jit(solution)/shard_map/ppermute | solution.py:510
  3.3 4.7 %collective-permute-start.1 = (f32[24,8,128]{2,1,0:T(8,128)S(1)}, f32[24,8,128]{2,1,0:T(8,128)S(1)}, u32[]{:S(2)}, u32[]{:S(2)}) collective-permute-start(f32[24,8,128]{2,1,0:T(8,128)S(1)} %get-tuple-element.13.up), channel_id=1, source_target_pairs={{0,1},{1,2},{2,3},{4,5},{5,6},{6,7},{8,9},{9,10},{10,11},{12,13},{... | collective-permute-start | bytes 294920 | tf_op jit(solution)/shard_map/ppermute | solution.py:510
  8.0 0.0 copy-done.2
  8.0 0.0 copy-done.1
  8.0 0.0 copy-done
  8.0 0.2 far.1
  8.2 4.4 %collective-permute-start = (f32[11,64,128]{2,1,0:T(8,128)S(1)}, f32[11,64,128]{2,1,0:T(8,128)S(1)}, u32[]{:S(2)}, u32[]{:S(2)}) collective-permute-start(f32[11,64,128]{2,1,0:T(8,128)S(1)} %far.1), channel_id=1, source_target_pairs={{4,8},{12,16},{20,24},{8,4},{16,12},{24,20},{5,9},{13,17},{21,25},... | collective-permute-start | bytes 1081352 | tf_op jit(solution)/shard_map/ppermute | solution.py:559
  12.6 0.0 collective-permute-done.2.from_high
  12.6 0.0 collective-permute-done.1.from_low
  12.6 0.2 near.1
  12.8 0.1 collective-permute-start.4
  12.9 0.5 %collective-permute-start.5 = (f32[6,72,128]{2,1,0:T(8,128)S(1)}, f32[6,72,128]{2,1,0:T(8,128)S(1)}, u32[]{:S(2)}, u32[]{:S(2)}) collective-permute-start(f32[6,72,128]{2,1,0:T(8,128)S(1)} %get-tuple-element.17), channel_id=1, source_target_pairs={{0,4},{8,12},{16,20},{24,28},{4,0},{12,8},{20,16},{28,24},{1,5},{9... | collective-permute-start | bytes 663560 | tf_op jit(solution)/shard_map/ppermute | solution.py:571
  13.4 3.1 %collective-permute-start.3 = (f32[7,8,128]{2,1,0:T(8,128)S(1)}, f32[7,8,128]{2,1,0:T(8,128)S(1)}, u32[]{:S(2)}, u32[]{:S(2)}) collective-permute-start(f32[7,8,128]{2,1,0:T(8,128)S(1)} %get-tuple-element.15), channel_id=1, source_target_pairs={{4,8},{12,16},{20,24},{8,4},{16,12},{24,20},{5,9},{13,17},{21,25},... | collective-permute-start | bytes 86024 | tf_op jit(solution)/shard_map/ppermute | solution.py:572
  16.4 0.0 collective-permute-done.4.near_a
  16.4 0.0 collective-permute-done.5.near_b
  16.5 4.6 %inner.1 = (f32[16,72,128]{2,1,0:T(8,128)S(1)}, f32[16,72,128]{2,1,0:T(8,128)S(1)}, f32[6,72,128]{2,1,0:T(8,128)S(1)}, f32[30,9,8,128]{3,2,1,0:T(8,128)S(1)}) custom-call(f32[16,64,128]{2,1,0:T(8,128)S(1)} %copy-done, s32[16,64,128]{2,1,0:T(8,128)S(1)} %copy-done.1, s32[16,64,128]{2,1,0:T(8,128)S(1)} %copy-done.2, f32[8,128]{1,0:T(8,128)S(1)} %get-tuple-element.12.table, ...), custom_call_target="tpu_custom_call" | custom-call | flops 1000 | bytes 1000 | tf_op jit(solution)/shard_map/inner/pallas_call | solution.py:581
  21.1 0.2 collective-permute-done.3.far_corner
  21.3 0.0 collective-permute-done.far
  21.3 1.8 %outer.1 = (f32[16,64,128]{2,1,0:T(8,128)}, f32[16,64,128]{2,1,0:T(8,128)}) custom-call(f32[11,64,128]{2,1,0:T(8,128)S(1)} %collective-permute-done.far, f32[7,8,128]{2,1,0:T(8,128)S(1)} %collective-permute-done.3.far_corner, f32[6,72,128]{2,1,0:T(8,128)S(1)} %get-tuple-element.18.edge, f32[30,9,8,128]{3,2,1,0:T(8,128)S(1)} %get-tuple-element.19.kept, ...), custom_call_target="tpu_custom_call" | custom-call | tf_op jit(solution)/shard_map/outer/pallas_call | solution.py:592
Async XLA Ops:
  0.6 7.4 %copy-start.2 = (s32[16,64,128]{2,1,0:T(8,128)S(1)}, s32[16,64,128]{2,1,0:T(8,128)}, u32[]{:S(2)}) copy-start(s32[16,64,128]{2,1,0:T(8,128)} %goal.7) | copy-start | bytes 1572868
  0.6 7.4 %copy-start.1 = (s32[16,64,128]{2,1,0:T(8,128)S(1)}, s32[16,64,128]{2,1,0:T(8,128)}, u32[]{:S(2)}) copy-start(s32[16,64,128]{2,1,0:T(8,128)} %material.7) | copy-start | bytes 1572868
  0.7 7.4 %copy-start = (f32[16,64,128]{2,1,0:T(8,128)S(1)}, f32[16,64,128]{2,1,0:T(8,128)}, u32[]{:S(2)}) copy-start(f32[16,64,128]{2,1,0:T(8,128)} %initial.3) | copy-start | bytes 1572868
  2.0 10.6 %collective-permute-start.2 = (f32[24,8,128]{2,1,0:T(8,128)S(1)}, f32[24,8,128]{2,1,0:T(8,128)S(1)}, u32[]{:S(2)}, u32[]{:S(2)}) collective-permute-start(f32[24,8,128]{2,1,0:T(8,128)S(1)} %get-tuple-element.14), channel_id=1, source_target_pairs={{1,0},{2,1},{3,2},{5,4},{6,5},{7,6},{9,8},{10,9},{11,10},{13,12},{... | collective-permute-start | bytes 294920 | tf_op jit(solution)/shard_map/ppermute | solution.py:510
  3.3 9.3 %collective-permute-start.1 = (f32[24,8,128]{2,1,0:T(8,128)S(1)}, f32[24,8,128]{2,1,0:T(8,128)S(1)}, u32[]{:S(2)}, u32[]{:S(2)}) collective-permute-start(f32[24,8,128]{2,1,0:T(8,128)S(1)} %get-tuple-element.13.up), channel_id=1, source_target_pairs={{0,1},{1,2},{2,3},{4,5},{5,6},{6,7},{8,9},{9,10},{10,11},{12,13},{... | collective-permute-start | bytes 294920 | tf_op jit(solution)/shard_map/ppermute | solution.py:510
  8.2 13.1 %collective-permute-start = (f32[11,64,128]{2,1,0:T(8,128)S(1)}, f32[11,64,128]{2,1,0:T(8,128)S(1)}, u32[]{:S(2)}, u32[]{:S(2)}) collective-permute-start(f32[11,64,128]{2,1,0:T(8,128)S(1)} %far.1), channel_id=1, source_target_pairs={{4,8},{12,16},{20,24},{8,4},{16,12},{24,20},{5,9},{13,17},{21,25},... | collective-permute-start | bytes 1081352 | tf_op jit(solution)/shard_map/ppermute | solution.py:559
  12.8 3.6 %collective-permute-start.4 = (f32[6,72,128]{2,1,0:T(8,128)S(1)}, f32[6,72,128]{2,1,0:T(8,128)S(1)}, u32[]{:S(2)}, u32[]{:S(2)}) collective-permute-start(f32[6,72,128]{2,1,0:T(8,128)S(1)} %get-tuple-element.16), channel_id=1, source_target_pairs={{0,4},{8,12},{16,20},{24,28},{4,0},{12,8},{20,16},{28,24},{1,5},{9... | collective-permute-start | bytes 663560 | tf_op jit(solution)/shard_map/ppermute | solution.py:570
  12.9 3.6 %collective-permute-start.5 = (f32[6,72,128]{2,1,0:T(8,128)S(1)}, f32[6,72,128]{2,1,0:T(8,128)S(1)}, u32[]{:S(2)}, u32[]{:S(2)}) collective-permute-start(f32[6,72,128]{2,1,0:T(8,128)S(1)} %get-tuple-element.17), channel_id=1, source_target_pairs={{0,4},{8,12},{16,20},{24,28},{4,0},{12,8},{20,16},{28,24},{1,5},{9... | collective-permute-start | bytes 663560 | tf_op jit(solution)/shard_map/ppermute | solution.py:571
  13.4 7.9 %collective-permute-start.3 = (f32[7,8,128]{2,1,0:T(8,128)S(1)}, f32[7,8,128]{2,1,0:T(8,128)S(1)}, u32[]{:S(2)}, u32[]{:S(2)}) collective-permute-start(f32[7,8,128]{2,1,0:T(8,128)S(1)} %get-tuple-element.15), channel_id=1, source_target_pairs={{4,8},{12,16},{20,24},{8,4},{16,12},{24,20},{5,9},{13,17},{21,25},... | collective-permute-start | bytes 86024 | tf_op jit(solution)/shard_map/ppermute | solution.py:572

commit v9 on v8

--- a/solution.py
+++ b/solution.py
@@ -28,13 +28,13 @@
     return jnp.take_along_axis(jnp.broadcast_to(table, index.shape), index, axis=1, mode="promise_in_bounds")
 
 
-def edge_kernel(initial, material, goal, cond, up, down, shared, u, ids, flags, values, sems):
+def edge_kernel(initial, material, goal, cond, first, second, shared, u, ids, flags, values, sems):
     cells_x, cells_y, cells_z = initial.shape
     moves = [pltpu.make_async_copy(cond, values, sems.at[6])]
-    for end, first in enumerate((0, cells_y - 8)):
+    for end, row in enumerate((0, cells_y - 8)):
         for k, (source, target) in enumerate(((material, ids), (initial, u), (goal, flags))):
             moves.append(pltpu.make_async_copy(
-                source.at[:, pl.ds(first, 8), :], target.at[end], sems.at[3 * end + k]))
+                source.at[:, pl.ds(row, 8), :], target.at[end], sems.at[3 * end + k]))
     for move in moves:
         move.start()
     low_half = lax.broadcasted_iota(jnp.int32, (8, cells_z), 0) < HALO
@@ -43,16 +43,21 @@
     shared[...] = jnp.broadcast_to(table, shared.shape)
     for move in moves[1:]:
         move.wait()
+    even = jnp.broadcast_to(lax.axis_index("gy") % 2 == 0, low_half.shape)
+
+    def put(i, up, down):
+        first[i] = jnp.where(even, up, down)
+        second[i] = jnp.where(even, down, up)
+
     for i in range(cells_x):
         k_low = pltpu.roll(gather_rows(table, ids[0, i]), HALO, 0)
         k_high = pltpu.roll(gather_rows(table, ids[1, i]), HALO, 0)
-        up[i] = jnp.where(low_half, k_high, u[1, i])
-        down[i] = jnp.where(low_half, u[0, i], k_low)
+        put(i, jnp.where(low_half, k_high, u[1, i]), jnp.where(low_half, u[0, i], k_low))
     for p in range(cells_x // 2):
-        one, two = flags[1, 2 * p], pltpu.roll(flags[1, 2 * p + 1], HALO, 0)
-        up[cells_x + p] = jnp.where(low_half, two, one).astype(jnp.float32)
-        one, two = flags[0, 2 * p], pltpu.roll(flags[0, 2 * p + 1], HALO, 0)
-        down[cells_x + p] = jnp.where(low_half, one, two).astype(jnp.float32)
+        high_one, high_two = flags[1, 2 * p], pltpu.roll(flags[1, 2 * p + 1], HALO, 0)
+        low_one, low_two = flags[0, 2 * p], pltpu.roll(flags[0, 2 * p + 1], HALO, 0)
+        put(cells_x + p, jnp.where(low_half, high_two, high_one).astype(jnp.float32),
+            jnp.where(low_half, low_one, low_two).astype(jnp.float32))
 
 
 def face_planes(send, start, u, material, goal, table):
@@ -71,7 +76,7 @@
     )
 
 
-def far_kernel(u, material, goal, table, up, far):
+def far_kernel(u, material, goal, table, sent, far):
     plane, cell = far_order(lax.axis_index("gx") % 2, u.shape[0])
     kappa = [gather_rows(table[0:1], material[plane(f)]) for f in range(HALO)]
     face = kappa[0] + kappa[1]
@@ -83,23 +88,24 @@
         far[7 + f] = goal[cell(f)].astype(jnp.float32)
 
 
-def halo_tiles(plane, cells_x, from_low, from_high, low_half):
-    below, above = from_low[plane], from_high[plane]
-    u = jnp.where(low_half, above, below)
-    k = pltpu.roll(jnp.where(low_half, below, above), HALO, 0)
-    return u, k
-
-
-def goal_tiles(pair, cells_x, from_low, from_high, low_half):
-    below, above = from_low[cells_x + pair], from_high[cells_x + pair]
-    one = jnp.where(low_half, above, below)
-    two = pltpu.roll(jnp.where(low_half, below, above), HALO, 0)
-    return one, two
-
-
-def near_kernel(u, material, goal, table, from_low, from_high, far, near_a, near_b, far_corner):
+def from_first(cells_z):
+    low_half = lax.broadcasted_iota(jnp.int32, (8, cells_z), 0) < HALO
+    even = jnp.broadcast_to(lax.axis_index("gy") % 2 == 0, low_half.shape)
+    return low_half == even
+
+
+def halo_tiles(plane, cells_x, first, second, chosen):
+    one, two = first[plane], second[plane]
+    return jnp.where(chosen, one, two), pltpu.roll(jnp.where(chosen, two, one), HALO, 0)
+
+
+def goal_tiles(pair, cells_x, first, second, chosen):
+    return halo_tiles(cells_x + pair, cells_x, first, second, chosen)
+
+
+def near_kernel(u, material, goal, table, first, second, far, near_a, near_b, far_corner):
     cells_x, cells_y, cells_z = u.shape
-    low_half = lax.broadcasted_iota(jnp.int32, (8, cells_z), 0) < HALO
+    chosen = from_first(cells_z)
     odd = lax.axis_index("gx") % 2
     last = cells_x - HALO
     near = Halves(near_a, near_b)
@@ -108,11 +114,11 @@
     def all_tiles(start):
         us, ks, gs = [], [], []
         for i in range(HALO):
-            hu, hk = halo_tiles(start + i, cells_x, from_low, from_high, low_half)
+            hu, hk = halo_tiles(start + i, cells_x, first, second, chosen)
             us.append(hu)
             ks.append(hk)
         for i in range(0, HALO, 2):
-            gs += goal_tiles(start // 2 + i // 2, cells_x, from_low, from_high, low_half)
+            gs += goal_tiles(start // 2 + i // 2, cells_x, first, second, chosen)
         return us, ks, gs
 
     for field, tiles in enumerate(all_tiles((1 - odd) * last)):
@@ -120,11 +126,11 @@
             near[field * HALO + i, pl.ds(cells_y, 8), :] = tiles[i]
 
     us, ks, gs = all_tiles(odd * last)
-    is_odd = jnp.broadcast_to(odd == 1, low_half.shape)
+    is_odd = jnp.broadcast_to(odd == 1, chosen.shape)
     us, ks = [[jnp.where(is_odd, t[f], t[HALO - 1 - f]) for f in range(HALO)] for t in (us, ks)]
     gs = [jnp.where(is_odd, gs[f], gs[max(HALO - 2 - f, 0)]) for f in range(HALO)]
     flux = gs[0] * (ks[0] + ks[1])
-    sub = lax.broadcasted_iota(jnp.int32, low_half.shape, 0)
+    sub = lax.broadcasted_iota(jnp.int32, chosen.shape, 0)
     two, four = (sub == 3) | (sub == 4), (sub >= 2) & (sub <= 5)
     far_corner[0] = jnp.where(two, pltpu.roll(us[1], HALO, 0), us[3])
     far_corner[1] = ks[3]
@@ -290,14 +296,14 @@
     return lambda i, j: ref[i, j]
 
 
-def inner_kernel(initial, material, goal, table, from_low, from_high, near_a, near_b, OI, OS, edge, kept,
+def inner_kernel(initial, material, goal, table, first, second, near_a, near_b, OI, OS, edge, kept,
                  U, K, G, Wx, Wy, Wz, S, EA, EB, ZA, ZB, M0, Q3, AC):
     cells_x, cells_y, cells_z = initial.shape
     H = HALO
     steps = Steps(cells_x, cells_y, cells_z)
     odd = steps.odd
     planes = cells_x + 2 * H
-    low_half = lax.broadcasted_iota(jnp.int32, (8, cells_z), 0) < H
+    chosen = from_first(cells_z)
     near = Halves(near_a, near_b)
     side, step = odd * (planes - 1), 1 - 2 * odd
 
@@ -305,14 +311,14 @@
         return side + step * natural
 
     def own(p, _):
-        ones = goal_tiles(p, cells_x, from_low, from_high, low_half)
+        ones = goal_tiles(p, cells_x, first, second, chosen)
         for d in range(2):
             i = 2 * p + d
             f = place(H + i)
             U[f, 0:cells_y, :] = initial[i]
             K[f, 0:cells_y, :] = gather_rows(table[0:1], material[i])
             G[f + 1 - odd, 0:cells_y, :] = goal[i].astype(jnp.float32)
-            U[f, cells_y:, :], K[f, cells_y:, :] = halo_tiles(i, cells_x, from_low, from_high, low_half)
+            U[f, cells_y:, :], K[f, cells_y:, :] = halo_tiles(i, cells_x, first, second, chosen)
             G[f + 1 - odd, cells_y:, :] = ones[d]
         return 0
 
@@ -377,10 +383,10 @@
     turns((cells_x - 4) // 2, lambda p: sweep(EA, ZA, H + 4 + 2 * p, store_c, (True, True)))
     refs = dict(EA=EA, ZA=ZA, EB=EB, ZB=ZB, Wx=Wx, Wy=Wy, Wz=Wz, S=S, M0=M0, Q3=Q3, AC=AC)
     at = 0
-    for name, first, count in KEPT:
+    for name, start, count in KEPT:
         shift = H if name in ("M0", "Q3", "AC") else 0
         for d in range(count):
-            kept[at + d] = refs[name][first - shift + d]
+            kept[at + d] = refs[name][start - shift + d]
         at += count
 
 
@@ -503,13 +509,6 @@
     return pl.BlockSpec(memory_space=memory or pltpu.VMEM)
 
 
-def exchange(up, down, axis):
-    count = lax.axis_size(axis)
-    forward = [(i, i + 1) for i in range(count - 1)]
-    backward = [(b, a) for a, b in forward]
-    return lax.ppermute(up, axis, forward), lax.ppermute(down, axis, backward)
-
-
 def swap(pairs):
     return [(a, b) for a, b in pairs] + [(b, a) for a, b in pairs]
 
@@ -531,7 +530,7 @@
 
     here = [pltpu.with_memory_space_constraint(x, pltpu.HBM) for x in (initial, material, goal_faces, conductivity)]
     ends = (2, cells_x, 8, cells_z)
-    up, down, table = pl.pallas_call(
+    first, second, table = pl.pallas_call(
         edge_kernel,
         out_shape=(send, send, shape((8, cells_z), f32)),
         in_specs=[hbm] * 4,
@@ -546,7 +545,12 @@
         compiler_params=small,
         name="edges",
     )(*here)
-    from_low, from_high = exchange(up, down, "gy")
+    first_sent = first
+    rows_y = lax.axis_size("gy")
+    first, second = (
+        lax.ppermute(value, "gy", swap([(i, i + 1) for i in range(start, rows_y - 1, 2)]))
+        for start, value in enumerate((first, second))
+    )
     far = pl.pallas_call(
         far_kernel,
         out_shape=shape((3 * HALO - 1, cells_y, cells_z), f32),
@@ -554,7 +558,7 @@
         out_specs=vmem,
         compiler_params=small,
         name="far",
-    )(initial, material, goal_faces, table, up)
+    )(initial, material, goal_faces, table, first_sent)
     far_sent = far
     far = lax.ppermute(far, "gx", swap(far_pairs))
     part = shape((3 * HALO // 2, rows, cells_z), f32)
@@ -566,7 +570,7 @@
         compiler_params=small,
         cost_estimate=pl.CostEstimate(flops=10**9, bytes_accessed=1000, transcendentals=0),
         name="near",
-    )(initial, material, goal_faces, table, from_low, from_high, far_sent)
+    )(initial, material, goal_faces, table, first, second, far_sent)
     near_a = lax.ppermute(near_a, "gx", swap(near_pairs))
     near_b = lax.ppermute(near_b, "gx", swap(near_pairs))
     far_corner = lax.ppermute(far_corner, "gx", swap(far_pairs))
@@ -588,7 +592,7 @@
         compiler_params=params,
         cost_estimate=pl.CostEstimate(flops=1000, bytes_accessed=1000, transcendentals=0),
         name="inner",
-    )(initial, material, goal_faces, table, from_low, from_high, near_a, near_b)
+    )(initial, material, goal_faces, table, first, second, near_a, near_b)
     return pl.pallas_call(
         outer_kernel,
         out_shape=(block, block),

time: 23.3 us -> 22.5 us (0.966)
  starting transfers between devices: 14 us -> 13.3 us
    ppermute x2, starting transfers between devices: 5.96 us -> 5.4 us  [per_device(): lax.ppermute(value, 'gy', swap([(i, i + 1) for i in range(start, rows_y -...]
  transfers between devices with their start and end apart: 6 -> 6, of which waited for: 1 -> 1; matrix products, arithmetic and copies ran while one was open for 0% -> 0% of each run, Pallas kernels for 21% -> 22%
where the time goes in v9:
time: 22.5 us; the launch traced here: 22.3 us
  starting transfers between devices  13.3 us (59%)
  Pallas kernels  8.12 us (36%)
  between operations  0.74 us (3%)
    ppermute x2, starting transfers between devices, per_device(): lax.ppermute(value, 'gy', swap([(i, i + 1) for i in range(start, rows_y -...  5.4 us
    pallas_call x1, Pallas kernels, per_device(): pl.pallas_call(inner_kernel, out_shape=(wide_block, wide_block, shape((6,...  4.61 us
    ppermute x1, starting transfers between devices, per_device(): far = lax.ppermute(far, 'gx', swap(far_pairs))  4.23 us
    ppermute x1, starting transfers between devices, per_device(): far_corner = lax.ppermute(far_corner, 'gx', swap(far_pairs))  3.07 us
    pallas_call x1, Pallas kernels, per_device(): pl.pallas_call(outer_kernel, out_shape=(block, block), in_specs=[vmem] *...  1.82 us
    pallas_call x1, Pallas kernels, per_device(): pl.pallas_call(edge_kernel, out_shape=(send, send, shape((8, cells_z), f3...  1.34 us
    ppermute x1, starting transfers between devices, per_device(): near_b = lax.ppermute(near_b, 'gx', swap(near_pairs))  0.5 us
  transfers between devices with their start and end apart: 6, of which 1 were waited for; matrix products, arithmetic and copies ran while one was open for 0% of the time, Pallas kernels for 22%

profile of v9, /device:TPU:1, one launch (start us, length us, event | category | flops | bytes accessed | tf_op | source)
XLA Modules:
  0.0 22.3 jit_solution(16686850682625581408)
XLA Ops:
  0.6 0.0 copy-start.2
  0.6 0.0 copy-start.1
  0.7 0.0 copy-start
  0.7 1.3 %edges.1 = (f32[24,8,128]{2,1,0:T(8,128)S(1)}, f32[24,8,128]{2,1,0:T(8,128)S(1)}, f32[8,128]{1,0:T(8,128)S(1)}) custom-call(f32[16,64,128]{2,1,0:T(8,128)} %initial.3, s32[16,64,128]{2,1,0:T(8,128)} %material.7, s32[16,64,128]{2,1,0:T(8,128)} %goal.7, f32[8]{0:T(128)} %cond.1), custom_call_target="tpu_custom_call" | custom-call | tf_op jit(solution)/shard_map/edges/pallas_call | solution.py:533
  2.0 0.7 %collective-permute-start.2 = (f32[24,8,128]{2,1,0:T(8,128)S(1)}, f32[24,8,128]{2,1,0:T(8,128)S(1)}, u32[]{:S(2)}, u32[]{:S(2)}) collective-permute-start(f32[24,8,128]{2,1,0:T(8,128)S(1)} %get-tuple-element.14), channel_id=1, source_target_pairs={{1,2},{2,1},{5,6},{6,5},{9,10},{10,9},{13,14},{14,13},{17,18},{18,... | collective-permute-start | bytes 294920 | tf_op jit(solution)/shard_map/ppermute | solution.py:551
  2.7 4.7 %collective-permute-start.1 = (f32[24,8,128]{2,1,0:T(8,128)S(1)}, f32[24,8,128]{2,1,0:T(8,128)S(1)}, u32[]{:S(2)}, u32[]{:S(2)}) collective-permute-start(f32[24,8,128]{2,1,0:T(8,128)S(1)} %get-tuple-element.13.sent), channel_id=1, source_target_pairs={{0,1},{2,3},{1,0},{3,2},{4,5},{6,7},{5,4},{7,6},{8,9},{10,11},{9,8... | collective-permute-start | bytes 294920 | tf_op jit(solution)/shard_map/ppermute | solution.py:551
  7.4 0.0 copy-done.2
  7.4 0.0 copy-done.1
  7.4 0.0 copy-done
  7.4 0.2 far.1
  7.6 4.2 %collective-permute-start = (f32[11,64,128]{2,1,0:T(8,128)S(1)}, f32[11,64,128]{2,1,0:T(8,128)S(1)}, u32[]{:S(2)}, u32[]{:S(2)}) collective-permute-start(f32[11,64,128]{2,1,0:T(8,128)S(1)} %far.1), channel_id=1, source_target_pairs={{4,8},{12,16},{20,24},{8,4},{16,12},{24,20},{5,9},{13,17},{21,25},... | collective-permute-start | bytes 1081352 | tf_op jit(solution)/shard_map/ppermute | solution.py:563
  11.8 0.0 collective-permute-done.2.second
  11.8 0.0 collective-permute-done.1.first
  11.9 0.2 near.1
  12.0 0.1 collective-permute-start.4
  12.1 0.5 %collective-permute-start.5 = (f32[6,72,128]{2,1,0:T(8,128)S(1)}, f32[6,72,128]{2,1,0:T(8,128)S(1)}, u32[]{:S(2)}, u32[]{:S(2)}) collective-permute-start(f32[6,72,128]{2,1,0:T(8,128)S(1)} %get-tuple-element.17), channel_id=1, source_target_pairs={{0,4},{8,12},{16,20},{24,28},{4,0},{12,8},{20,16},{28,24},{1,5},{9... | collective-permute-start | bytes 663560 | tf_op jit(solution)/shard_map/ppermute | solution.py:575
  12.6 3.1 %collective-permute-start.3 = (f32[7,8,128]{2,1,0:T(8,128)S(1)}, f32[7,8,128]{2,1,0:T(8,128)S(1)}, u32[]{:S(2)}, u32[]{:S(2)}) collective-permute-start(f32[7,8,128]{2,1,0:T(8,128)S(1)} %get-tuple-element.15), channel_id=1, source_target_pairs={{4,8},{12,16},{20,24},{8,4},{16,12},{24,20},{5,9},{13,17},{21,25},... | collective-permute-start | bytes 86024 | tf_op jit(solution)/shard_map/ppermute | solution.py:576
  15.7 0.0 collective-permute-done.4.near_a
  15.7 0.0 collective-permute-done.5.near_b
  15.7 4.6 %inner.1 = (f32[16,72,128]{2,1,0:T(8,128)S(1)}, f32[16,72,128]{2,1,0:T(8,128)S(1)}, f32[6,72,128]{2,1,0:T(8,128)S(1)}, f32[30,9,8,128]{3,2,1,0:T(8,128)S(1)}) custom-call(f32[16,64,128]{2,1,0:T(8,128)S(1)} %copy-done, s32[16,64,128]{2,1,0:T(8,128)S(1)} %copy-done.1, s32[16,64,128]{2,1,0:T(8,128)S(1)} %copy-done.2, f32[8,128]{1,0:T(8,128)S(1)} %get-tuple-element.12.table, ...), custom_call_target="tpu_custom_call" | custom-call | flops 1000 | bytes 1000 | tf_op jit(solution)/shard_map/inner/pallas_call | solution.py:585
  20.3 0.2 collective-permute-done.3.far_corner
  20.5 0.0 collective-permute-done.far
  20.5 1.8 %outer.1 = (f32[16,64,128]{2,1,0:T(8,128)}, f32[16,64,128]{2,1,0:T(8,128)}) custom-call(f32[11,64,128]{2,1,0:T(8,128)S(1)} %collective-permute-done.far, f32[7,8,128]{2,1,0:T(8,128)S(1)} %collective-permute-done.3.far_corner, f32[6,72,128]{2,1,0:T(8,128)S(1)} %get-tuple-element.18.edge, f32[30,9,8,128]{3,2,1,0:T(8,128)S(1)} %get-tuple-element.19.kept, ...), custom_call_target="tpu_custom_call" | custom-call | tf_op jit(solution)/shard_map/outer/pallas_call | solution.py:596
Async XLA Ops:
  0.6 6.8 %copy-start.2 = (s32[16,64,128]{2,1,0:T(8,128)S(1)}, s32[16,64,128]{2,1,0:T(8,128)}, u32[]{:S(2)}) copy-start(s32[16,64,128]{2,1,0:T(8,128)} %goal.7) | copy-start | bytes 1572868
  0.6 6.8 %copy-start.1 = (s32[16,64,128]{2,1,0:T(8,128)S(1)}, s32[16,64,128]{2,1,0:T(8,128)}, u32[]{:S(2)}) copy-start(s32[16,64,128]{2,1,0:T(8,128)} %material.7) | copy-start | bytes 1572868
  0.7 6.8 %copy-start = (f32[16,64,128]{2,1,0:T(8,128)S(1)}, f32[16,64,128]{2,1,0:T(8,128)}, u32[]{:S(2)}) copy-start(f32[16,64,128]{2,1,0:T(8,128)} %initial.3) | copy-start | bytes 1572868
  2.0 9.8 %collective-permute-start.2 = (f32[24,8,128]{2,1,0:T(8,128)S(1)}, f32[24,8,128]{2,1,0:T(8,128)S(1)}, u32[]{:S(2)}, u32[]{:S(2)}) collective-permute-start(f32[24,8,128]{2,1,0:T(8,128)S(1)} %get-tuple-element.14), channel_id=1, source_target_pairs={{1,2},{2,1},{5,6},{6,5},{9,10},{10,9},{13,14},{14,13},{17,18},{18,... | collective-permute-start | bytes 294920 | tf_op jit(solution)/shard_map/ppermute | solution.py:551
  2.7 9.2 %collective-permute-start.1 = (f32[24,8,128]{2,1,0:T(8,128)S(1)}, f32[24,8,128]{2,1,0:T(8,128)S(1)}, u32[]{:S(2)}, u32[]{:S(2)}) collective-permute-start(f32[24,8,128]{2,1,0:T(8,128)S(1)} %get-tuple-element.13.sent), channel_id=1, source_target_pairs={{0,1},{2,3},{1,0},{3,2},{4,5},{6,7},{5,4},{7,6},{8,9},{10,11},{9,8... | collective-permute-start | bytes 294920 | tf_op jit(solution)/shard_map/ppermute | solution.py:551
  7.6 12.9 %collective-permute-start = (f32[11,64,128]{2,1,0:T(8,128)S(1)}, f32[11,64,128]{2,1,0:T(8,128)S(1)}, u32[]{:S(2)}, u32[]{:S(2)}) collective-permute-start(f32[11,64,128]{2,1,0:T(8,128)S(1)} %far.1), channel_id=1, source_target_pairs={{4,8},{12,16},{20,24},{8,4},{16,12},{24,20},{5,9},{13,17},{21,25},... | collective-permute-start | bytes 1081352 | tf_op jit(solution)/shard_map/ppermute | solution.py:563
  12.0 3.6 %collective-permute-start.4 = (f32[6,72,128]{2,1,0:T(8,128)S(1)}, f32[6,72,128]{2,1,0:T(8,128)S(1)}, u32[]{:S(2)}, u32[]{:S(2)}) collective-permute-start(f32[6,72,128]{2,1,0:T(8,128)S(1)} %get-tuple-element.16), channel_id=1, source_target_pairs={{0,4},{8,12},{16,20},{24,28},{4,0},{12,8},{20,16},{28,24},{1,5},{9... | collective-permute-start | bytes 663560 | tf_op jit(solution)/shard_map/ppermute | solution.py:574
  12.1 3.6 %collective-permute-start.5 = (f32[6,72,128]{2,1,0:T(8,128)S(1)}, f32[6,72,128]{2,1,0:T(8,128)S(1)}, u32[]{:S(2)}, u32[]{:S(2)}) collective-permute-start(f32[6,72,128]{2,1,0:T(8,128)S(1)} %get-tuple-element.17), channel_id=1, source_target_pairs={{0,4},{8,12},{16,20},{24,28},{4,0},{12,8},{20,16},{28,24},{1,5},{9... | collective-permute-start | bytes 663560 | tf_op jit(solution)/shard_map/ppermute | solution.py:575
  12.6 7.9 %collective-permute-start.3 = (f32[7,8,128]{2,1,0:T(8,128)S(1)}, f32[7,8,128]{2,1,0:T(8,128)S(1)}, u32[]{:S(2)}, u32[]{:S(2)}) collective-permute-start(f32[7,8,128]{2,1,0:T(8,128)S(1)} %get-tuple-element.15), channel_id=1, source_target_pairs={{4,8},{12,16},{20,24},{8,4},{16,12},{24,20},{5,9},{13,17},{21,25},... | collective-permute-start | bytes 86024 | tf_op jit(solution)/shard_map/ppermute | solution.py:576

commit v10 on v9

--- a/solution.py
+++ b/solution.py
@@ -310,7 +310,7 @@
     def place(natural):
         return side + step * natural
 
-    def own(p, _):
+    def own(p):
         ones = goal_tiles(p, cells_x, first, second, chosen)
         for d in range(2):
             i = 2 * p + d
@@ -320,18 +320,19 @@
             G[f + 1 - odd, 0:cells_y, :] = goal[i].astype(jnp.float32)
             U[f, cells_y:, :], K[f, cells_y:, :] = halo_tiles(i, cells_x, first, second, chosen)
             G[f + 1 - odd, cells_y:, :] = ones[d]
-        return 0
-
-    lax.fori_loop(0, cells_x // 2, own, 0)
+
+    turns(cells_x // 2, own)
     for i in range(H):
         f = (1 - odd) * (H + cells_x + i) + odd * (planes - 1 - i)
         U[f] = near[i]
         K[f] = near[H + i]
         G[f + 1 - odd] = near[2 * H + i]
     for d in range(2):
-        edge[d] = U[H + d]
-        edge[2 + d] = K[H + d]
-        edge[4 + d] = G[H + d + 1 - odd]
+        for j in range(steps.T):
+            here = pl.ds(j, 8, stride=steps.T)
+            edge[d, j] = U[H + d, here, :]
+            edge[2 + d, j] = K[H + d, here, :]
+            edge[4 + d, j] = G[H + d + 1 - odd, here, :]
 
     def first_goal(i, j):
         return G[i + 1, pl.ds(j, 8, stride=steps.T), :]
@@ -420,10 +421,6 @@
         for f in range(1, H):
             ref[f + 1 if ref is G else f, cells_y:, :] = values[f - 1]
     FG[cells_y:, :] = turned[2]
-    for d in range(2):
-        U[H + d] = edge[d]
-        K[H + d] = edge[2 + d]
-        G[H + d + 1 - odd] = edge[4 + d]
 
     places, at = {}, 0
     for name, first, count in KEPT:
@@ -440,8 +437,18 @@
 
         return load
 
+    sub_shape = (8, cells_z)
+    is_odd = jnp.broadcast_to(odd == 1, sub_shape)
+
+    def beside(ref, at):
+        rows = steps.rower(ref)
+        return lambda i, j: rows(i, j) if i < H else edge[at + i - H, j]
+
     def first_goal(i, j):
-        return G[i + 1, pl.ds(j, 8, stride=steps.T), :]
+        if i < H - 1:
+            return G[i + 1, pl.ds(j, 8, stride=steps.T), :]
+        other = edge[4, j] if i == H else G[H, pl.ds(j, 8, stride=steps.T), :]
+        return jnp.where(is_odd, edge[5 + i - H, j], other)
 
     sub = lax.broadcasted_iota(jnp.int32, (8, cells_z), 0)
     T = steps.T
@@ -463,7 +470,7 @@
     def fluxes(ref):
         return lambda j: ref[pl.ds(j, 8, stride=steps.T), :]
 
-    fields = (steps.rower(K), steps.rower(U), first_goal)
+    fields = (beside(K, 2), beside(U, 0), first_goal)
     steps.prelude(fields, 3, 2, begin)
     steps.prelude(fields, 1, 2, begin, (fluxes(FU), fluxes(FG)))
     weights = (mixed(Wx, "Wx", 1, H), mixed(Wy, "Wy", 1, H), mixed(Wz, "Wz", 1, H), mixed(S, "S", 1, H))
@@ -584,7 +591,7 @@
     wide_block = shape((cells_x, rows, cells_z), f32)
     ind, sens, edge, kept = pl.pallas_call(
         inner_kernel,
-        out_shape=(wide_block, wide_block, shape((6, rows, cells_z), f32), shape((KEPT_PLANES, rows // 8, 8, cells_z), f32)),
+        out_shape=(wide_block, wide_block, shape((6, rows // 8, 8, cells_z), f32), shape((KEPT_PLANES, rows // 8, 8, cells_z), f32)),
         in_specs=[vmem] * 8,
         out_specs=(vmem,) * 4,
         scratch_shapes=[natural(planes), natural(planes), natural(planes + 1)]
@@ -598,7 +605,7 @@
         out_shape=(block, block),
         in_specs=[vmem] * 6,
         out_specs=(hbm, hbm),
-        scratch_shapes=[natural(HALO + 2), natural(HALO + 2), natural(HALO + 3)]
+        scratch_shapes=[natural(HALO), natural(HALO), natural(HALO + 1)]
         + [pltpu.VMEM((rows, cells_z), f32)] * 2 + [tiles(2 * HALO)] * 13 + [natural(cells_x)] * 2 + [pltpu.SemaphoreType.DMA((2, 3))],
         compiler_params=small,
         name="outer",

time: 22.5 us -> 22.5 us (level)
  waiting for transfers between devices: 0.2 us -> 0.63 us
  Pallas kernels: 8.12 us -> 7.71 us
    ppermute x1, waiting for transfers between devices: 0.19 us -> 0.62 us  [per_device(): far_corner = lax.ppermute(far_corner, 'gx', swap(far_pairs))]
    pallas_call x1, Pallas kernels: 4.61 us -> 4.19 us  [per_device(): pl.pallas_call(inner_kernel, out_shape=(wide_block, wide_block, shape((6,...]
  transfers between devices with their start and end apart: 6 -> 6, of which waited for: 1 -> 1; matrix products, arithmetic and copies ran while one was open for 0% -> 0% of each run, Pallas kernels for 22% -> 20%
where the time goes in v10:
time: 22.5 us; the launch traced here: 22.3 us
  starting transfers between devices  13.3 us (59%)
  Pallas kernels  7.71 us (34%)
  between operations  0.74 us (3%)
  waiting for transfers between devices  0.63 us (3%)
    ppermute x2, starting transfers between devices, per_device(): lax.ppermute(value, 'gy', swap([(i, i + 1) for i in range(start, rows_y -...  5.4 us
    ppermute x1, starting transfers between devices, per_device(): far = lax.ppermute(far, 'gx', swap(far_pairs))  4.23 us
    pallas_call x1, Pallas kernels, per_device(): pl.pallas_call(inner_kernel, out_shape=(wide_block, wide_block, shape((6,...  4.19 us
    ppermute x1, starting transfers between devices, per_device(): far_corner = lax.ppermute(far_corner, 'gx', swap(far_pairs))  3.07 us
    pallas_call x1, Pallas kernels, per_device(): pl.pallas_call(outer_kernel, out_shape=(block, block), in_specs=[vmem] *...  1.83 us
    pallas_call x1, Pallas kernels, per_device(): pl.pallas_call(edge_kernel, out_shape=(send, send, shape((8, cells_z), f3...  1.34 us
    ppermute x1, waiting for transfers between devices, per_device(): far_corner = lax.ppermute(far_corner, 'gx', swap(far_pairs))  0.62 us
    ppermute x1, starting transfers between devices, per_device(): near_b = lax.ppermute(near_b, 'gx', swap(near_pairs))  0.5 us
  transfers between devices with their start and end apart: 6, of which 1 were waited for; matrix products, arithmetic and copies ran while one was open for 0% of the time, Pallas kernels for 20%

profile of v10, /device:TPU:1, one launch (start us, length us, event | category | flops | bytes accessed | tf_op | source)
XLA Modules:
  0.0 22.3 jit_solution(12678437429109248606)
XLA Ops:
  0.6 0.0 copy-start.2
  0.6 0.0 copy-start.1
  0.7 0.0 copy-start
  0.7 1.3 %edges.1 = (f32[24,8,128]{2,1,0:T(8,128)S(1)}, f32[24,8,128]{2,1,0:T(8,128)S(1)}, f32[8,128]{1,0:T(8,128)S(1)}) custom-call(f32[16,64,128]{2,1,0:T(8,128)} %initial.3, s32[16,64,128]{2,1,0:T(8,128)} %material.7, s32[16,64,128]{2,1,0:T(8,128)} %goal.7, f32[8]{0:T(128)} %cond.1), custom_call_target="tpu_custom_call" | custom-call | tf_op jit(solution)/shard_map/edges/pallas_call | solution.py:540
  2.0 0.7 %collective-permute-start.2 = (f32[24,8,128]{2,1,0:T(8,128)S(1)}, f32[24,8,128]{2,1,0:T(8,128)S(1)}, u32[]{:S(2)}, u32[]{:S(2)}) collective-permute-start(f32[24,8,128]{2,1,0:T(8,128)S(1)} %get-tuple-element.14), channel_id=1, source_target_pairs={{1,2},{2,1},{5,6},{6,5},{9,10},{10,9},{13,14},{14,13},{17,18},{18,... | collective-permute-start | bytes 294920 | tf_op jit(solution)/shard_map/ppermute | solution.py:558
  2.7 4.7 %collective-permute-start.1 = (f32[24,8,128]{2,1,0:T(8,128)S(1)}, f32[24,8,128]{2,1,0:T(8,128)S(1)}, u32[]{:S(2)}, u32[]{:S(2)}) collective-permute-start(f32[24,8,128]{2,1,0:T(8,128)S(1)} %get-tuple-element.13.sent), channel_id=1, source_target_pairs={{0,1},{2,3},{1,0},{3,2},{4,5},{6,7},{5,4},{7,6},{8,9},{10,11},{9,8... | collective-permute-start | bytes 294920 | tf_op jit(solution)/shard_map/ppermute | solution.py:558
  7.4 0.0 copy-done.2
  7.4 0.0 copy-done.1
  7.4 0.0 copy-done
  7.4 0.2 far.1
  7.6 4.2 %collective-permute-start = (f32[11,64,128]{2,1,0:T(8,128)S(1)}, f32[11,64,128]{2,1,0:T(8,128)S(1)}, u32[]{:S(2)}, u32[]{:S(2)}) collective-permute-start(f32[11,64,128]{2,1,0:T(8,128)S(1)} %far.1), channel_id=1, source_target_pairs={{4,8},{12,16},{20,24},{8,4},{16,12},{24,20},{5,9},{13,17},{21,25},... | collective-permute-start | bytes 1081352 | tf_op jit(solution)/shard_map/ppermute | solution.py:570
  11.8 0.0 collective-permute-done.2.second
  11.8 0.0 collective-permute-done.1.first
  11.9 0.2 near.1
  12.0 0.1 collective-permute-start.4
  12.1 0.5 %collective-permute-start.5 = (f32[6,72,128]{2,1,0:T(8,128)S(1)}, f32[6,72,128]{2,1,0:T(8,128)S(1)}, u32[]{:S(2)}, u32[]{:S(2)}) collective-permute-start(f32[6,72,128]{2,1,0:T(8,128)S(1)} %get-tuple-element.17), channel_id=1, source_target_pairs={{0,4},{8,12},{16,20},{24,28},{4,0},{12,8},{20,16},{28,24},{1,5},{9... | collective-permute-start | bytes 663560 | tf_op jit(solution)/shard_map/ppermute | solution.py:582
  12.6 3.1 %collective-permute-start.3 = (f32[7,8,128]{2,1,0:T(8,128)S(1)}, f32[7,8,128]{2,1,0:T(8,128)S(1)}, u32[]{:S(2)}, u32[]{:S(2)}) collective-permute-start(f32[7,8,128]{2,1,0:T(8,128)S(1)} %get-tuple-element.15), channel_id=1, source_target_pairs={{4,8},{12,16},{20,24},{8,4},{16,12},{24,20},{5,9},{13,17},{21,25},... | collective-permute-start | bytes 86024 | tf_op jit(solution)/shard_map/ppermute | solution.py:583
  15.7 0.0 collective-permute-done.4.near_a
  15.7 0.0 collective-permute-done.5.near_b
  15.7 4.2 %inner.1 = (f32[16,72,128]{2,1,0:T(8,128)S(1)}, f32[16,72,128]{2,1,0:T(8,128)S(1)}, f32[6,9,8,128]{3,2,1,0:T(8,128)S(1)}, f32[30,9,8,128]{3,2,1,0:T(8,128)S(1)}) custom-call(f32[16,64,128]{2,1,0:T(8,128)S(1)} %copy-done, s32[16,64,128]{2,1,0:T(8,128)S(1)} %copy-done.1, s32[16,64,128]{2,1,0:T(8,128)S(1)} %copy-done.2, f32[8,128]{1,0:T(8,128)S(1)} %get-tuple-element.12.table, ...), custom_call_target="tpu_custom_call" | custom-call | flops 1000 | bytes 1000 | tf_op jit(solution)/shard_map/inner/pallas_call | solution.py:592
  19.9 0.6 %collective-permute-done.3.far_corner = f32[7,8,128]{2,1,0:T(8,128)S(1)} collective-permute-done((f32[7,8,128]{2,1,0:T(8,128)S(1)}, f32[7,8,128]{2,1,0:T(8,128)S(1)}, u32[]{:S(2)}, u32[]{:S(2)}) %collective-permute-start.3) | collective-permute-done | bytes 28704 | tf_op jit(solution)/shard_map/ppermute | solution.py:583
  20.5 0.0 collective-permute-done.far
  20.5 1.8 %outer.1 = (f32[16,64,128]{2,1,0:T(8,128)}, f32[16,64,128]{2,1,0:T(8,128)}) custom-call(f32[11,64,128]{2,1,0:T(8,128)S(1)} %collective-permute-done.far, f32[7,8,128]{2,1,0:T(8,128)S(1)} %collective-permute-done.3.far_corner, f32[6,9,8,128]{3,2,1,0:T(8,128)S(1)} %get-tuple-element.18.edge, f32[30,9,8,128]{3,2,1,0:T(8,128)S(1)} %get-tuple-element.19.kept, ...), custom_call_target="tpu_custom_call" | custom-call | tf_op jit(solution)/shard_map/outer/pallas_call | solution.py:603
Async XLA Ops:
  0.6 6.8 %copy-start.2 = (s32[16,64,128]{2,1,0:T(8,128)S(1)}, s32[16,64,128]{2,1,0:T(8,128)}, u32[]{:S(2)}) copy-start(s32[16,64,128]{2,1,0:T(8,128)} %goal.7) | copy-start | bytes 1572868
  0.6 6.8 %copy-start.1 = (s32[16,64,128]{2,1,0:T(8,128)S(1)}, s32[16,64,128]{2,1,0:T(8,128)}, u32[]{:S(2)}) copy-start(s32[16,64,128]{2,1,0:T(8,128)} %material.7) | copy-start | bytes 1572868
  0.7 6.8 %copy-start = (f32[16,64,128]{2,1,0:T(8,128)S(1)}, f32[16,64,128]{2,1,0:T(8,128)}, u32[]{:S(2)}) copy-start(f32[16,64,128]{2,1,0:T(8,128)} %initial.3) | copy-start | bytes 1572868
  2.0 9.8 %collective-permute-start.2 = (f32[24,8,128]{2,1,0:T(8,128)S(1)}, f32[24,8,128]{2,1,0:T(8,128)S(1)}, u32[]{:S(2)}, u32[]{:S(2)}) collective-permute-start(f32[24,8,128]{2,1,0:T(8,128)S(1)} %get-tuple-element.14), channel_id=1, source_target_pairs={{1,2},{2,1},{5,6},{6,5},{9,10},{10,9},{13,14},{14,13},{17,18},{18,... | collective-permute-start | bytes 294920 | tf_op jit(solution)/shard_map/ppermute | solution.py:558
  2.7 9.2 %collective-permute-start.1 = (f32[24,8,128]{2,1,0:T(8,128)S(1)}, f32[24,8,128]{2,1,0:T(8,128)S(1)}, u32[]{:S(2)}, u32[]{:S(2)}) collective-permute-start(f32[24,8,128]{2,1,0:T(8,128)S(1)} %get-tuple-element.13.sent), channel_id=1, source_target_pairs={{0,1},{2,3},{1,0},{3,2},{4,5},{6,7},{5,4},{7,6},{8,9},{10,11},{9,8... | collective-permute-start | bytes 294920 | tf_op jit(solution)/shard_map/ppermute | solution.py:558
  7.6 12.9 %collective-permute-start = (f32[11,64,128]{2,1,0:T(8,128)S(1)}, f32[11,64,128]{2,1,0:T(8,128)S(1)}, u32[]{:S(2)}, u32[]{:S(2)}) collective-permute-start(f32[11,64,128]{2,1,0:T(8,128)S(1)} %far.1), channel_id=1, source_target_pairs={{4,8},{12,16},{20,24},{8,4},{16,12},{24,20},{5,9},{13,17},{21,25},... | collective-permute-start | bytes 1081352 | tf_op jit(solution)/shard_map/ppermute | solution.py:570
  12.0 3.6 %collective-permute-start.4 = (f32[6,72,128]{2,1,0:T(8,128)S(1)}, f32[6,72,128]{2,1,0:T(8,128)S(1)}, u32[]{:S(2)}, u32[]{:S(2)}) collective-permute-start(f32[6,72,128]{2,1,0:T(8,128)S(1)} %get-tuple-element.16), channel_id=1, source_target_pairs={{0,4},{8,12},{16,20},{24,28},{4,0},{12,8},{20,16},{28,24},{1,5},{9... | collective-permute-start | bytes 663560 | tf_op jit(solution)/shard_map/ppermute | solution.py:581
  12.1 3.6 %collective-permute-start.5 = (f32[6,72,128]{2,1,0:T(8,128)S(1)}, f32[6,72,128]{2,1,0:T(8,128)S(1)}, u32[]{:S(2)}, u32[]{:S(2)}) collective-permute-start(f32[6,72,128]{2,1,0:T(8,128)S(1)} %get-tuple-element.17), channel_id=1, source_target_pairs={{0,4},{8,12},{16,20},{24,28},{4,0},{12,8},{20,16},{28,24},{1,5},{9... | collective-permute-start | bytes 663560 | tf_op jit(solution)/shard_map/ppermute | solution.py:582
  12.6 7.9 %collective-permute-start.3 = (f32[7,8,128]{2,1,0:T(8,128)S(1)}, f32[7,8,128]{2,1,0:T(8,128)S(1)}, u32[]{:S(2)}, u32[]{:S(2)}) collective-permute-start(f32[7,8,128]{2,1,0:T(8,128)S(1)} %get-tuple-element.15), channel_id=1, source_target_pairs={{4,8},{12,16},{20,24},{8,4},{16,12},{24,20},{5,9},{13,17},{21,25},... | collective-permute-start | bytes 86024 | tf_op jit(solution)/shard_map/ppermute | solution.py:583

commit v11 on v10

--- a/solution.py
+++ b/solution.py
@@ -43,11 +43,11 @@
     shared[...] = jnp.broadcast_to(table, shared.shape)
     for move in moves[1:]:
         move.wait()
-    even = jnp.broadcast_to(lax.axis_index("gy") % 2 == 0, low_half.shape)
+    upward = jnp.broadcast_to(lax.axis_index("gy") % 2 == 1, low_half.shape)
 
     def put(i, up, down):
-        first[i] = jnp.where(even, up, down)
-        second[i] = jnp.where(even, down, up)
+        first[i] = jnp.where(upward, up, down)
+        second[i] = jnp.where(upward, down, up)
 
     for i in range(cells_x):
         k_low = pltpu.roll(gather_rows(table, ids[0, i]), HALO, 0)
@@ -90,8 +90,8 @@
 
 def from_first(cells_z):
     low_half = lax.broadcasted_iota(jnp.int32, (8, cells_z), 0) < HALO
-    even = jnp.broadcast_to(lax.axis_index("gy") % 2 == 0, low_half.shape)
-    return low_half == even
+    upward = jnp.broadcast_to(lax.axis_index("gy") % 2 == 1, low_half.shape)
+    return low_half == upward
 
 
 def halo_tiles(plane, cells_x, first, second, chosen):
@@ -556,7 +556,7 @@
     rows_y = lax.axis_size("gy")
     first, second = (
         lax.ppermute(value, "gy", swap([(i, i + 1) for i in range(start, rows_y - 1, 2)]))
-        for start, value in enumerate((first, second))
+        for start, value in ((1, first), (0, second))
     )
     far = pl.pallas_call(
         far_kernel,

time: 22.5 us -> 22.6 us (level)
  the two profiles are of different devices: /device:TPU:1 before, /device:TPU:12 now
where the time goes in v11:
time: 22.6 us; the launch traced here: 22.4 us
  starting transfers between devices  12 us (53%)
  Pallas kernels  7.7 us (34%)
  waiting for transfers between devices  1.92 us (8%)
  between operations  0.74 us (3%)
    ppermute x2, starting transfers between devices, per_device(): lax.ppermute(value, 'gy', swap([(i, i + 1) for i in range(start, rows_y -...  5.11 us
    pallas_call x1, Pallas kernels, per_device(): pl.pallas_call(inner_kernel, out_shape=(wide_block, wide_block, shape((6,...  4.19 us
    ppermute x1, starting transfers between devices, per_device(): far_corner = lax.ppermute(far_corner, 'gx', swap(far_pairs))  3.37 us
    ppermute x1, starting transfers between devices, per_device(): far = lax.ppermute(far, 'gx', swap(far_pairs))  2.22 us
    pallas_call x1, Pallas kernels, per_device(): pl.pallas_call(outer_kernel, out_shape=(block, block), in_specs=[vmem] *...  1.83 us
    ppermute x1, waiting for transfers between devices, per_device(): far_corner = lax.ppermute(far_corner, 'gx', swap(far_pairs))  1.76 us
    pallas_call x1, Pallas kernels, per_device(): pl.pallas_call(edge_kernel, out_shape=(send, send, shape((8, cells_z), f3...  1.34 us
    ppermute x1, starting transfers between devices, per_device(): near_a = lax.ppermute(near_a, 'gx', swap(near_pairs))  1.23 us
  transfers between devices with their start and end apart: 6, of which 2 were waited for; matrix products, arithmetic and copies ran while one was open for 0% of the time, Pallas kernels for 20%

profile of v11, /device:TPU:12, one launch (start us, length us, event | category | flops | bytes accessed | tf_op | source)
XLA Modules:
  0.0 22.4 jit_solution(17777031500634370192)
XLA Ops:
  0.6 0.0 copy-start.2
  0.6 0.0 copy-start.1
  0.7 0.0 copy-start
  0.7 1.3 %edges.1 = (f32[24,8,128]{2,1,0:T(8,128)S(1)}, f32[24,8,128]{2,1,0:T(8,128)S(1)}, f32[8,128]{1,0:T(8,128)S(1)}) custom-call(f32[16,64,128]{2,1,0:T(8,128)} %initial.3, s32[16,64,128]{2,1,0:T(8,128)} %material.7, s32[16,64,128]{2,1,0:T(8,128)} %goal.7, f32[8]{0:T(128)} %cond.1), custom_call_target="tpu_custom_call" | custom-call | tf_op jit(solution)/shard_map/edges/pallas_call | solution.py:540
  2.0 0.5 %collective-permute-start.2 = (f32[24,8,128]{2,1,0:T(8,128)S(1)}, f32[24,8,128]{2,1,0:T(8,128)S(1)}, u32[]{:S(2)}, u32[]{:S(2)}) collective-permute-start(f32[24,8,128]{2,1,0:T(8,128)S(1)} %get-tuple-element.14), channel_id=1, source_target_pairs={{0,1},{2,3},{1,0},{3,2},{4,5},{6,7},{5,4},{7,6},{8,9},{10,11},{9,8... | collective-permute-start | bytes 294920 | tf_op jit(solution)/shard_map/ppermute | solution.py:558
  2.5 4.6 %collective-permute-start.1 = (f32[24,8,128]{2,1,0:T(8,128)S(1)}, f32[24,8,128]{2,1,0:T(8,128)S(1)}, u32[]{:S(2)}, u32[]{:S(2)}) collective-permute-start(f32[24,8,128]{2,1,0:T(8,128)S(1)} %get-tuple-element.13.sent), channel_id=1, source_target_pairs={{1,2},{2,1},{5,6},{6,5},{9,10},{10,9},{13,14},{14,13},{17,18},{18,... | collective-permute-start | bytes 294920 | tf_op jit(solution)/shard_map/ppermute | solution.py:558
  7.1 0.0 copy-done.2
  7.1 0.0 copy-done.1
  7.2 0.0 copy-done
  7.2 0.2 far.1
  7.3 2.2 %collective-permute-start = (f32[11,64,128]{2,1,0:T(8,128)S(1)}, f32[11,64,128]{2,1,0:T(8,128)S(1)}, u32[]{:S(2)}, u32[]{:S(2)}) collective-permute-start(f32[11,64,128]{2,1,0:T(8,128)S(1)} %far.1), channel_id=1, source_target_pairs={{4,8},{12,16},{20,24},{8,4},{16,12},{24,20},{5,9},{13,17},{21,25},... | collective-permute-start | bytes 1081352 | tf_op jit(solution)/shard_map/ppermute | solution.py:570
  9.6 0.0 collective-permute-done.2.second
  9.6 0.1 collective-permute-done.1.first
  9.7 0.2 near.1
  9.9 1.2 %collective-permute-start.4 = (f32[6,72,128]{2,1,0:T(8,128)S(1)}, f32[6,72,128]{2,1,0:T(8,128)S(1)}, u32[]{:S(2)}, u32[]{:S(2)}) collective-permute-start(f32[6,72,128]{2,1,0:T(8,128)S(1)} %get-tuple-element.16), channel_id=1, source_target_pairs={{0,4},{8,12},{16,20},{24,28},{4,0},{12,8},{20,16},{28,24},{1,5},{9... | collective-permute-start | bytes 663560 | tf_op jit(solution)/shard_map/ppermute | solution.py:581
  11.1 0.1 collective-permute-start.5
  11.2 3.4 %collective-permute-start.3 = (f32[7,8,128]{2,1,0:T(8,128)S(1)}, f32[7,8,128]{2,1,0:T(8,128)S(1)}, u32[]{:S(2)}, u32[]{:S(2)}) collective-permute-start(f32[7,8,128]{2,1,0:T(8,128)S(1)} %get-tuple-element.15), channel_id=1, source_target_pairs={{4,8},{12,16},{20,24},{8,4},{16,12},{24,20},{5,9},{13,17},{21,25},... | collective-permute-start | bytes 86024 | tf_op jit(solution)/shard_map/ppermute | solution.py:583
  14.6 0.0 collective-permute-done.4.near_a
  14.6 0.0 collective-permute-done.5.near_b
  14.6 4.2 %inner.1 = (f32[16,72,128]{2,1,0:T(8,128)S(1)}, f32[16,72,128]{2,1,0:T(8,128)S(1)}, f32[6,9,8,128]{3,2,1,0:T(8,128)S(1)}, f32[30,9,8,128]{3,2,1,0:T(8,128)S(1)}) custom-call(f32[16,64,128]{2,1,0:T(8,128)S(1)} %copy-done, s32[16,64,128]{2,1,0:T(8,128)S(1)} %copy-done.1, s32[16,64,128]{2,1,0:T(8,128)S(1)} %copy-done.2, f32[8,128]{1,0:T(8,128)S(1)} %get-tuple-element.12.table, ...), custom_call_target="tpu_custom_call" | custom-call | flops 1000 | bytes 1000 | tf_op jit(solution)/shard_map/inner/pallas_call | solution.py:592
  18.8 1.8 %collective-permute-done.3.far_corner = f32[7,8,128]{2,1,0:T(8,128)S(1)} collective-permute-done((f32[7,8,128]{2,1,0:T(8,128)S(1)}, f32[7,8,128]{2,1,0:T(8,128)S(1)}, u32[]{:S(2)}, u32[]{:S(2)}) %collective-permute-start.3) | collective-permute-done | bytes 28704 | tf_op jit(solution)/shard_map/ppermute | solution.py:583
  20.5 0.0 collective-permute-done.far
  20.5 1.8 %outer.1 = (f32[16,64,128]{2,1,0:T(8,128)}, f32[16,64,128]{2,1,0:T(8,128)}) custom-call(f32[11,64,128]{2,1,0:T(8,128)S(1)} %collective-permute-done.far, f32[7,8,128]{2,1,0:T(8,128)S(1)} %collective-permute-done.3.far_corner, f32[6,9,8,128]{3,2,1,0:T(8,128)S(1)} %get-tuple-element.18.edge, f32[30,9,8,128]{3,2,1,0:T(8,128)S(1)} %get-tuple-element.19.kept, ...), custom_call_target="tpu_custom_call" | custom-call | tf_op jit(solution)/shard_map/outer/pallas_call | solution.py:603
Async XLA Ops:
  0.6 6.5 %copy-start.2 = (s32[16,64,128]{2,1,0:T(8,128)S(1)}, s32[16,64,128]{2,1,0:T(8,128)}, u32[]{:S(2)}) copy-start(s32[16,64,128]{2,1,0:T(8,128)} %goal.7) | copy-start | bytes 1572868
  0.6 6.5 %copy-start.1 = (s32[16,64,128]{2,1,0:T(8,128)S(1)}, s32[16,64,128]{2,1,0:T(8,128)}, u32[]{:S(2)}) copy-start(s32[16,64,128]{2,1,0:T(8,128)} %material.7) | copy-start | bytes 1572868
  0.7 6.5 %copy-start = (f32[16,64,128]{2,1,0:T(8,128)S(1)}, f32[16,64,128]{2,1,0:T(8,128)}, u32[]{:S(2)}) copy-start(f32[16,64,128]{2,1,0:T(8,128)} %initial.3) | copy-start | bytes 1572868
  2.0 7.6 %collective-permute-start.2 = (f32[24,8,128]{2,1,0:T(8,128)S(1)}, f32[24,8,128]{2,1,0:T(8,128)S(1)}, u32[]{:S(2)}, u32[]{:S(2)}) collective-permute-start(f32[24,8,128]{2,1,0:T(8,128)S(1)} %get-tuple-element.14), channel_id=1, source_target_pairs={{0,1},{2,3},{1,0},{3,2},{4,5},{6,7},{5,4},{7,6},{8,9},{10,11},{9,8... | collective-permute-start | bytes 294920 | tf_op jit(solution)/shard_map/ppermute | solution.py:558
  2.5 7.2 %collective-permute-start.1 = (f32[24,8,128]{2,1,0:T(8,128)S(1)}, f32[24,8,128]{2,1,0:T(8,128)S(1)}, u32[]{:S(2)}, u32[]{:S(2)}) collective-permute-start(f32[24,8,128]{2,1,0:T(8,128)S(1)} %get-tuple-element.13.sent), channel_id=1, source_target_pairs={{1,2},{2,1},{5,6},{6,5},{9,10},{10,9},{13,14},{14,13},{17,18},{18,... | collective-permute-start | bytes 294920 | tf_op jit(solution)/shard_map/ppermute | solution.py:558
  7.3 13.2 %collective-permute-start = (f32[11,64,128]{2,1,0:T(8,128)S(1)}, f32[11,64,128]{2,1,0:T(8,128)S(1)}, u32[]{:S(2)}, u32[]{:S(2)}) collective-permute-start(f32[11,64,128]{2,1,0:T(8,128)S(1)} %far.1), channel_id=1, source_target_pairs={{4,8},{12,16},{20,24},{8,4},{16,12},{24,20},{5,9},{13,17},{21,25},... | collective-permute-start | bytes 1081352 | tf_op jit(solution)/shard_map/ppermute | solution.py:570
  9.9 4.7 %collective-permute-start.4 = (f32[6,72,128]{2,1,0:T(8,128)S(1)}, f32[6,72,128]{2,1,0:T(8,128)S(1)}, u32[]{:S(2)}, u32[]{:S(2)}) collective-permute-start(f32[6,72,128]{2,1,0:T(8,128)S(1)} %get-tuple-element.16), channel_id=1, source_target_pairs={{0,4},{8,12},{16,20},{24,28},{4,0},{12,8},{20,16},{28,24},{1,5},{9... | collective-permute-start | bytes 663560 | tf_op jit(solution)/shard_map/ppermute | solution.py:581
  11.1 3.5 %collective-permute-start.5 = (f32[6,72,128]{2,1,0:T(8,128)S(1)}, f32[6,72,128]{2,1,0:T(8,128)S(1)}, u32[]{:S(2)}, u32[]{:S(2)}) collective-permute-start(f32[6,72,128]{2,1,0:T(8,128)S(1)} %get-tuple-element.17), channel_id=1, source_target_pairs={{0,4},{8,12},{16,20},{24,28},{4,0},{12,8},{20,16},{28,24},{1,5},{9... | collective-permute-start | bytes 663560 | tf_op jit(solution)/shard_map/ppermute | solution.py:582
  11.2 9.4 %collective-permute-start.3 = (f32[7,8,128]{2,1,0:T(8,128)S(1)}, f32[7,8,128]{2,1,0:T(8,128)S(1)}, u32[]{:S(2)}, u32[]{:S(2)}) collective-permute-start(f32[7,8,128]{2,1,0:T(8,128)S(1)} %get-tuple-element.15), channel_id=1, source_target_pairs={{4,8},{12,16},{20,24},{8,4},{16,12},{24,20},{5,9},{13,17},{21,25},... | collective-permute-start | bytes 86024 | tf_op jit(solution)/shard_map/ppermute | solution.py:583

commit v12 on v10

--- a/solution.py
+++ b/solution.py
@@ -498,10 +498,8 @@
     first = (mixed(EA, "EA", 1, H), mixed(ZA, "ZA", 1, H)) + weights
     second = (mixed(EB, "EB", 2, H + 1), mixed(ZB, "ZB", 2, H + 1)) + weights
     third = (mixed(EC, "EA", 3, H + 2), mixed(ZC, "ZA", 3, H + 2)) + weights
-    steps.sweep(first, 4, 2, store_a, (True, True))
-    steps.sweep(first, 2, 2, store_a, (False, False))
-    steps.sweep(second, 5, 2, store_b, (True, True))
-    steps.sweep(second, 3, 2, store_b, (False, True))
+    steps.sweep(first, 2, 4, store_a, (False, False, True, True))
+    steps.sweep(second, 3, 4, store_b, (False, True, True, True))
     for p in (1, 0):
         f = H + 2 * p
         steps.sweep(third, f, 2, store_c, (True, True))

time: 22.5 us -> 22.6 us (level)
  no operation moved by 1% of the time
where the time goes in v12:
time: 22.6 us; the launch traced here: 22.4 us
  starting transfers between devices  13.3 us (59%)
  Pallas kernels  7.77 us (34%)
  between operations  0.74 us (3%)
  waiting for transfers between devices  0.63 us (3%)
    ppermute x2, starting transfers between devices, per_device(): lax.ppermute(value, 'gy', swap([(i, i + 1) for i in range(start, rows_y -...  5.4 us
    ppermute x1, starting transfers between devices, per_device(): far = lax.ppermute(far, 'gx', swap(far_pairs))  4.23 us
    pallas_call x1, Pallas kernels, per_device(): pl.pallas_call(inner_kernel, out_shape=(wide_block, wide_block, shape((6,...  4.19 us
    ppermute x1, starting transfers between devices, per_device(): far_corner = lax.ppermute(far_corner, 'gx', swap(far_pairs))  3.07 us
    pallas_call x1, Pallas kernels, per_device(): pl.pallas_call(outer_kernel, out_shape=(block, block), in_specs=[vmem] *...  1.89 us
    pallas_call x1, Pallas kernels, per_device(): pl.pallas_call(edge_kernel, out_shape=(send, send, shape((8, cells_z), f3...  1.34 us
    ppermute x1, waiting for transfers between devices, per_device(): far_corner = lax.ppermute(far_corner, 'gx', swap(far_pairs))  0.62 us
    ppermute x1, starting transfers between devices, per_device(): near_b = lax.ppermute(near_b, 'gx', swap(near_pairs))  0.5 us
  transfers between devices with their start and end apart: 6, of which 1 were waited for; matrix products, arithmetic and copies ran while one was open for 0% of the time, Pallas kernels for 20%

profile of v12, /device:TPU:1, one launch (start us, length us, event | category | flops | bytes accessed | tf_op | source)
XLA Modules:
  0.0 22.4 jit_solution(12008210673041334937)
XLA Ops:
  0.6 0.0 copy-start.2
  0.6 0.0 copy-start.1
  0.7 0.0 copy-start
  0.7 1.3 %edges.1 = (f32[24,8,128]{2,1,0:T(8,128)S(1)}, f32[24,8,128]{2,1,0:T(8,128)S(1)}, f32[8,128]{1,0:T(8,128)S(1)}) custom-call(f32[16,64,128]{2,1,0:T(8,128)} %initial.3, s32[16,64,128]{2,1,0:T(8,128)} %material.7, s32[16,64,128]{2,1,0:T(8,128)} %goal.7, f32[8]{0:T(128)} %cond.1), custom_call_target="tpu_custom_call" | custom-call | tf_op jit(solution)/shard_map/edges/pallas_call | solution.py:538
  2.0 0.7 %collective-permute-start.2 = (f32[24,8,128]{2,1,0:T(8,128)S(1)}, f32[24,8,128]{2,1,0:T(8,128)S(1)}, u32[]{:S(2)}, u32[]{:S(2)}) collective-permute-start(f32[24,8,128]{2,1,0:T(8,128)S(1)} %get-tuple-element.14), channel_id=1, source_target_pairs={{1,2},{2,1},{5,6},{6,5},{9,10},{10,9},{13,14},{14,13},{17,18},{18,... | collective-permute-start | bytes 294920 | tf_op jit(solution)/shard_map/ppermute | solution.py:556
  2.7 4.7 %collective-permute-start.1 = (f32[24,8,128]{2,1,0:T(8,128)S(1)}, f32[24,8,128]{2,1,0:T(8,128)S(1)}, u32[]{:S(2)}, u32[]{:S(2)}) collective-permute-start(f32[24,8,128]{2,1,0:T(8,128)S(1)} %get-tuple-element.13.sent), channel_id=1, source_target_pairs={{0,1},{2,3},{1,0},{3,2},{4,5},{6,7},{5,4},{7,6},{8,9},{10,11},{9,8... | collective-permute-start | bytes 294920 | tf_op jit(solution)/shard_map/ppermute | solution.py:556
  7.4 0.0 copy-done.2
  7.4 0.0 copy-done.1
  7.4 0.0 copy-done
  7.4 0.2 far.1
  7.6 4.2 %collective-permute-start = (f32[11,64,128]{2,1,0:T(8,128)S(1)}, f32[11,64,128]{2,1,0:T(8,128)S(1)}, u32[]{:S(2)}, u32[]{:S(2)}) collective-permute-start(f32[11,64,128]{2,1,0:T(8,128)S(1)} %far.1), channel_id=1, source_target_pairs={{4,8},{12,16},{20,24},{8,4},{16,12},{24,20},{5,9},{13,17},{21,25},... | collective-permute-start | bytes 1081352 | tf_op jit(solution)/shard_map/ppermute | solution.py:568
  11.8 0.0 collective-permute-done.2.second
  11.8 0.0 collective-permute-done.1.first
  11.9 0.2 near.1
  12.0 0.1 collective-permute-start.4
  12.1 0.5 %collective-permute-start.5 = (f32[6,72,128]{2,1,0:T(8,128)S(1)}, f32[6,72,128]{2,1,0:T(8,128)S(1)}, u32[]{:S(2)}, u32[]{:S(2)}) collective-permute-start(f32[6,72,128]{2,1,0:T(8,128)S(1)} %get-tuple-element.17), channel_id=1, source_target_pairs={{0,4},{8,12},{16,20},{24,28},{4,0},{12,8},{20,16},{28,24},{1,5},{9... | collective-permute-start | bytes 663560 | tf_op jit(solution)/shard_map/ppermute | solution.py:580
  12.6 3.1 %collective-permute-start.3 = (f32[7,8,128]{2,1,0:T(8,128)S(1)}, f32[7,8,128]{2,1,0:T(8,128)S(1)}, u32[]{:S(2)}, u32[]{:S(2)}) collective-permute-start(f32[7,8,128]{2,1,0:T(8,128)S(1)} %get-tuple-element.15), channel_id=1, source_target_pairs={{4,8},{12,16},{20,24},{8,4},{16,12},{24,20},{5,9},{13,17},{21,25},... | collective-permute-start | bytes 86024 | tf_op jit(solution)/shard_map/ppermute | solution.py:581
  15.7 0.0 collective-permute-done.4.near_a
  15.7 0.0 collective-permute-done.5.near_b
  15.7 4.2 %inner.1 = (f32[16,72,128]{2,1,0:T(8,128)S(1)}, f32[16,72,128]{2,1,0:T(8,128)S(1)}, f32[6,9,8,128]{3,2,1,0:T(8,128)S(1)}, f32[30,9,8,128]{3,2,1,0:T(8,128)S(1)}) custom-call(f32[16,64,128]{2,1,0:T(8,128)S(1)} %copy-done, s32[16,64,128]{2,1,0:T(8,128)S(1)} %copy-done.1, s32[16,64,128]{2,1,0:T(8,128)S(1)} %copy-done.2, f32[8,128]{1,0:T(8,128)S(1)} %get-tuple-element.12.table, ...), custom_call_target="tpu_custom_call" | custom-call | flops 1000 | bytes 1000 | tf_op jit(solution)/shard_map/inner/pallas_call | solution.py:590
  19.9 0.6 %collective-permute-done.3.far_corner = f32[7,8,128]{2,1,0:T(8,128)S(1)} collective-permute-done((f32[7,8,128]{2,1,0:T(8,128)S(1)}, f32[7,8,128]{2,1,0:T(8,128)S(1)}, u32[]{:S(2)}, u32[]{:S(2)}) %collective-permute-start.3) | collective-permute-done | bytes 28704 | tf_op jit(solution)/shard_map/ppermute | solution.py:581
  20.5 0.0 collective-permute-done.far
  20.5 1.9 %outer.1 = (f32[16,64,128]{2,1,0:T(8,128)}, f32[16,64,128]{2,1,0:T(8,128)}) custom-call(f32[11,64,128]{2,1,0:T(8,128)S(1)} %collective-permute-done.far, f32[7,8,128]{2,1,0:T(8,128)S(1)} %collective-permute-done.3.far_corner, f32[6,9,8,128]{3,2,1,0:T(8,128)S(1)} %get-tuple-element.18.edge, f32[30,9,8,128]{3,2,1,0:T(8,128)S(1)} %get-tuple-element.19.kept, ...), custom_call_target="tpu_custom_call" | custom-call | tf_op jit(solution)/shard_map/outer/pallas_call | solution.py:601
Async XLA Ops:
  0.6 6.8 %copy-start.2 = (s32[16,64,128]{2,1,0:T(8,128)S(1)}, s32[16,64,128]{2,1,0:T(8,128)}, u32[]{:S(2)}) copy-start(s32[16,64,128]{2,1,0:T(8,128)} %goal.7) | copy-start | bytes 1572868
  0.6 6.8 %copy-start.1 = (s32[16,64,128]{2,1,0:T(8,128)S(1)}, s32[16,64,128]{2,1,0:T(8,128)}, u32[]{:S(2)}) copy-start(s32[16,64,128]{2,1,0:T(8,128)} %material.7) | copy-start | bytes 1572868
  0.7 6.8 %copy-start = (f32[16,64,128]{2,1,0:T(8,128)S(1)}, f32[16,64,128]{2,1,0:T(8,128)}, u32[]{:S(2)}) copy-start(f32[16,64,128]{2,1,0:T(8,128)} %initial.3) | copy-start | bytes 1572868
  2.0 9.8 %collective-permute-start.2 = (f32[24,8,128]{2,1,0:T(8,128)S(1)}, f32[24,8,128]{2,1,0:T(8,128)S(1)}, u32[]{:S(2)}, u32[]{:S(2)}) collective-permute-start(f32[24,8,128]{2,1,0:T(8,128)S(1)} %get-tuple-element.14), channel_id=1, source_target_pairs={{1,2},{2,1},{5,6},{6,5},{9,10},{10,9},{13,14},{14,13},{17,18},{18,... | collective-permute-start | bytes 294920 | tf_op jit(solution)/shard_map/ppermute | solution.py:556
  2.7 9.2 %collective-permute-start.1 = (f32[24,8,128]{2,1,0:T(8,128)S(1)}, f32[24,8,128]{2,1,0:T(8,128)S(1)}, u32[]{:S(2)}, u32[]{:S(2)}) collective-permute-start(f32[24,8,128]{2,1,0:T(8,128)S(1)} %get-tuple-element.13.sent), channel_id=1, source_target_pairs={{0,1},{2,3},{1,0},{3,2},{4,5},{6,7},{5,4},{7,6},{8,9},{10,11},{9,8... | collective-permute-start | bytes 294920 | tf_op jit(solution)/shard_map/ppermute | solution.py:556
  7.6 12.9 %collective-permute-start = (f32[11,64,128]{2,1,0:T(8,128)S(1)}, f32[11,64,128]{2,1,0:T(8,128)S(1)}, u32[]{:S(2)}, u32[]{:S(2)}) collective-permute-start(f32[11,64,128]{2,1,0:T(8,128)S(1)} %far.1), channel_id=1, source_target_pairs={{4,8},{12,16},{20,24},{8,4},{16,12},{24,20},{5,9},{13,17},{21,25},... | collective-permute-start | bytes 1081352 | tf_op jit(solution)/shard_map/ppermute | solution.py:568
  12.0 3.6 %collective-permute-start.4 = (f32[6,72,128]{2,1,0:T(8,128)S(1)}, f32[6,72,128]{2,1,0:T(8,128)S(1)}, u32[]{:S(2)}, u32[]{:S(2)}) collective-permute-start(f32[6,72,128]{2,1,0:T(8,128)S(1)} %get-tuple-element.16), channel_id=1, source_target_pairs={{0,4},{8,12},{16,20},{24,28},{4,0},{12,8},{20,16},{28,24},{1,5},{9... | collective-permute-start | bytes 663560 | tf_op jit(solution)/shard_map/ppermute | solution.py:579
  12.1 3.6 %collective-permute-start.5 = (f32[6,72,128]{2,1,0:T(8,128)S(1)}, f32[6,72,128]{2,1,0:T(8,128)S(1)}, u32[]{:S(2)}, u32[]{:S(2)}) collective-permute-start(f32[6,72,128]{2,1,0:T(8,128)S(1)} %get-tuple-element.17), channel_id=1, source_target_pairs={{0,4},{8,12},{16,20},{24,28},{4,0},{12,8},{20,16},{28,24},{1,5},{9... | collective-permute-start | bytes 663560 | tf_op jit(solution)/shard_map/ppermute | solution.py:580
  12.6 7.9 %collective-permute-start.3 = (f32[7,8,128]{2,1,0:T(8,128)S(1)}, f32[7,8,128]{2,1,0:T(8,128)S(1)}, u32[]{:S(2)}, u32[]{:S(2)}) collective-permute-start(f32[7,8,128]{2,1,0:T(8,128)S(1)} %get-tuple-element.15), channel_id=1, source_target_pairs={{4,8},{12,16},{20,24},{8,4},{16,12},{24,20},{5,9},{13,17},{21,25},... | collective-permute-start | bytes 86024 | tf_op jit(solution)/shard_map/ppermute | solution.py:581
